TPU v7x, 32 devices: a whole 2x2x4 slice. The times are simulated.
32 devices in a mesh: grp: 4 (over y, core), exp: 8 (over z, x).
Axes of the slice: x: 2, y: 2, z: 4, core: 2. Of those that a mesh axis runs over, the one named last changes fastest.
Arguments:
- attention_rows: bfloat16 [8, 2048, 2048], P('exp', None, 'grp'), may hold values from -6 to 6
- expert_choice: int32 [8, 2048, 2], P('exp', 'grp'), may hold values from 0 to 15, all different within a row; in each aligned block of 512 rows (0 to 511, 512 to 1023, ..., all dimensions but the last counted through in order) at most 96 rows name the same one
- gate_weights: float32 [8, 2048, 2], P('exp', 'grp'), may hold values from 0.05 to 1
- up_blocks: int32 [16, 32, 2], P('exp'), may hold values from 0 to 15, as said below
- up_values: bfloat16 [16, 32, 2, 128, 128], P('exp'), may hold values from -0.375 to 0.375
- down_blocks: int32 [16, 16, 4], P('exp'), may hold values from 0 to 31, as said below
- down_values: bfloat16 [16, 16, 4, 128, 128], P('exp'), may hold values from -0.25 to 0.25
Outputs:
- moe_out: bfloat16 [8, 2048, 2048], P('exp', 'grp')
Inputs may be any that keep to these rules, and one draw needn't show every extreme that they name: `expert_choice`: each token names two different experts; among the 512 tokens of one device no expert is named by more than 96 tokens, and in some device one expert is named by exactly 96. `up_blocks`: for each expert and each block column, 2 different block rows. `down_blocks`: for each expert and each block column, 4 different block rows.
All inputs are finite; a program needn't handle non-finite values.
Results may differ from a plain program's by a relative error of at most 0.0057.
Values may be sent and summed in bfloat16 or wider, within the bound.
No kernel may reach another device: no remote copies, remote signals or barrier semaphores. Data moves between devices by JAX's collectives and lax.ppermute only.
A program may use at most 128 MiB of HBM per device.

v0:
```python
import math

import jax
import jax.numpy as jnp
from jax import lax
from jax.sharding import PartitionSpec as P


def expert_ffn(token_rows, up_rows, up_vals, down_rows, down_vals):
    row_count, row_width = token_rows.shape
    block_size = up_vals.shape[-1]
    in_blocks = row_width // block_size
    mid_blocks = up_rows.shape[0]
    pick_up = (up_rows[:, :, None] == jnp.arange(in_blocks)[None, None, :]).astype(jnp.bfloat16)
    chosen = jnp.einsum(
        "rnb,cin->rcib",
        token_rows.reshape(row_count, in_blocks, block_size),
        pick_up,
        preferred_element_type=jnp.float32,
    ).astype(jnp.bfloat16)
    hidden = jnp.einsum("rcib,cibd->rcd", chosen, up_vals, preferred_element_type=jnp.float32)
    hidden = jax.nn.gelu(hidden, approximate=True).astype(jnp.bfloat16)
    pick_down = (down_rows[:, :, None] == jnp.arange(mid_blocks)[None, None, :]).astype(
        jnp.bfloat16
    )
    chosen_mid = jnp.einsum(
        "rcb,jic->rjib", hidden, pick_down, preferred_element_type=jnp.float32
    ).astype(jnp.bfloat16)
    result = jnp.einsum("rjib,jibd->rjd", chosen_mid, down_vals, preferred_element_type=jnp.float32)
    return result.reshape(row_count, row_width).astype(jnp.bfloat16)


def padded_rows(all_rows, weights):
    total_rows, row_width = all_rows.shape
    tile_rows = math.gcd(total_rows, 128)
    tiles = all_rows.reshape(total_rows // tile_rows, tile_rows, row_width)
    mapped = lax.map(
        lambda tile_block: expert_ffn(tile_block, weights[0], weights[1], weights[2], weights[3]),
        tiles,
    )
    return mapped.reshape(total_rows, row_width)


def slot_targets(route_ids, expert_total, capacity):
    pair_ids = route_ids.reshape(-1)
    one_hot = (pair_ids[:, None] == jnp.arange(expert_total, dtype=jnp.int32)[None, :]).astype(
        jnp.int32
    )
    earlier = jnp.cumsum(one_hot, axis=0) - one_hot
    slot_number = jnp.sum(earlier * one_hot, axis=1)
    return (pair_ids * capacity + slot_number).reshape(route_ids.shape)


def place_rows(token_rows, targets, slot_total):
    buffer_rows = jnp.zeros((slot_total, token_rows.shape[1]), token_rows.dtype)
    buffer_rows = buffer_rows.at[targets[:, 0]].set(token_rows)
    return buffer_rows.at[targets[:, 1]].set(token_rows)


def per_device(
    attention_rows, expert_choice, gate_weights, up_blocks, up_values, down_blocks, down_values
):
    group_count = lax.axis_size("grp")
    expert_devices = lax.axis_size("exp")
    local_experts = up_values.shape[0]
    expert_total = local_experts * expert_devices
    own_tokens = expert_choice.shape[1]
    capacity = 3 * own_tokens // expert_total
    head_width = attention_rows.shape[2]
    row_width = head_width * group_count
    targets = slot_targets(expert_choice[0], expert_total, capacity)
    token_rows = lax.all_to_all(attention_rows, "grp", split_axis=1, concat_axis=2, tiled=True)[0]
    send_rows = place_rows(token_rows, targets, expert_total * capacity)
    send_rows = send_rows.reshape(expert_devices, local_experts, capacity, row_width)
    received = lax.all_to_all(send_rows, "exp", split_axis=0, concat_axis=0, tiled=True)
    outputs = []
    for local_index in range(local_experts):
        weights = (
            up_blocks[local_index],
            up_values[local_index],
            down_blocks[local_index],
            down_values[local_index],
        )
        expert_rows = received[:, local_index].reshape(expert_devices * capacity, row_width)
        expert_result = padded_rows(expert_rows, weights)
        outputs.append(expert_result.reshape(expert_devices, capacity, row_width))
    stacked = jnp.stack(outputs, axis=1)
    returned = lax.all_to_all(stacked, "exp", split_axis=0, concat_axis=0, tiled=True).reshape(
        expert_total * capacity, row_width
    )
    picked = returned[targets.reshape(-1)].reshape(own_tokens, 2, row_width)
    combined = jnp.sum(gate_weights[0][:, :, None] * picked.astype(jnp.float32), axis=1)
    return combined.astype(jnp.bfloat16)[None]


def solution(mesh):
    return jax.shard_map(
        per_device,
        mesh=mesh,
        in_specs=(
            P("exp", None, "grp"),
            P("exp", "grp", None),
            P("exp", "grp", None),
            P("exp", None, None),
            P("exp", None, None, None, None),
            P("exp", None, None),
            P("exp", None, None, None, None),
        ),
        out_specs=P("exp", "grp", None),
        check_vma=False,
    )
```

profile of v0, /device:TPU:0, one launch (start us, length us, event | category | flops | bytes accessed | tf_op | source)
XLA Modules:
  0.0 525.9 jit_solution(6306617346492606835)
XLA Ops:
  0.0 7.5 %copy.121 = bf16[1,2048,512]{2,0,1:T(2,128)(2,1)} copy(bf16[1,2048,512]{2,1,0:T(8,128)(2,1)} %param.11) | data formatting | bytes 4194304 | tf_op args[0]
  8.0 14.1 %reduce.4 = bf16[2048,512]{1,0:T(8,128)(2,1)S(1)} reduce(bf16[2048,1,512]{2,1,0:T(2,128)(2,1)} %bitcast.191, bf16[]{:T(256)} %broadcast.102), dimensions={1}, to_apply=%bitcast.127.reduce_sub_computation | reduce | bytes 4194306
  22.1 2.8 reshape.151
  24.8 4.4 all-to-all-start
  29.7 4.5 reduce-window.6
  35.2 19.7 %all-to-all-done = bf16[4,2,131072]{2,1,0:T(2,128)(2,1)S(1)} async-done(((bf16[4,2,131072]{2,1,0:T(2,128)(2,1)}), bf16[4,2,131072]{2,1,0:T(2,128)(2,1)S(1)}, u32[]{:S(2)}, u32[]{:S(2)}) %all-to-all-start) | async-done | bytes 2097184 | tf_op jit(solution)/shard_map/all_to_all | solution.py:72
  54.9 3.4 reshape.152
  58.2 2.8 copy.85
  61.0 2.4 copy.65
  63.4 2.9 copy.66
  66.3 7.4 %scatter_custom_fusion = bf16[1536,2048]{1,0:T(8,128)(2,1)} fusion(s32[512]{0:T(512)S(1)} %get-tuple-element.82, bf16[512,2048]{1,0:T(8,128)(2,1)S(1)} %copy.66, bf16[]{:T(256)} %constant.30.clone.1), kind=kCustom, calls=%fused_computation.59 | custom fusion | bytes 6291458 | tf_op jit(solution)/shard_map/scatter | solution.py:56
  73.7 10.2 %scatter_fusion = bf16[1536,2048]{1,0:T(8,128)(2,1)} fusion(bf16[1536,2048]{1,0:T(8,128)(2,1)} %scatter_custom_fusion, s32[512]{0:T(512)S(1)} %get-tuple-element.81, bf16[512,2048]{1,0:T(8,128)(2,1)S(1)} %copy.66), kind=kCustom, calls=%fused_computation.2 | custom fusion | bytes 6293504 | tf_op jit(solution)/shard_map/scatter | solution.py:57
  83.9 6.6 %all-to-all-start.1 = ((bf16[8,2,96,2048]{3,2,1,0:T(8,128)(2,1)}), bf16[8,2,96,2048]{3,2,1,0:T(8,128)(2,1)}, u32[]{:S(2)}, u32[]{:S(2)}) async-start(bf16[8,2,96,2048]{3,2,1,0:T(8,128)(2,1)} %bitcast.188), calls=%async_computation.1 | async-start | bytes 12582912 | tf_op jit(solution)/shard_map/all_to_all | solution.py:75
  90.5 4.0 fusion.65
  94.5 3.9 copy.86
  98.4 2.6 copy.87
  101.0 4.9 slice_bitcast_fusion.1
  105.9 122.6 %all-to-all-done.1 = bf16[8,2,96,2048]{3,2,1,0:T(8,128)(2,1)} async-done(((bf16[8,2,96,2048]{3,2,1,0:T(8,128)(2,1)}), bf16[8,2,96,2048]{3,2,1,0:T(8,128)(2,1)}, u32[]{:S(2)}, u32[]{:S(2)}) %all-to-all-start.1) | async-done | bytes 6291488 | tf_op jit(solution)/shard_map/all_to_all | solution.py:75
  228.5 6.6 %fusion.64 = (bf16[8,1,96,2048]{3,2,1,0:T(8,128)(2,1)}, bf16[8,1,96,2048]{3,2,1,0:T(8,128)(2,1)}) fusion(bf16[8,2,96,2048]{3,2,1,0:T(8,128)(2,1)} %all-to-all-done.1), kind=kLoop, calls=%fused_computation.80 | loop fusion | bytes 12582912 | tf_op jit(solution)/shard_map/slice | solution.py:84
  235.1 2.1 broadcast.77.clone2.1
  237.2 50.4 %while.20 = (s32[]{:T(128)}, bf16[6,128,2048]{2,1,0:T(8,128)(2,1)}, s32[1,16,4]{1,2,0:T(4,128)S(1)}, s32[1,32,2]{1,2,0:T(2,128)S(1)}, bf16[6,128,2048]{2,1,0:T(8...) while((s32[]{:T(128)}, bf16[6,128,2048]{2,1,0:T(8,128)(2,1)}, ...), condition=%wide.region_6.7_spmd, body=%wide.region_5.6_spmd.sunk | while | flops 644615168 | bytes 28312692 | solution.py:37
  237.2 1.1 dynamic-slice_bitcast_fusion.4
  239.2 3.0 fusion.102
  245.6 1.1 dynamic-slice_bitcast_fusion.4
  247.6 3.0 fusion.102
  256.0 3.0 fusion.102
  262.4 1.1 dynamic-slice_bitcast_fusion.4
  264.3 3.0 fusion.102
  272.7 3.0 fusion.102
  281.1 3.0 fusion.102
  287.6 2.1 broadcast.77.clone2
  289.6 50.3 %while.21 = (s32[]{:T(128)}, bf16[6,128,2048]{2,1,0:T(8,128)(2,1)}, s32[1,16,4]{1,2,0:T(4,128)S(1)}, s32[1,32,2]{1,2,0:T(2,128)S(1)}, bf16[6,128,2048]{2,1,0:T(8...) while((s32[]{:T(128)}, bf16[6,128,2048]{2,1,0:T(8,128)(2,1)}, ...), condition=%wide.region_8.9_spmd, body=%wide.region_7.8_spmd.sunk | while | flops 644615168 | bytes 28312692 | solution.py:37
  291.6 3.0 fusion.112
  298.0 1.1 dynamic-slice_bitcast_fusion.5
  300.0 3.0 fusion.112
  306.4 1.1 dynamic-slice_bitcast_fusion.5
  308.4 3.0 fusion.112
  316.8 3.0 fusion.112
  323.2 1.1 dynamic-slice_bitcast_fusion.5
  325.2 3.0 fusion.112
  333.5 3.0 fusion.112
  340.0 3.4 pad_maximum_fusion
  343.4 3.2 copy.72
  346.6 4.9 all-to-all-start.2
  351.9 136.9 %all-to-all-done.2 = bf16[8,2,96,2048]{3,2,1,0:T(8,128)(2,1)} async-done(((bf16[8,2,96,2048]{3,2,1,0:T(8,128)(2,1)}), bf16[8,2,96,2048]{3,2,1,0:T(8,128)(2,1)}, u32[]{:S(2)}, u32[]{:S(2)}) %all-to-all-start.2) | async-done | bytes 6291488 | tf_op jit(solution)/shard_map/all_to_all | solution.py:88
  488.8 12.4 %gather_fusion = bf16[1024,2048]{1,0:T(8,128)(2,1)} fusion(bf16[1536,2048]{1,0:T(8,128)(2,1)} %bitcast.49, s32[1024]{0:T(1024)S(1)} %broadcast_clamp_fusion), kind=kCustom, calls=%fused_computation | custom fusion | bytes 8392704 | tf_op jit(solution)/shard_map/gather | solution.py:91
  501.2 9.6 %reshape.108 = f32[512,2,2048]{2,1,0:T(2,128)} reshape(bf16[1024,2048]{1,0:T(8,128)(2,1)} %gather_fusion) | data formatting | bytes 12582912 | tf_op jit(solution)/shard_map/convert_element_type | solution.py:92
  510.9 15.0 %multiply_reduce_fusion = bf16[512,2048]{1,0:T(8,128)(2,1)} fusion(f32[512,2,2048]{2,1,0:T(2,128)} %reshape.108, f32[512,2]{1,0:T(8,128)S(1)} %copy.58), kind=kLoop, calls=%fused_computation.57 | loop fusion | flops 3145728 | bytes 10489856 | tf_op jit(solution)/shard_map/reduce_sum | solution.py:92
  (132 shorter events, 59.8 us)
Async XLA Ops:
  24.8 4.4 copy-start.2
  24.8 30.1 %all-to-all-start = ((bf16[4,2,131072]{2,1,0:T(2,128)(2,1)}), bf16[4,2,131072]{2,1,0:T(2,128)(2,1)S(1)}, u32[]{:S(2)}, u32[]{:S(2)}) async-start(bf16[4,2,131072]{2,1,0:T(2,128)(2,1)} %reshape.151), calls=%async_computation | async-start | bytes 4194304 | tf_op jit(solution)/shard_map/all_to_all | solution.py:72
  83.9 144.6 %all-to-all-start.1 = ((bf16[8,2,96,2048]{3,2,1,0:T(8,128)(2,1)}), bf16[8,2,96,2048]{3,2,1,0:T(8,128)(2,1)}, u32[]{:S(2)}, u32[]{:S(2)}) async-start(bf16[8,2,96,2048]{3,2,1,0:T(8,128)(2,1)} %bitcast.188), calls=%async_computation.1 | async-start | bytes 12582912 | tf_op jit(solution)/shard_map/all_to_all | solution.py:75
  98.4 2.6 copy-start.5
  98.4 2.6 copy-start.4
  242.2 1.6 copy-start.1
  250.6 1.6 copy-start.1
  259.0 1.6 copy-start.1
  267.4 1.6 copy-start.1
  275.8 1.6 copy-start.1
  284.2 1.6 copy-start.1
  294.6 1.6 copy-start
  303.0 1.6 copy-start
  311.4 1.6 copy-start
  319.8 1.6 copy-start
  328.2 1.6 copy-start
  336.6 1.6 copy-start
  346.6 5.1 copy-start.3
  346.6 142.2 %all-to-all-start.2 = ((bf16[8,2,96,2048]{3,2,1,0:T(8,128)(2,1)}), bf16[8,2,96,2048]{3,2,1,0:T(8,128)(2,1)}, u32[]{:S(2)}, u32[]{:S(2)}) async-start(bf16[8,2,96,2048]{3,2,1,0:T(8,128)(2,1)} %copy.72), calls=%async_computation.2 | async-start | bytes 12582912 | tf_op jit(solution)/shard_map/all_to_all | solution.py:88
where the time goes:
time: 528 us; the launch traced here: 526 us
  waiting for transfers between devices  279 us (53%)
  local copies, waits for them, and re-layouts  127 us (24%)
  matrix products  65.5 us (12%)
  other arithmetic  37.6 us (7%)
  starting transfers between devices  15.8 us (3%)
    all_to_all x1, waiting for transfers between devices, per_device(): lax.all_to_all(stacked, 'exp', split_axis=0, concat_axis=0, tiled=True)  137 us
    all_to_all x1, waiting for transfers between devices, per_device(): lax.all_to_all(send_rows, 'exp', split_axis=0, concat_axis=0, tiled=True)  123 us
    dot_general x12, matrix products, expert_ffn(): jnp.einsum('rcib,cibd->rcd', chosen, up_vals, preferred_element_type=jnp....  36.1 us
    unnamed x16, local copies, waits for them, and re-layouts  23.6 us
    while x48, local copies, waits for them, and re-layouts  21.8 us
    all_to_all x1, waiting for transfers between devices, per_device(): lax.all_to_all(attention_rows, 'grp', split_axis=1, concat_axis=2, tiled=...  19.7 us
    reduce_sum x1, other arithmetic, per_device(): jnp.sum(gate_weights[0][:, :, None] * picked.astype(jnp.float32), axis=1)  15 us
    unnamed x1, other arithmetic  14.1 us
  transfers between devices with their start and end apart: 3, of which 3 were waited for; matrix products, arithmetic and copies ran while one was open for 4% of the time, Pallas kernels for 0%

commit v1 on v0

--- a/solution.py
+++ b/solution.py
@@ -1,9 +1,426 @@
+import functools
 import math
 
 import jax
 import jax.numpy as jnp
+import numpy as np
 from jax import lax
+from jax.experimental import pallas as pl
+from jax.experimental.pallas import tpu as pltpu
 from jax.sharding import PartitionSpec as P
+
+AXES = ("grp", "exp")
+
+
+def place(core, plane):
+    return jnp.where(plane < 2, core, 3 - core)
+
+
+def all_pairs(rule):
+    pairs = []
+    for y in range(2):
+        for core in range(2):
+            for z in range(4):
+                for x in range(2):
+                    to = rule(y, core, z, x)
+                    if to is not None:
+                        ty, tc, tz, tx = to
+                        pairs.append(((y * 2 + core) * 8 + z * 2 + x, (ty * 2 + tc) * 8 + tz * 2 + tx))
+    return pairs
+
+
+def along_z(step, senders):
+    return all_pairs(lambda y, c, z, x: (y, c, z + step, x) if (z, c) in senders else None)
+
+
+def peer_pairs(other_x, k):
+    return all_pairs(lambda y, c, z, x: (y ^ (k >> 1), c ^ (k & 1), z, x ^ other_x))
+
+
+def send(value, pairs):
+    return lax.ppermute(value, AXES, pairs)
+
+
+def after(value, other):
+    return lax.optimization_barrier((value, other))[0]
+
+
+TABLE_ROWS = 48
+
+
+def pack_kernel(pieces, which, up_ref, down_ref, up_at, down_at, out_ref):
+    step = pl.program_id(0)
+
+    @pl.when(step < pieces)
+    def _():
+        out_ref[...] = up_ref[0]
+
+    @pl.when((step >= pieces) & (step < 2 * pieces))
+    def _():
+        out_ref[...] = down_ref[0]
+
+    @pl.when(step == 2 * pieces)
+    def _():
+        ups, downs = up_at.shape[1], down_at.shape[1]
+        out_ref[0:TABLE_ROWS, :] = jnp.zeros((TABLE_ROWS, out_ref.shape[1]), jnp.bfloat16)
+        out_ref[0:ups, 0 : up_at.shape[2]] = up_at[0].astype(jnp.float32).astype(jnp.bfloat16)
+        out_ref[ups : ups + downs, 0 : down_at.shape[2]] = (
+            down_at[0].astype(jnp.float32).astype(jnp.bfloat16)
+        )
+
+
+def pack_weights(which, up, down, up_at, down_at):
+    pieces = 2
+    size, blk = up.shape[1], up.shape[2]
+    step = size // pieces
+    return pl.pallas_call(
+        lambda *a: pack_kernel(pieces, *a),
+        grid_spec=pltpu.PrefetchScalarGridSpec(
+            num_scalar_prefetch=1,
+            grid=(2 * pieces + 1,),
+            in_specs=[
+                pl.BlockSpec((1, step, blk), lambda i, w: (w[0], jnp.minimum(i, pieces - 1), 0)),
+                pl.BlockSpec(
+                    (1, step, blk), lambda i, w: (w[0], jnp.clip(i - pieces, 0, pieces - 1), 0)
+                ),
+                pl.BlockSpec((1,) + up_at.shape[1:], lambda i, w: (w[0], 0, 0)),
+                pl.BlockSpec((1,) + down_at.shape[1:], lambda i, w: (w[0], 0, 0)),
+            ],
+            out_specs=pl.BlockSpec((step, blk), lambda i, w: (i, 0)),
+        ),
+        out_shape=jax.ShapeDtypeStruct((2 * size + TABLE_ROWS, blk), up.dtype),
+        cost_estimate=pl.CostEstimate(flops=0, bytes_accessed=8_400_000, transcendentals=0),
+        compiler_params=pltpu.CompilerParams(vmem_limit_bytes=24 * 2**20),
+    )(which[None].astype(jnp.int32), up, down, up_at, down_at)
+
+
+def slot_rows(first, second, experts):
+    tokens = first.shape[1]
+    ids = lax.broadcasted_iota(jnp.int32, (experts, tokens), 0)
+    named = (ids == first) | (ids == second)
+    before = lax.broadcasted_iota(jnp.int32, (tokens, tokens), 0) < lax.broadcasted_iota(
+        jnp.int32, (tokens, tokens), 1
+    )
+    count = jnp.dot(
+        jnp.where(named, 1.0, 0.0).astype(jnp.bfloat16),
+        jnp.where(before, 1.0, 0.0).astype(jnp.bfloat16),
+        preferred_element_type=jnp.float32,
+    )
+    return jnp.where(named, count.astype(jnp.int32), -1)
+
+
+def gather_kernel(experts, cap, order, x_ref, choice_ref, *refs):
+    outs, (slots, pick) = refs[:4], refs[4:]
+    tokens = x_ref.shape[0]
+    slots[...] = slot_rows(choice_ref[0, 0:1, :], choice_ref[0, 1:2, :], experts)
+    row = lax.broadcasted_iota(jnp.int32, (cap, tokens), 0)
+    for n in range(8):
+        line = slots[pl.ds(order[n], 1), :]
+        pick[n * cap : (n + 1) * cap, :] = jnp.where(line == row, 1.0, 0.0).astype(jnp.bfloat16)
+    for k in range(4):
+        rows = jnp.dot(
+            pick[k * 2 * cap : (k + 1) * 2 * cap, :],
+            x_ref[...],
+            preferred_element_type=jnp.float32,
+        ).astype(jnp.bfloat16)
+        outs[k][0] = rows[:cap]
+        outs[k][1] = rows[cap:]
+
+
+def gather_rows(features, choices, order, experts, cap):
+    parts, _, tokens = choices.shape
+    width = features.shape[1]
+    return pl.pallas_call(
+        functools.partial(
+            lambda *a: gather_kernel(experts, cap, *a),
+        ),
+        grid_spec=pltpu.PrefetchScalarGridSpec(
+            num_scalar_prefetch=1,
+            grid=(parts,),
+            in_specs=[
+                pl.BlockSpec((tokens, width), lambda b, order: (b, 0)),
+                pl.BlockSpec((1, 2, tokens), lambda b, order: (b, 0, 0)),
+            ],
+            out_specs=[pl.BlockSpec((2, cap, width), lambda b, order: (0, b, 0))] * 4,
+            scratch_shapes=[
+                pltpu.VMEM((experts, tokens), jnp.int32),
+                pltpu.VMEM((8 * cap, tokens), jnp.bfloat16),
+            ],
+        ),
+        out_shape=[jax.ShapeDtypeStruct((2, parts * cap, width), jnp.bfloat16)] * 4,
+        cost_estimate=pl.CostEstimate(
+            flops=2 * parts * 8 * cap * tokens * width, bytes_accessed=12_000_000, transcendentals=0
+        ),
+        compiler_params=pltpu.CompilerParams(vmem_limit_bytes=24 * 2**20),
+    )(order, features, choices)
+
+
+def gelu(v):
+    half = 0.5 * v
+    inner = v * (math.sqrt(2 / math.pi) + (math.sqrt(2 / math.pi) * 0.044715) * (v * v))
+    return half + half * jnp.tanh(inner)
+
+
+def ffn_kernel(phase, n_weights, cap, meta, *refs):
+    bufs, refs = refs[:8], refs[8:]
+    sources, refs = refs[:n_weights], refs[n_weights:]
+    outs, refs = refs[:8], refs[8:]
+    xs, wts, hid, res, packed, wide, table, x_sem, w_sem, o_sem = refs
+    part_rows, width = bufs[0].shape[1], bufs[0].shape[2]
+    blk = wts.shape[1]
+    up_cols = hid.shape[1] // blk
+    down_cols = res.shape[1] // blk
+    up_depth, down_depth = 2 * blk, 4 * blk
+    up_size = up_cols * up_depth
+    g, chosen = meta[0], meta[1]
+    in_copies = []
+    for n in range(8):
+        col = pl.multiple_of((g ^ (n & 3)) * width, width)
+        in_copies.append(
+            pltpu.make_async_copy(
+                bufs[n].at[phase],
+                xs.at[pl.ds((n >> 2) * part_rows, part_rows), pl.ds(col, width)],
+                x_sem.at[n],
+            )
+        )
+        in_copies[-1].start()
+
+    def weight_copies(source):
+        return [
+            pltpu.make_async_copy(
+                source.at[pl.ds(0, up_size)], wts.at[pl.ds(0, up_size)], w_sem.at[0]
+            ),
+            pltpu.make_async_copy(
+                source.at[pl.ds(up_size, down_cols * down_depth)],
+                wts.at[pl.ds(up_size, down_cols * down_depth)],
+                w_sem.at[1],
+            ),
+            pltpu.make_async_copy(
+                source.at[pl.ds(up_size + down_cols * down_depth, TABLE_ROWS)], packed, w_sem.at[2]
+            ),
+        ]
+
+    for i in range(n_weights):
+
+        @pl.when(chosen == i)
+        def _(i=i):
+            for one in weight_copies(sources[i])[::-1]:
+                one.start()
+
+    weight_copies(sources[0])[2].wait()
+    wide[...] = packed[...].astype(jnp.float32).astype(jnp.int32)
+    to_scalars = pltpu.make_async_copy(wide, table, w_sem.at[3])
+    to_scalars.start()
+    for one in in_copies:
+        one.wait()
+    to_scalars.wait()
+    weight_copies(sources[0])[0].wait()
+
+    def up_step(col):
+        parts = []
+        for i in range(2):
+            at = pl.multiple_of(table[col, i] * blk, blk)
+            parts.append(xs[:, pl.ds(at, blk)])
+        got = jnp.dot(
+            jnp.concatenate(parts, axis=1),
+            wts[pl.ds(pl.multiple_of(col * up_depth, up_depth), up_depth), :],
+            preferred_element_type=jnp.float32,
+        )
+        hid[:, pl.ds(pl.multiple_of(col * blk, blk), blk)] = gelu(got).astype(jnp.bfloat16)
+
+    def down_step(col):
+        parts = []
+        for i in range(4):
+            at = pl.multiple_of(table[up_cols + col, i] * blk, blk)
+            parts.append(hid[:, pl.ds(at, blk)])
+        got = jnp.dot(
+            jnp.concatenate(parts, axis=1),
+            wts[pl.ds(pl.multiple_of(up_size + col * down_depth, down_depth), down_depth), :],
+            preferred_element_type=jnp.float32,
+        )
+        res[:, pl.ds(pl.multiple_of(col * blk, blk), blk)] = got.astype(jnp.bfloat16)
+
+    @pl.loop(0, up_cols // 2)
+    def _(step):
+        for i in range(2):
+            up_step(step * 2 + i)
+
+    weight_copies(sources[0])[1].wait()
+
+    @pl.loop(0, down_cols // 2)
+    def _(step):
+        for i in range(2):
+            down_step(step * 2 + i)
+
+    out_copies = []
+    for n in range(8):
+        at = pl.multiple_of((n >> 2) * part_rows + (g ^ (n & 3)) * cap, 32)
+        out_copies.append(
+            pltpu.make_async_copy(res.at[pl.ds(at, cap)], outs[n], o_sem.at[n])
+        )
+        out_copies[-1].start()
+    for one in out_copies:
+        one.wait()
+
+
+def expert_rows(phase, meta, bufs, weights, cap, hidden):
+    _, part_rows, width = bufs[0].shape
+    blk = weights[0].shape[1]
+    rows, row_width = 2 * part_rows, 4 * width
+    hbm = pl.BlockSpec(memory_space=pltpu.HBM)
+    anywhere = pl.BlockSpec(memory_space=pl.ANY)
+    smem = pl.BlockSpec(memory_space=pltpu.SMEM)
+    up_and_down = weights[0].shape[0] - TABLE_ROWS
+    return pl.pallas_call(
+        lambda *a: ffn_kernel(phase, len(weights), cap, *a),
+        in_specs=[smem] + [anywhere] * 8 + [hbm] * len(weights),
+        out_specs=[anywhere] * 8,
+        out_shape=[jax.ShapeDtypeStruct((cap, row_width), jnp.bfloat16)] * 8,
+        scratch_shapes=[
+            pltpu.VMEM((rows, row_width), jnp.bfloat16),
+            pltpu.VMEM((up_and_down, blk), jnp.bfloat16),
+            pltpu.VMEM((rows, hidden), jnp.bfloat16),
+            pltpu.VMEM((rows, row_width), jnp.bfloat16),
+            pltpu.VMEM((TABLE_ROWS, blk), jnp.bfloat16),
+            pltpu.VMEM((TABLE_ROWS, blk), jnp.int32),
+            pltpu.SMEM((TABLE_ROWS, blk), jnp.int32),
+            pltpu.SemaphoreType.DMA((8,)),
+            pltpu.SemaphoreType.DMA((4,)),
+            pltpu.SemaphoreType.DMA((8,)),
+        ],
+        cost_estimate=pl.CostEstimate(
+            flops=4 * rows * up_and_down * blk,
+            bytes_accessed=12_000_000,
+            transcendentals=rows * hidden,
+        ),
+        compiler_params=pltpu.CompilerParams(vmem_limit_bytes=40 * 2**20),
+    )(meta, *bufs, *weights)
+
+
+def combine_kernel(experts, cap, last, order, choice_ref, gate_ref, *refs):
+    rows, refs = refs[:8], refs[8:]
+    if last:
+        sum_ref, refs = refs[0], refs[1:]
+    out_ref, slots, high, low, stack = refs
+    tokens = choice_ref.shape[1]
+
+    @pl.when(pl.program_id(0) == 0)
+    def _():
+        slots[...] = slot_rows(choice_ref[0:1, :], choice_ref[1:2, :], experts)
+        row = lax.broadcasted_iota(jnp.int32, (cap, tokens), 0)
+        for n in range(8):
+            line = slots[pl.ds(order[n], 1), :]
+            gate = jnp.where(choice_ref[0:1, :] == order[n], gate_ref[0:1, :], gate_ref[1:2, :])
+            top = gate.astype(jnp.bfloat16).astype(jnp.float32)
+            here = line == row
+            high[n * cap : (n + 1) * cap, :] = jnp.where(here, top, 0.0).astype(jnp.bfloat16)
+            low[n * cap : (n + 1) * cap, :] = jnp.where(here, gate - top, 0.0).astype(jnp.bfloat16)
+
+    for n in range(8):
+        stack[n * cap : (n + 1) * cap, :] = rows[n][...]
+    contract = (((0,), (0,)), ((), ()))
+    total = lax.dot_general(high[...], stack[...], contract, preferred_element_type=jnp.float32)
+    total += lax.dot_general(low[...], stack[...], contract, preferred_element_type=jnp.float32)
+    if last:
+        total += sum_ref[...]
+    out_ref[...] = total.astype(out_ref.dtype)
+
+
+def combine_rows(order, choice, gates, rows, so_far, experts, cap):
+    tokens = choice.shape[1]
+    row_width = rows[0].shape[1]
+    last = so_far is not None
+    chunk = 512
+    block = lambda height: pl.BlockSpec((height, chunk), lambda j, order: (0, j))
+    whole = pl.BlockSpec((2, tokens), lambda j, order: (0, 0))
+    return pl.pallas_call(
+        lambda *a: combine_kernel(experts, cap, last, *a),
+        grid_spec=pltpu.PrefetchScalarGridSpec(
+            num_scalar_prefetch=1,
+            grid=(row_width // chunk,),
+            in_specs=[whole, whole] + [block(cap)] * 8 + [block(tokens)] * last,
+            out_specs=block(tokens),
+            scratch_shapes=[
+                pltpu.VMEM((experts, tokens), jnp.int32),
+                pltpu.VMEM((8 * cap, tokens), jnp.bfloat16),
+                pltpu.VMEM((8 * cap, tokens), jnp.bfloat16),
+                pltpu.VMEM((8 * cap, chunk), jnp.bfloat16),
+            ],
+        ),
+        out_shape=jax.ShapeDtypeStruct(
+            (tokens, row_width), jnp.bfloat16 if last else jnp.float32
+        ),
+        cost_estimate=pl.CostEstimate(
+            flops=4 * 8 * cap * tokens * row_width, bytes_accessed=9_000_000, transcendentals=0
+        ),
+        compiler_params=pltpu.CompilerParams(vmem_limit_bytes=24 * 2**20),
+    )(order, choice, gates, *rows, *([so_far] if last else []))
+
+
+def per_device_planes(
+    attention_rows, expert_choice, gate_weights, up_blocks, up_values, down_blocks, down_values
+):
+    experts = 2 * lax.axis_size("exp")
+    own_tokens = expert_choice.shape[1]
+    cap = 3 * own_tokens // experts
+    blk = up_values.shape[-1]
+    hidden = up_values.shape[1] * blk
+    g, at = lax.axis_index("grp"), lax.axis_index("exp")
+    y, core, z, x = g // 2, g % 2, at // 2, at % 2
+    features = attention_rows[0]
+
+    own = pack_weights(
+        y, up_values.reshape(2, -1, blk), down_values.reshape(2, -1, blk), up_blocks, down_blocks
+    )
+    r1 = send(own, along_z(1, ((0, 0), (1, 1), (2, 1))))
+    l1 = send(own, along_z(-1, ((3, 0), (2, 1), (1, 1))))
+
+    choice = expert_choice[0].T
+    gates = gate_weights[0].T
+    far_choice = send(choice, peer_pairs(1, 0))
+    both_choices = jnp.stack([choice, far_choice])
+    both_choices = lax.all_gather(after(both_choices, own), "grp", axis=1)
+    far_features = send(after(features, far_choice), peer_pairs(1, 0))
+
+    def first_second(other_x, k):
+        to = g ^ k
+        plane = place(to % 2, z)
+        base = 2 * (x ^ other_x) + to // 2
+        return 4 * plane + base, 4 * (3 - plane) + base
+
+    order = jnp.stack([e for k in range(4) for e in first_second(0, k)]).astype(jnp.int32)
+
+    def dispatch(rows, choices):
+        parts = gather_rows(rows, choices, order, experts, cap)
+        return [parts[0]] + [send(parts[k], peer_pairs(0, k)) for k in range(1, 4)]
+
+    near = dispatch(features, both_choices[0])
+    r1, l1, near, far_features = lax.optimization_barrier((r1, l1, near, far_features))
+    r2 = send(r1, along_z(1, ((1, 0), (2, 1))))
+    l2 = send(l1, along_z(-1, ((2, 0), (1, 1))))
+    bufs = near + dispatch(far_features, both_choices[1])
+    r2, l2, bufs = lax.optimization_barrier((r2, l2, bufs))
+    r3 = send(r2, along_z(1, ((2, 0),)))
+    l3 = send(l2, along_z(-1, ((1, 0),)))
+
+    take_a = jnp.array([0, 2, 1, 0, 2, 0, 0, 1], jnp.int32)[z * 2 + core]
+    take_b = jnp.array([5, 3, 3, 1, 2, 0, 4, 2], jnp.int32)[z * 2 + core]
+    meta_a = jnp.stack([g, take_a]).astype(jnp.int32)
+    meta_b = jnp.stack([g, take_b]).astype(jnp.int32)
+    peers = [first_second(n >> 2, n & 3) for n in range(8)]
+    order_a = jnp.stack([p[0] for p in peers]).astype(jnp.int32)
+    order_b = jnp.stack([p[1] for p in peers]).astype(jnp.int32)
+
+    def give_back(rows):
+        return [rows[0]] + [send(rows[n], peer_pairs(n >> 2, n & 3)) for n in range(1, 8)]
+
+    first = expert_rows(0, meta_a, bufs, (own, r1, l1), cap, hidden)
+    back_a = give_back(first)
+    r3, l3, back_a = lax.optimization_barrier((r3, l3, back_a))
+    second = expert_rows(1, meta_b, bufs, (r1, l1, r2, l2, r3, l3), cap, hidden)
+    back_b = give_back(second)
+    sum_a = combine_rows(after(order_a, second[0]), choice, gates, back_a, None, experts, cap)
+    return combine_rows(order_b, choice, gates, back_b, sum_a, experts, cap)[None]
 
 
 def expert_ffn(token_rows, up_rows, up_vals, down_rows, down_vals):
@@ -94,8 +511,9 @@
 
 
 def solution(mesh):
+    planes = mesh.shape["grp"] == 4 and mesh.shape["exp"] == 8
     return jax.shard_map(
-        per_device,
+        per_device_planes if planes else per_device,
         mesh=mesh,
         in_specs=(
             P("exp", None, "grp"),

time: 528 us -> 260 us (0.49)
  waiting for transfers between devices: 279 us -> 122 us
  local copies, waits for them, and re-layouts: 127 us -> 25.1 us
  matrix products: 65.5 us -> 0 us
  Pallas kernels: 0 us -> 62 us
  other arithmetic: 37.6 us -> 1.27 us
  starting transfers between devices: 15.8 us -> 43.4 us
    all_to_all x3 -> x0, waiting for transfers between devices: 279 us -> none  [the longest x1 137 us: per_device(): lax.all_to_all(stacked, 'exp', split_axis=0, concat_axis=0, tiled=True)]
    ppermute x0 -> x28, waiting for transfers between devices: none -> 122 us  [send(): return lax.ppermute(value, AXES, pairs)]
    dot_general x48 -> x0, matrix products: 65.5 us -> none  [the longest x12 36.1 us: expert_ffn(): jnp.einsum('rcib,cibd->rcd', chosen, up_vals, preferred_element_type=jnp....]
    pallas_call x0 -> x7, Pallas kernels: none -> 62 us  [the longest x2 36.5 us: expert_rows(): pl.pallas_call(lambda *a: ffn_kernel(phase, len(weights), cap, *a), in_sp...]
    ppermute x0 -> x28, starting transfers between devices: none -> 43.4 us  [send(): return lax.ppermute(value, AXES, pairs)]
    while x48 -> x0, local copies, waits for them, and re-layouts: 21.8 us -> none
    scatter x2 -> x0, local copies, waits for them, and re-layouts: 17.5 us -> none  [the longest x1 10.2 us: place_rows(): return buffer_rows.at[targets[:, 1]].set(token_rows)]
    all_to_all x3 -> x0, starting transfers between devices: 15.8 us -> none  [the longest x1 6.6 us: per_device(): lax.all_to_all(send_rows, 'exp', split_axis=0, concat_axis=0, tiled=True)]
  transfers between devices with their start and end apart: 3 -> 28, of which waited for: 3 -> 15; matrix products, arithmetic and copies ran while one was open for 4% -> 1% of each run, Pallas kernels for 0% -> 13%
where the time goes in v1:
time: 260 us; the launch traced here: 259 us
  waiting for transfers between devices  122 us (47%)
  Pallas kernels  62 us (24%)
  starting transfers between devices  43.4 us (17%)
  local copies, waits for them, and re-layouts  25.1 us (10%)
  blocking collectives  5.19 us (2%)
    ppermute x28, waiting for transfers between devices, send(): return lax.ppermute(value, AXES, pairs)  122 us
    ppermute x28, starting transfers between devices, send(): return lax.ppermute(value, AXES, pairs)  43.4 us
    pallas_call x2, Pallas kernels, expert_rows(): pl.pallas_call(lambda *a: ffn_kernel(phase, len(weights), cap, *a), in_sp...  36.5 us
    unnamed x70, local copies, waits for them, and re-layouts  23.5 us
    pallas_call x2, Pallas kernels, combine_rows(): pl.pallas_call(lambda *a: combine_kernel(experts, cap, last, *a), grid_sp...  12.5 us
    pallas_call x2, Pallas kernels, gather_rows(): pl.pallas_call(functools.partial(lambda *a: gather_kernel(experts, cap, *...  10.3 us
  transfers between devices with their start and end apart: 28, of which 15 were waited for; matrix products, arithmetic and copies ran while one was open for 1% of the time, Pallas kernels for 13%

profile of v1, /device:TPU:0, one launch (start us, length us, event | category | flops | bytes accessed | tf_op | source)
XLA Modules:
  0.0 259.0 jit_solution(1837203876350949998)
XLA Ops:
  1.5 2.2 copy-done
  3.7 2.2 copy-done.1
  5.9 2.7 %shard_map.91.a_9_ = bf16[16432,128]{1,0:T(8,128)(2,1)} custom-call(s32[1]{0:T(128)} %bitcast.13.a_0_, bf16[2,8192,128]{2,1,0:T(8,128)(2,1)S(1)} %bitcast.31, bf16[2,8192,128]{2,1,0:T(8,128)(2,1)S(1)} %bitcast.32, s32[2,32,2]{2,1,0:T(8,128)S(1)} %copy.12.a_3_, s32[2,16,4]{2,1,0:T(8,128)S(1)} %copy.13.a_4_), custom_call_target="tpu_custom_call" | custom-call | bytes 8400000 | tf_op jit(solution)/shard_map/pallas_call | solution.py:76
  8.6 2.7 %collective-permute-start.1 = (bf16[16432,128]{1,0:T(8,128)(2,1)}, bf16[16432,128]{1,0:T(8,128)(2,1)}, u32[]{:S(2)}, u32[]{:S(2)}) collective-permute-start(bf16[16432,128]{1,0:T(8,128)(2,1)} %shard_map.91.a_9_), channel_id=1, source_target_pairs={{6,4},{7,5},{10,8},{11,9},{12,10},{13,11},{22,20},{23,21},{26,24},... | collective-permute-start | bytes 12619784 | tf_op jit(solution)/shard_map/ppermute | solution.py:41
  11.3 6.9 %collective-permute-start = (bf16[16432,128]{1,0:T(8,128)(2,1)}, bf16[16432,128]{1,0:T(8,128)(2,1)}, u32[]{:S(2)}, u32[]{:S(2)}) collective-permute-start(bf16[16432,128]{1,0:T(8,128)(2,1)} %shard_map.91.a_9_), channel_id=1, source_target_pairs={{0,2},{1,3},{10,12},{11,13},{12,14},{13,15},{16,18},{17,19},{26,28... | collective-permute-start | bytes 12619784 | tf_op jit(solution)/shard_map/ppermute | solution.py:41
  18.2 1.5 collective-permute-start.2
  19.7 2.2 collective-permute-done.2
  21.9 1.5 collective-permute-start.6
  23.5 5.2 %all-gather = s32[2,8,512]{2,0,1:T(2,128)S(1)} all-gather(s32[2,2,512]{2,0,1:T(2,128)S(1)} %copy.14), channel_id=2, replica_groups=mesh['grp'=4,'exp'=8] {'grp'}, dimensions={1}, use_global_device_ids=true | all-gather | bytes 40960 | tf_op jit(solution)/shard_map/all_gather | solution.py:382
  28.8 5.2 %shard_map.92 = (bf16[2,384,512]{2,1,0:T(8,128)(2,1)S(1)}, bf16[2,384,512]{2,1,0:T(8,128)(2,1)S(1)}, bf16[2,384,512]{2,1,0:T(8,128)(2,1)S(1)}, bf16[2,384,512]{2,1,0:T(8,128)(2,1)S(1)}) custom-call(s32[8]{0:T(128)S(1)} %stack.99.a_0_, bf16[2048,512]{1,0:T(8,128)(2,1)} %bitcast.20.a_1_, s32[4,2,512]{2,1,0:T(2,128)S(1)} %squeeze.18.a_2_), custom_call_target="tpu_custom_call" | custom-call | flops 1610612736 | bytes 12000000 | tf_op jit(solution)/shard_map/pallas_call | solution.py:133
  34.4 1.5 collective-permute-start.4
  36.3 1.4 collective-permute-start.5
  37.8 17.0 %collective-permute-done.4.a_3_ = bf16[2,384,512]{2,1,0:T(8,128)(2,1)S(1)} collective-permute-done((bf16[2,384,512]{2,1,0:T(8,128)(2,1)S(1)}, bf16[2,384,512]{2,1,0:T(8,128)(2,1)S(1)}, u32[]{:S(2)}, u32[]{:S(2)}) %collective-permute-start.4) | collective-permute-done | bytes 786464 | tf_op jit(solution)/shard_map/ppermute | solution.py:41
  54.8 15.4 %collective-permute-done.5.a_4_ = bf16[2,384,512]{2,1,0:T(8,128)(2,1)S(1)} collective-permute-done((bf16[2,384,512]{2,1,0:T(8,128)(2,1)S(1)}, bf16[2,384,512]{2,1,0:T(8,128)(2,1)S(1)}, u32[]{:S(2)}, u32[]{:S(2)}) %collective-permute-start.5) | collective-permute-done | bytes 786464 | tf_op jit(solution)/shard_map/ppermute | solution.py:41
  70.1 2.7 %collective-permute-start.7 = (bf16[16432,128]{1,0:T(8,128)(2,1)}, bf16[16432,128]{1,0:T(8,128)(2,1)}, u32[]{:S(2)}, u32[]{:S(2)}) collective-permute-start(bf16[16432,128]{1,0:T(8,128)(2,1)} %collective-permute-done.a_10_.a_9_), channel_id=1, source_target_pairs={{2,4},{3,5},{12,14},{13,15},{18,20},{19,21},{28,30},{29,31}} | collective-permute-start | bytes 12619784 | tf_op jit(solution)/shard_map/ppermute | solution.py:41
  72.9 2.6 %collective-permute-start.8 = (bf16[16432,128]{1,0:T(8,128)(2,1)}, bf16[16432,128]{1,0:T(8,128)(2,1)}, u32[]{:S(2)}, u32[]{:S(2)}) collective-permute-start(bf16[16432,128]{1,0:T(8,128)(2,1)} %collective-permute-done.1.a_11_.a_10_), channel_id=1, source_target_pairs={{4,2},{5,3},{10,8},{11,9},{20,18},{21,19},{26,24},{27,25}} | collective-permute-start | bytes 12619784 | tf_op jit(solution)/shard_map/ppermute | solution.py:41
  75.5 5.2 %shard_map.93 = (bf16[2,384,512]{2,1,0:T(8,128)(2,1)S(1)}, bf16[2,384,512]{2,1,0:T(8,128)(2,1)S(1)}, bf16[2,384,512]{2,1,0:T(8,128)(2,1)S(1)}, bf16[2,384,512]{2,1,0:T(8,128)(2,1)S(1)}) custom-call(s32[8]{0:T(128)S(1)} %stack.99.a_0_, bf16[2048,512]{1,0:T(8,128)(2,1)} %collective-permute-done.6.a_1_, s32[4,2,512]{2,1,0:T(2,128)S(1)} %squeeze.19.a_2_), custom_call_target="tpu_custom_call" | custom-call | flops 1610612736 | bytes 12000000 | tf_op jit(solution)/shard_map/pallas_call | solution.py:133
  81.6 1.5 collective-permute-start.10
  84.7 17.2 %collective-permute-done.10.a_7_ = bf16[2,384,512]{2,1,0:T(8,128)(2,1)S(1)} collective-permute-done((bf16[2,384,512]{2,1,0:T(8,128)(2,1)S(1)}, bf16[2,384,512]{2,1,0:T(8,128)(2,1)S(1)}, u32[]{:S(2)}, u32[]{:S(2)}) %collective-permute-start.10) | collective-permute-done | bytes 786464 | tf_op jit(solution)/shard_map/ppermute | solution.py:41
  102.8 15.2 %collective-permute-done.11.a_8_ = bf16[2,384,512]{2,1,0:T(8,128)(2,1)S(1)} collective-permute-done((bf16[2,384,512]{2,1,0:T(8,128)(2,1)S(1)}, bf16[2,384,512]{2,1,0:T(8,128)(2,1)S(1)}, u32[]{:S(2)}, u32[]{:S(2)}) %collective-permute-start.11) | collective-permute-done | bytes 786464 | tf_op jit(solution)/shard_map/ppermute | solution.py:41
  118.9 2.6 %collective-permute-start.12 = (bf16[16432,128]{1,0:T(8,128)(2,1)}, bf16[16432,128]{1,0:T(8,128)(2,1)}, u32[]{:S(2)}, u32[]{:S(2)}) collective-permute-start(bf16[16432,128]{1,0:T(8,128)(2,1)} %collective-permute-done.7.a_11_), channel_id=1, source_target_pairs={{4,6},{5,7},{20,22},{21,23}} | collective-permute-start | bytes 12619784 | tf_op jit(solution)/shard_map/ppermute | solution.py:41
  121.5 1.3 collective-permute-start.13
  124.0 1.3 pad_add_fusion.1
  125.3 1.1 copy-done.3
  126.4 1.1 copy-done.5
  127.5 1.1 copy-done.7
  128.7 1.1 copy-done.10
  129.8 18.1 %shard_map.94 = (bf16[96,2048]{1,0:T(8,128)(2,1)S(1)}, bf16[96,2048]{1,0:T(8,128)(2,1)S(1)}, bf16[96,2048]{1,0:T(8,128)(2,1)S(1)}, bf16[96,2048]{1,0:T(8,128)(2,...) custom-call(s32[2]{0:T(128)S(1)} %get-tuple-element.116.a_0_, ...), custom_call_target="tpu_custom_call" | custom-call | flops 6442450944 | bytes 12000000 | tf_op jit(solution)/shard_map/pallas_call | solution.py:274
  148.7 5.6 %collective-permute-start.14 = (bf16[96,2048]{1,0:T(8,128)(2,1)S(1)}, bf16[96,2048]{1,0:T(8,128)(2,1)S(1)}, u32[]{:S(2)}, u32[]{:S(2)}) collective-permute-start(bf16[96,2048]{1,0:T(8,128)(2,1)S(1)} %get-tuple-element.87), channel_id=1, source_target_pairs={{0,8},{1,9},{2,10},{3,11},{4,12},{5,13},{6,14},{7,15},{8,0},{9,1},... | collective-permute-start | bytes 1179656 | tf_op jit(solution)/shard_map/ppermute | solution.py:41
  154.3 1.5 collective-permute-start.15
  156.4 9.9 %collective-permute-done.15.a_5_ = bf16[96,2048]{1,0:T(8,128)(2,1)S(1)} collective-permute-done((bf16[96,2048]{1,0:T(8,128)(2,1)S(1)}, bf16[96,2048]{1,0:T(8,128)(2,1)S(1)}, u32[]{:S(2)}, u32[]{:S(2)}) %collective-permute-start.15) | collective-permute-done | bytes 393248 | tf_op jit(solution)/shard_map/ppermute | solution.py:41
  166.3 6.5 %collective-permute-done.16.a_6_ = bf16[96,2048]{1,0:T(8,128)(2,1)S(1)} collective-permute-done((bf16[96,2048]{1,0:T(8,128)(2,1)S(1)}, bf16[96,2048]{1,0:T(8,128)(2,1)S(1)}, u32[]{:S(2)}, u32[]{:S(2)}) %collective-permute-start.16) | collective-permute-done | bytes 393248 | tf_op jit(solution)/shard_map/ppermute | solution.py:41
  172.8 1.5 collective-permute-start.19
  174.3 2.0 collective-permute-start.20
  176.8 8.9 %collective-permute-done.19.a_9_ = bf16[96,2048]{1,0:T(8,128)(2,1)S(1)} collective-permute-done((bf16[96,2048]{1,0:T(8,128)(2,1)S(1)}, bf16[96,2048]{1,0:T(8,128)(2,1)S(1)}, u32[]{:S(2)}, u32[]{:S(2)}) %collective-permute-start.19) | collective-permute-done | bytes 393248 | tf_op jit(solution)/shard_map/ppermute | solution.py:41
  185.7 8.8 %collective-permute-done.20.a_10_ = bf16[96,2048]{1,0:T(8,128)(2,1)S(1)} collective-permute-done((bf16[96,2048]{1,0:T(8,128)(2,1)S(1)}, bf16[96,2048]{1,0:T(8,128)(2,1)S(1)}, u32[]{:S(2)}, u32[]{:S(2)}) %collective-permute-start.20) | collective-permute-done | bytes 393248 | tf_op jit(solution)/shard_map/ppermute | solution.py:41
  194.6 18.3 %shard_map.95 = (bf16[96,2048]{1,0:T(8,128)(2,1)S(1)}, bf16[96,2048]{1,0:T(8,128)(2,1)S(1)}, bf16[96,2048]{1,0:T(8,128)(2,1)S(1)}, bf16[96,2048]{1,0:T(8,128)(2,...) custom-call(s32[2]{0:T(128)S(1)} %get-tuple-element.115.a_0_, ...), custom_call_target="tpu_custom_call" | custom-call | flops 6442450944 | bytes 12000000 | tf_op jit(solution)/shard_map/pallas_call | solution.py:274
  213.8 1.0 collective-permute-start.22
  215.7 1.4 collective-permute-start.24
  217.3 1.5 collective-permute-start.26
  218.7 7.0 %collective-permute-done.22.a_5_ = bf16[96,2048]{1,0:T(8,128)(2,1)S(1)} collective-permute-done((bf16[96,2048]{1,0:T(8,128)(2,1)S(1)}, bf16[96,2048]{1,0:T(8,128)(2,1)S(1)}, u32[]{:S(2)}, u32[]{:S(2)}) %collective-permute-start.22) | collective-permute-done | bytes 393248 | tf_op jit(solution)/shard_map/ppermute | solution.py:41
  226.1 1.0 copy-done.14
  227.1 1.0 copy-done.16
  231.1 1.0 copy-done.24
  234.1 5.8 %shard_map.96.a_11_ = f32[512,2048]{1,0:T(8,128)S(1)} custom-call(s32[8]{0:T(128)S(1)} %stack.108.a_0_, s32[2,512]{1,0:T(2,128)S(1)} %bitcast.35, f32[2,512]{1,0:T(2,128)S(1)} %bitcast.37, bf16[96,2048]{1,0:T(8,128)(2,1)S(1)} %copy-done.31, bf16[96,2048]{1,0:T(8,128)(2,1)S(1)} %copy-done.14, bf16[96,2048]{1,0:T(8,128)(2,1)S(1)} %copy-done.16, ...), custom_call_target="tpu_custom_call" | custom-call | flops 3221225472 | bytes 9000000 | tf_op jit(solution)/shard_map/pallas_call | solution.py:336
  239.9 5.2 %collective-permute-done.26.a_9_ = bf16[96,2048]{1,0:T(8,128)(2,1)S(1)} collective-permute-done((bf16[96,2048]{1,0:T(8,128)(2,1)}, bf16[96,2048]{1,0:T(8,128)(2,1)S(1)}, u32[]{:S(2)}, u32[]{:S(2)}) %collective-permute-start.26) | collective-permute-done | bytes 393248 | tf_op jit(solution)/shard_map/ppermute | solution.py:41
  245.1 7.1 %collective-permute-done.27.a_10_ = bf16[96,2048]{1,0:T(8,128)(2,1)S(1)} collective-permute-done((bf16[96,2048]{1,0:T(8,128)(2,1)}, bf16[96,2048]{1,0:T(8,128)(2,1)S(1)}, u32[]{:S(2)}, u32[]{:S(2)}) %collective-permute-start.27) | collective-permute-done | bytes 393248 | tf_op jit(solution)/shard_map/ppermute | solution.py:41
  252.3 6.7 %shard_map.97 = bf16[512,2048]{1,0:T(8,128)(2,1)} custom-call(s32[8]{0:T(128)S(1)} %stack.92.a_0_, s32[2,512]{1,0:T(2,128)S(1)} %bitcast.36, f32[2,512]{1,0:T(2,128)S(1)} %bitcast.38, bf16[96,2048]{1,0:T(8,128)(2,1)S(1)} %copy-done.28, bf16[96,2048]{1,0:T(8,128)(2,1)S(1)} %collective-permute-done.21.a_4_, bf16[96,2048]{1,0:T(8,128)(2,1)S(1)} %collective-permute-done.22.a_5_, ...), custom_call_target="tpu_custom_call" | custom-call | flops 3221225472 | bytes 9000000 | tf_op jit(solution)/shard_map/pallas_call | solution.py:336
  (97 shorter events, 17.3 us)
Async XLA Ops:
  1.5 2.2 copy-start
  3.7 2.2 copy-start.1
  5.9 12.3 %copy-start.12 = (s32[1,512,2]{1,2,0:T(2,128)S(1)}, s32[1,512,2]{1,2,0:T(2,128)}, u32[]{:S(2)}) copy-start(s32[1,512,2]{1,2,0:T(2,128)} %param.10) | copy-start | bytes 12292
  8.6 61.5 %collective-permute-start.1 = (bf16[16432,128]{1,0:T(8,128)(2,1)}, bf16[16432,128]{1,0:T(8,128)(2,1)}, u32[]{:S(2)}, u32[]{:S(2)}) collective-permute-start(bf16[16432,128]{1,0:T(8,128)(2,1)} %shard_map.91.a_9_), channel_id=1, source_target_pairs={{6,4},{7,5},{10,8},{11,9},{12,10},{13,11},{22,20},{23,21},{26,24},... | collective-permute-start | bytes 12619784 | tf_op jit(solution)/shard_map/ppermute | solution.py:41
  11.3 58.9 %collective-permute-start = (bf16[16432,128]{1,0:T(8,128)(2,1)}, bf16[16432,128]{1,0:T(8,128)(2,1)}, u32[]{:S(2)}, u32[]{:S(2)}) collective-permute-start(bf16[16432,128]{1,0:T(8,128)(2,1)} %shard_map.91.a_9_), channel_id=1, source_target_pairs={{0,2},{1,3},{10,12},{11,13},{12,14},{13,15},{16,18},{17,19},{26,28... | collective-permute-start | bytes 12619784 | tf_op jit(solution)/shard_map/ppermute | solution.py:41
  18.2 3.7 %collective-permute-start.2 = (s32[2,512]{1,0:T(2,128)S(1)}, s32[2,512]{1,0:T(2,128)S(1)}, u32[]{:S(2)}, u32[]{:S(2)}) collective-permute-start(s32[2,512]{1,0:T(2,128)S(1)} %bitcast.33), channel_id=1, source_target_pairs={{0,1},{1,0},{2,3},{3,2},{4,5},{5,4},{6,7},{7,6},{8,9},{9,8},{10,11... | collective-permute-start | bytes 12296 | tf_op jit(solution)/shard_map/ppermute | solution.py:41
  21.9 48.2 %collective-permute-start.6 = (bf16[2048,512]{1,0:T(8,128)(2,1)}, bf16[2048,512]{1,0:T(8,128)(2,1)}, u32[]{:S(2)}, u32[]{:S(2)}) collective-permute-start(bf16[2048,512]{1,0:T(8,128)(2,1)} %bitcast.20.a_1_), channel_id=1, source_target_pairs={{0,1},{1,0},{2,3},{3,2},{4,5},{5,4},{6,7},{7,6},{8,9},{9,8},{10,11... | collective-permute-start | bytes 6291464 | tf_op jit(solution)/shard_map/ppermute | solution.py:41
  34.0 88.9 %copy-start.33 = (s32[8]{0:T(128)S(1)}, s32[8]{0:T(128)}, u32[]{:S(2)}) copy-start(s32[8]{0:T(128)} %constant.125.clone) | copy-start | bytes 100
  34.0 89.4 %copy-start.32 = (s32[8]{0:T(128)S(1)}, s32[8]{0:T(128)}, u32[]{:S(2)}) copy-start(s32[8]{0:T(128)} %constant.124.clone) | copy-start | bytes 100
  34.0 2.4 collective-permute-start.3
  34.4 20.4 %collective-permute-start.4 = (bf16[2,384,512]{2,1,0:T(8,128)(2,1)S(1)}, bf16[2,384,512]{2,1,0:T(8,128)(2,1)S(1)}, u32[]{:S(2)}, u32[]{:S(2)}) collective-permute-start(bf16[2,384,512]{2,1,0:T(8,128)(2,1)S(1)} %get-tuple-element.62), channel_id=1, source_target_pairs={{0,16},{1,17},{2,18},{3,19},{4,20},{5,21},{6,22},{7,23},{8,24},{9,... | collective-permute-start | bytes 2359304 | tf_op jit(solution)/shard_map/ppermute | solution.py:41
  36.3 33.8 %collective-permute-start.5 = (bf16[2,384,512]{2,1,0:T(8,128)(2,1)S(1)}, bf16[2,384,512]{2,1,0:T(8,128)(2,1)S(1)}, u32[]{:S(2)}, u32[]{:S(2)}) collective-permute-start(bf16[2,384,512]{2,1,0:T(8,128)(2,1)S(1)} %get-tuple-element.63), channel_id=1, source_target_pairs={{0,24},{1,25},{2,26},{3,27},{4,28},{5,29},{6,30},{7,31},{8,16},{9,... | collective-permute-start | bytes 2359304 | tf_op jit(solution)/shard_map/ppermute | solution.py:41
  70.1 48.7 %collective-permute-start.7 = (bf16[16432,128]{1,0:T(8,128)(2,1)}, bf16[16432,128]{1,0:T(8,128)(2,1)}, u32[]{:S(2)}, u32[]{:S(2)}) collective-permute-start(bf16[16432,128]{1,0:T(8,128)(2,1)} %collective-permute-done.a_10_.a_9_), channel_id=1, source_target_pairs={{2,4},{3,5},{12,14},{13,15},{18,20},{19,21},{28,30},{29,31}} | collective-permute-start | bytes 12619784 | tf_op jit(solution)/shard_map/ppermute | solution.py:41
  72.9 46.0 %collective-permute-start.8 = (bf16[16432,128]{1,0:T(8,128)(2,1)}, bf16[16432,128]{1,0:T(8,128)(2,1)}, u32[]{:S(2)}, u32[]{:S(2)}) collective-permute-start(bf16[16432,128]{1,0:T(8,128)(2,1)} %collective-permute-done.1.a_11_.a_10_), channel_id=1, source_target_pairs={{4,2},{5,3},{10,8},{11,9},{20,18},{21,19},{26,24},{27,25}} | collective-permute-start | bytes 12619784 | tf_op jit(solution)/shard_map/ppermute | solution.py:41
  81.6 2.3 collective-permute-start.9
  81.6 20.3 %collective-permute-start.10 = (bf16[2,384,512]{2,1,0:T(8,128)(2,1)S(1)}, bf16[2,384,512]{2,1,0:T(8,128)(2,1)S(1)}, u32[]{:S(2)}, u32[]{:S(2)}) collective-permute-start(bf16[2,384,512]{2,1,0:T(8,128)(2,1)S(1)} %get-tuple-element.74), channel_id=1, source_target_pairs={{0,16},{1,17},{2,18},{3,19},{4,20},{5,21},{6,22},{7,23},{8,24},{9,... | collective-permute-start | bytes 2359304 | tf_op jit(solution)/shard_map/ppermute | solution.py:41
  83.1 34.9 %collective-permute-start.11 = (bf16[2,384,512]{2,1,0:T(8,128)(2,1)S(1)}, bf16[2,384,512]{2,1,0:T(8,128)(2,1)S(1)}, u32[]{:S(2)}, u32[]{:S(2)}) collective-permute-start(bf16[2,384,512]{2,1,0:T(8,128)(2,1)S(1)} %get-tuple-element.75), channel_id=1, source_target_pairs={{0,24},{1,25},{2,26},{3,27},{4,28},{5,29},{6,30},{7,31},{8,16},{9,... | collective-permute-start | bytes 2359304 | tf_op jit(solution)/shard_map/ppermute | solution.py:41
  118.9 75.7 %collective-permute-start.12 = (bf16[16432,128]{1,0:T(8,128)(2,1)}, bf16[16432,128]{1,0:T(8,128)(2,1)}, u32[]{:S(2)}, u32[]{:S(2)}) collective-permute-start(bf16[16432,128]{1,0:T(8,128)(2,1)} %collective-permute-done.7.a_11_), channel_id=1, source_target_pairs={{4,6},{5,7},{20,22},{21,23}} | collective-permute-start | bytes 12619784 | tf_op jit(solution)/shard_map/ppermute | solution.py:41
  121.5 73.1 %collective-permute-start.13 = (bf16[16432,128]{1,0:T(8,128)(2,1)}, bf16[16432,128]{1,0:T(8,128)(2,1)}, u32[]{:S(2)}, u32[]{:S(2)}) collective-permute-start(bf16[16432,128]{1,0:T(8,128)(2,1)} %collective-permute-done.8.a_12_), channel_id=1, source_target_pairs={{2,0},{3,1},{18,16},{19,17}} | collective-permute-start | bytes 12619784 | tf_op jit(solution)/shard_map/ppermute | solution.py:41
  125.3 1.1 copy-start.3
  126.4 1.1 copy-start.5
  127.5 1.1 copy-start.7
  128.7 1.1 copy-start.10
  129.8 64.8 %copy-start.8 = (bf16[2,384,512]{2,1,0:T(8,128)(2,1)S(1)}, bf16[2,384,512]{2,1,0:T(8,128)(2,1)}, u32[]{:S(2)}) copy-start(bf16[2,384,512]{2,1,0:T(8,128)(2,1)} %copy-done.6) | copy-start | bytes 2359300
  129.8 64.8 %copy-start.11 = (bf16[2,384,512]{2,1,0:T(8,128)(2,1)S(1)}, bf16[2,384,512]{2,1,0:T(8,128)(2,1)}, u32[]{:S(2)}) copy-start(bf16[2,384,512]{2,1,0:T(8,128)(2,1)} %copy-done.9) | copy-start | bytes 2359300
  148.7 7.1 %collective-permute-start.14 = (bf16[96,2048]{1,0:T(8,128)(2,1)S(1)}, bf16[96,2048]{1,0:T(8,128)(2,1)S(1)}, u32[]{:S(2)}, u32[]{:S(2)}) collective-permute-start(bf16[96,2048]{1,0:T(8,128)(2,1)S(1)} %get-tuple-element.87), channel_id=1, source_target_pairs={{0,8},{1,9},{2,10},{3,11},{4,12},{5,13},{6,14},{7,15},{8,0},{9,1},... | collective-permute-start | bytes 1179656 | tf_op jit(solution)/shard_map/ppermute | solution.py:41
  154.3 12.0 %collective-permute-start.15 = (bf16[96,2048]{1,0:T(8,128)(2,1)S(1)}, bf16[96,2048]{1,0:T(8,128)(2,1)S(1)}, u32[]{:S(2)}, u32[]{:S(2)}) collective-permute-start(bf16[96,2048]{1,0:T(8,128)(2,1)S(1)} %get-tuple-element.88), channel_id=1, source_target_pairs={{0,16},{1,17},{2,18},{3,19},{4,20},{5,21},{6,22},{7,23},{8,24},{9,... | collective-permute-start | bytes 1179656 | tf_op jit(solution)/shard_map/ppermute | solution.py:41
  155.8 17.0 %collective-permute-start.16 = (bf16[96,2048]{1,0:T(8,128)(2,1)S(1)}, bf16[96,2048]{1,0:T(8,128)(2,1)S(1)}, u32[]{:S(2)}, u32[]{:S(2)}) collective-permute-start(bf16[96,2048]{1,0:T(8,128)(2,1)S(1)} %get-tuple-element.89), channel_id=1, source_target_pairs={{0,24},{1,25},{2,26},{3,27},{4,28},{5,29},{6,30},{7,31},{8,16},{9,... | collective-permute-start | bytes 1179656 | tf_op jit(solution)/shard_map/ppermute | solution.py:41
  155.8 57.2 %copy-start.13 = (bf16[96,2048]{1,0:T(8,128)(2,1)}, bf16[96,2048]{1,0:T(8,128)(2,1)S(1)}, u32[]{:S(2)}) copy-start(bf16[96,2048]{1,0:T(8,128)(2,1)S(1)} %collective-permute-done.14.a_4_) | copy-start | bytes 1179652
  155.8 18.4 %collective-permute-start.17 = (bf16[96,2048]{1,0:T(8,128)(2,1)S(1)}, bf16[96,2048]{1,0:T(8,128)(2,1)S(1)}, u32[]{:S(2)}, u32[]{:S(2)}) collective-permute-start(bf16[96,2048]{1,0:T(8,128)(2,1)S(1)} %get-tuple-element.90), channel_id=1, source_target_pairs={{0,1},{1,0},{2,3},{3,2},{4,5},{5,4},{6,7},{7,6},{8,9},{9,8},{10,11... | collective-permute-start | bytes 1179656 | tf_op jit(solution)/shard_map/ppermute | solution.py:41
  166.3 46.7 %copy-start.15 = (bf16[96,2048]{1,0:T(8,128)(2,1)}, bf16[96,2048]{1,0:T(8,128)(2,1)S(1)}, u32[]{:S(2)}) copy-start(bf16[96,2048]{1,0:T(8,128)(2,1)S(1)} %collective-permute-done.15.a_5_) | copy-start | bytes 1179652
  166.3 10.5 %collective-permute-start.18 = (bf16[96,2048]{1,0:T(8,128)(2,1)S(1)}, bf16[96,2048]{1,0:T(8,128)(2,1)S(1)}, u32[]{:S(2)}, u32[]{:S(2)}) collective-permute-start(bf16[96,2048]{1,0:T(8,128)(2,1)S(1)} %get-tuple-element.91), channel_id=1, source_target_pairs={{0,9},{1,8},{2,11},{3,10},{4,13},{5,12},{6,15},{7,14},{8,1},{9,0},... | collective-permute-start | bytes 1179656 | tf_op jit(solution)/shard_map/ppermute | solution.py:41
  172.8 40.2 %copy-start.17 = (bf16[96,2048]{1,0:T(8,128)(2,1)}, bf16[96,2048]{1,0:T(8,128)(2,1)S(1)}, u32[]{:S(2)}) copy-start(bf16[96,2048]{1,0:T(8,128)(2,1)S(1)} %collective-permute-done.16.a_6_) | copy-start | bytes 1179652
  172.8 13.0 %collective-permute-start.19 = (bf16[96,2048]{1,0:T(8,128)(2,1)S(1)}, bf16[96,2048]{1,0:T(8,128)(2,1)S(1)}, u32[]{:S(2)}, u32[]{:S(2)}) collective-permute-start(bf16[96,2048]{1,0:T(8,128)(2,1)S(1)} %get-tuple-element.92), channel_id=1, source_target_pairs={{0,17},{1,16},{2,19},{3,18},{4,21},{5,20},{6,23},{7,22},{8,25},{9,... | collective-permute-start | bytes 1179656 | tf_op jit(solution)/shard_map/ppermute | solution.py:41
  174.3 38.7 %copy-start.19 = (bf16[96,2048]{1,0:T(8,128)(2,1)}, bf16[96,2048]{1,0:T(8,128)(2,1)S(1)}, u32[]{:S(2)}) copy-start(bf16[96,2048]{1,0:T(8,128)(2,1)S(1)} %collective-permute-done.17.a_7_) | copy-start | bytes 1179652
  174.3 20.3 %collective-permute-start.20 = (bf16[96,2048]{1,0:T(8,128)(2,1)S(1)}, bf16[96,2048]{1,0:T(8,128)(2,1)S(1)}, u32[]{:S(2)}, u32[]{:S(2)}) collective-permute-start(bf16[96,2048]{1,0:T(8,128)(2,1)S(1)} %get-tuple-element.93), channel_id=1, source_target_pairs={{0,25},{1,24},{2,27},{3,26},{4,29},{5,28},{6,31},{7,30},{8,17},{9,... | collective-permute-start | bytes 1179656 | tf_op jit(solution)/shard_map/ppermute | solution.py:41
  176.8 36.2 %copy-start.21 = (bf16[96,2048]{1,0:T(8,128)(2,1)}, bf16[96,2048]{1,0:T(8,128)(2,1)S(1)}, u32[]{:S(2)}) copy-start(bf16[96,2048]{1,0:T(8,128)(2,1)S(1)} %collective-permute-done.18.a_8_) | copy-start | bytes 1179652
  185.7 27.3 %copy-start.23 = (bf16[96,2048]{1,0:T(8,128)(2,1)}, bf16[96,2048]{1,0:T(8,128)(2,1)S(1)}, u32[]{:S(2)}) copy-start(bf16[96,2048]{1,0:T(8,128)(2,1)S(1)} %collective-permute-done.19.a_9_) | copy-start | bytes 1179652
  194.6 18.5 %copy-start.25 = (bf16[96,2048]{1,0:T(8,128)(2,1)}, bf16[96,2048]{1,0:T(8,128)(2,1)S(1)}, u32[]{:S(2)}) copy-start(bf16[96,2048]{1,0:T(8,128)(2,1)S(1)} %collective-permute-done.20.a_10_) | copy-start | bytes 1179652
  194.6 31.5 %copy-start.29 = (f32[1,512,2]{1,2,0:T(2,128)S(1)}, f32[1,512,2]{1,2,0:T(2,128)}, u32[]{:S(2)}) copy-start(f32[1,512,2]{1,2,0:T(2,128)} %param.11) | copy-start | bytes 12292
  213.8 3.5 %collective-permute-start.21 = (bf16[96,2048]{1,0:T(8,128)(2,1)S(1)}, bf16[96,2048]{1,0:T(8,128)(2,1)S(1)}, u32[]{:S(2)}, u32[]{:S(2)}) collective-permute-start(bf16[96,2048]{1,0:T(8,128)(2,1)S(1)} %get-tuple-element.97), channel_id=1, source_target_pairs={{0,8},{1,9},{2,10},{3,11},{4,12},{5,13},{6,14},{7,15},{8,0},{9,1},... | collective-permute-start | bytes 1179656 | tf_op jit(solution)/shard_map/ppermute | solution.py:41
  213.8 11.9 %collective-permute-start.22 = (bf16[96,2048]{1,0:T(8,128)(2,1)S(1)}, bf16[96,2048]{1,0:T(8,128)(2,1)S(1)}, u32[]{:S(2)}, u32[]{:S(2)}) collective-permute-start(bf16[96,2048]{1,0:T(8,128)(2,1)S(1)} %get-tuple-element.98), channel_id=1, source_target_pairs={{0,16},{1,17},{2,18},{3,19},{4,20},{5,21},{6,22},{7,23},{8,24},{9,... | collective-permute-start | bytes 1179656 | tf_op jit(solution)/shard_map/ppermute | solution.py:41
  214.8 25.1 %collective-permute-start.23 = (bf16[96,2048]{1,0:T(8,128)(2,1)}, bf16[96,2048]{1,0:T(8,128)(2,1)S(1)}, u32[]{:S(2)}, u32[]{:S(2)}) collective-permute-start(bf16[96,2048]{1,0:T(8,128)(2,1)} %get-tuple-element.99), channel_id=1, source_target_pairs={{0,24},{1,25},{2,26},{3,27},{4,28},{5,29},{6,30},{7,31},{8,16},{9,... | collective-permute-start | bytes 1179656 | tf_op jit(solution)/shard_map/ppermute | solution.py:41
  215.7 24.3 %collective-permute-start.24 = (bf16[96,2048]{1,0:T(8,128)(2,1)}, bf16[96,2048]{1,0:T(8,128)(2,1)S(1)}, u32[]{:S(2)}, u32[]{:S(2)}) collective-permute-start(bf16[96,2048]{1,0:T(8,128)(2,1)} %get-tuple-element.100), channel_id=1, source_target_pairs={{0,1},{1,0},{2,3},{3,2},{4,5},{5,4},{6,7},{7,6},{8,9},{9,8},{10,11... | collective-permute-start | bytes 1179656 | tf_op jit(solution)/shard_map/ppermute | solution.py:41
  217.0 22.9 %collective-permute-start.25 = (bf16[96,2048]{1,0:T(8,128)(2,1)}, bf16[96,2048]{1,0:T(8,128)(2,1)S(1)}, u32[]{:S(2)}, u32[]{:S(2)}) collective-permute-start(bf16[96,2048]{1,0:T(8,128)(2,1)} %get-tuple-element.101), channel_id=1, source_target_pairs={{0,9},{1,8},{2,11},{3,10},{4,13},{5,12},{6,15},{7,14},{8,1},{9,0},... | collective-permute-start | bytes 1179656 | tf_op jit(solution)/shard_map/ppermute | solution.py:41
  217.3 27.8 %collective-permute-start.26 = (bf16[96,2048]{1,0:T(8,128)(2,1)}, bf16[96,2048]{1,0:T(8,128)(2,1)S(1)}, u32[]{:S(2)}, u32[]{:S(2)}) collective-permute-start(bf16[96,2048]{1,0:T(8,128)(2,1)} %get-tuple-element.102), channel_id=1, source_target_pairs={{0,17},{1,16},{2,19},{3,18},{4,21},{5,20},{6,23},{7,22},{8,25},{9,... | collective-permute-start | bytes 1179656 | tf_op jit(solution)/shard_map/ppermute | solution.py:41
  225.7 26.6 %collective-permute-start.27 = (bf16[96,2048]{1,0:T(8,128)(2,1)}, bf16[96,2048]{1,0:T(8,128)(2,1)S(1)}, u32[]{:S(2)}, u32[]{:S(2)}) collective-permute-start(bf16[96,2048]{1,0:T(8,128)(2,1)} %get-tuple-element.103), channel_id=1, source_target_pairs={{0,25},{1,24},{2,27},{3,26},{4,29},{5,28},{6,31},{7,30},{8,17},{9,... | collective-permute-start | bytes 1179656 | tf_op jit(solution)/shard_map/ppermute | solution.py:41
  234.1 18.2 %copy-start.28 = (bf16[96,2048]{1,0:T(8,128)(2,1)S(1)}, bf16[96,2048]{1,0:T(8,128)(2,1)}, u32[]{:S(2)}) copy-start(bf16[96,2048]{1,0:T(8,128)(2,1)} %copy-done.27) | copy-start | bytes 1179652
  (14 other events, 13.1 us)

commit v2 on v1

v2 whole, which is shorter than its diff:
```python
import functools
import math

import jax
import jax.numpy as jnp
import numpy as np
from jax import lax
from jax.experimental import pallas as pl
from jax.experimental.pallas import tpu as pltpu
from jax.sharding import PartitionSpec as P

AXES = ("grp", "z", "x")
PLANE = ("x", "grp")


def place(core, plane):
    return jnp.where(plane < 2, core, 3 - core)


def all_pairs(rule):
    pairs = []
    for y in range(2):
        for core in range(2):
            for z in range(4):
                for x in range(2):
                    to = rule(y, core, z, x)
                    if to is not None:
                        ty, tc, tz, tx = to
                        pairs.append(((y * 2 + core) * 8 + z * 2 + x, (ty * 2 + tc) * 8 + tz * 2 + tx))
    return pairs


def along_z(step, senders):
    return all_pairs(lambda y, c, z, x: (y, c, z + step, x) if (z, c) in senders else None)


def send(value, pairs):
    return lax.ppermute(value, AXES, pairs)


def after(value, other):
    return lax.optimization_barrier((value, other))[0]


PIECES = 2
TABLE_ROWS = 16


def pack_kernel(pieces, which, up_ref, down_ref, up_at, down_at, out_ref):
    step = pl.program_id(0)

    @pl.when(step < pieces)
    def _():
        out_ref[...] = up_ref[0]

    @pl.when((step >= pieces) & (step < 2 * pieces))
    def _():
        out_ref[...] = down_ref[0]

    @pl.when(step == 2 * pieces)
    def _():
        ups, downs = up_at.shape[1], down_at.shape[1]
        out_ref[0:TABLE_ROWS, :] = jnp.zeros((TABLE_ROWS, out_ref.shape[1]), jnp.bfloat16)
        out_ref[0:ups, 0 : up_at.shape[2]] = up_at[0].astype(jnp.float32).astype(jnp.bfloat16)
        out_ref[ups : ups + downs, 0 : down_at.shape[2]] = (
            down_at[0].astype(jnp.float32).astype(jnp.bfloat16)
        )


def pack_weights(which, up, down, up_at, down_at):
    pieces = 2
    size, blk = up.shape[1], up.shape[2]
    step = size // pieces
    return pl.pallas_call(
        lambda *a: pack_kernel(pieces, *a),
        grid_spec=pltpu.PrefetchScalarGridSpec(
            num_scalar_prefetch=1,
            grid=(2 * pieces + 1,),
            in_specs=[
                pl.BlockSpec((1, step, blk), lambda i, w: (w[0], jnp.minimum(i, pieces - 1), 0)),
                pl.BlockSpec(
                    (1, step, blk), lambda i, w: (w[0], jnp.clip(i - pieces, 0, pieces - 1), 0)
                ),
                pl.BlockSpec((1,) + up_at.shape[1:], lambda i, w: (w[0], 0, 0)),
                pl.BlockSpec((1,) + down_at.shape[1:], lambda i, w: (w[0], 0, 0)),
            ],
            out_specs=pl.BlockSpec((step, blk), lambda i, w: (i, 0)),
        ),
        out_shape=jax.ShapeDtypeStruct((2 * size + TABLE_ROWS, blk), up.dtype),
        cost_estimate=pl.CostEstimate(flops=0, bytes_accessed=8_400_000, transcendentals=0),
        compiler_params=pltpu.CompilerParams(vmem_limit_bytes=60 * 2**20),
    )(which[None].astype(jnp.int32), up, down, up_at, down_at)


def slot_rows(first, second, experts):
    tokens = first.shape[1]
    ids = lax.broadcasted_iota(jnp.int32, (experts, tokens), 0)
    named = (ids == first) | (ids == second)
    before = lax.broadcasted_iota(jnp.int32, (tokens, tokens), 0) < lax.broadcasted_iota(
        jnp.int32, (tokens, tokens), 1
    )
    count = jnp.dot(
        jnp.where(named, 1.0, 0.0).astype(jnp.bfloat16),
        jnp.where(before, 1.0, 0.0).astype(jnp.bfloat16),
        preferred_element_type=jnp.float32,
    )
    return jnp.where(named, count.astype(jnp.int32), -1)


def exchange(rows):
    return lax.all_to_all(rows, PLANE, split_axis=0, concat_axis=0, tiled=True)


def gather_kernel(experts, cap, order, x_ref, choice_ref, out_ref, slots, pick):
    tokens = x_ref.shape[0]
    slots[...] = slot_rows(choice_ref[0, 0:1, :], choice_ref[0, 1:2, :], experts)
    row = lax.broadcasted_iota(jnp.int32, (cap, tokens), 0)
    for n in range(8):
        line = slots[pl.ds(order[n], 1), :]
        pick[n * cap : (n + 1) * cap, :] = jnp.where(line == row, 1.0, 0.0).astype(jnp.bfloat16)
    for n in range(0, 8, 2):
        rows = jnp.dot(
            pick[n * cap : (n + 2) * cap, :], x_ref[...], preferred_element_type=jnp.float32
        )
        out_ref[n] = rows[:cap].astype(jnp.bfloat16)
        out_ref[n + 1] = rows[cap:].astype(jnp.bfloat16)


def gather_rows(features, choices, order, experts, cap):
    parts, _, tokens = choices.shape
    width = features.shape[1]
    return pl.pallas_call(
        lambda *a: gather_kernel(experts, cap, *a),
        grid_spec=pltpu.PrefetchScalarGridSpec(
            num_scalar_prefetch=1,
            grid=(parts,),
            in_specs=[
                pl.BlockSpec((tokens, width), lambda b, order: (b, 0)),
                pl.BlockSpec((1, 2, tokens), lambda b, order: (b, 0, 0)),
            ],
            out_specs=pl.BlockSpec((8, cap, width), lambda b, order: (0, b, 0)),
            scratch_shapes=[
                pltpu.VMEM((experts, tokens), jnp.int32),
                pltpu.VMEM((8 * cap, tokens), jnp.bfloat16),
            ],
        ),
        out_shape=jax.ShapeDtypeStruct((8, parts * cap, width), jnp.bfloat16),
        cost_estimate=pl.CostEstimate(
            flops=2 * parts * 8 * cap * tokens * width, bytes_accessed=9_000_000, transcendentals=0
        ),
        compiler_params=pltpu.CompilerParams(vmem_limit_bytes=60 * 2**20),
    )(order, features, choices)


def gelu(v):
    half = 0.5 * v
    inner = v * (math.sqrt(2 / math.pi) + (math.sqrt(2 / math.pi) * 0.044715) * (v * v))
    return half + half * jnp.tanh(inner)


def ffn_kernel(n_weights, chosen, got_ref, *refs):
    sources, refs = refs[:n_weights], refs[n_weights:]
    out_ref, xs, wts, hid, res, packed, wide, table, x_sem, w_sem, o_sem = refs
    part_rows, width = got_ref.shape[1], got_ref.shape[2]
    blk = wts.shape[1]
    up_cols = hid.shape[1] // blk
    down_cols = res.shape[1] // blk
    up_depth, down_depth = 2 * blk, 4 * blk
    up_size = up_cols * up_depth

    total = up_size + down_cols * down_depth
    piece = total // PIECES

    def weight_copies(source):
        copies = [pltpu.make_async_copy(source.at[pl.ds(total, TABLE_ROWS)], packed, w_sem.at[0])]
        for n in range(PIECES):
            at = pl.ds(n * piece, piece)
            copies.append(pltpu.make_async_copy(source.at[at], wts.at[at], w_sem.at[2 + n]))
        return copies

    for i in range(n_weights):

        @pl.when(chosen[0] == i)
        def _(i=i):
            for one in weight_copies(sources[i]):
                one.start()

    in_copies = []
    for n in range(8):
        in_copies.append(
            pltpu.make_async_copy(
                got_ref.at[n],
                xs.at[
                    pl.ds((n // 4) * part_rows, part_rows), pl.ds((n % 4) * width, width)
                ],
                x_sem.at[n],
            )
        )
        in_copies[-1].start()
    waits = weight_copies(sources[0])
    waits[0].wait()
    wide[...] = packed[...].astype(jnp.float32).astype(jnp.int32)
    to_scalars = pltpu.make_async_copy(wide, table, w_sem.at[1])
    to_scalars.start()
    for one in in_copies:
        one.wait()
    to_scalars.wait()

    def block_product(source, rows, count, line, col, base):
        parts = []
        for i in range(count):
            at = pl.multiple_of(table[line + i, col] * blk, blk)
            parts.append(source[rows, pl.ds(at, blk)])
        return jnp.dot(
            jnp.concatenate(parts, axis=1),
            wts[base : base + count * blk, :],
            preferred_element_type=jnp.float32,
        )

    halves = [slice(0, part_rows), slice(part_rows, 2 * part_rows)]
    for col in range(up_cols):
        if (col * up_depth) % piece == 0:
            waits[1 + col * up_depth // piece].wait()
        for rows in halves:
            got = block_product(xs, rows, 2, 0, col, col * up_depth)
            hid[rows, col * blk : (col + 1) * blk] = gelu(got).astype(jnp.bfloat16)

    out_copies = []
    for col in range(down_cols):
        base = up_size + col * down_depth
        if base % piece == 0:
            waits[1 + base // piece].wait()
        for rows in halves:
            got = block_product(hid, rows, 4, 2, col, base)
            res[rows, col * blk : (col + 1) * blk] = got.astype(jnp.bfloat16)
        if (col + 1) % (down_cols // 2) == 0:
            half = (col + 1) // (down_cols // 2) - 1
            cols = pl.ds(half * (down_cols // 2) * blk, (down_cols // 2) * blk)
            out_copies.append(
                pltpu.make_async_copy(res.at[:, cols], out_ref.at[:, cols], o_sem.at[half])
            )
            out_copies[-1].start()
    for one in out_copies:
        one.wait()


def expert_rows(chosen, got, weights, hidden):
    _, part_rows, width = got.shape
    blk = weights[0].shape[1]
    rows, row_width = 2 * part_rows, 4 * width
    hbm = pl.BlockSpec(memory_space=pltpu.HBM)
    smem = pl.BlockSpec(memory_space=pltpu.SMEM)
    up_and_down = weights[0].shape[0] - TABLE_ROWS
    return pl.pallas_call(
        lambda *a: ffn_kernel(len(weights), *a),
        in_specs=[smem] + [hbm] * (1 + len(weights)),
        out_specs=hbm,
        out_shape=jax.ShapeDtypeStruct((rows, row_width), jnp.bfloat16),
        scratch_shapes=[
            pltpu.VMEM((rows, row_width), jnp.bfloat16),
            pltpu.VMEM((up_and_down, blk), jnp.bfloat16),
            pltpu.VMEM((rows, hidden), jnp.bfloat16),
            pltpu.VMEM((rows, row_width), jnp.bfloat16),
            pltpu.VMEM((TABLE_ROWS, blk), jnp.bfloat16),
            pltpu.VMEM((TABLE_ROWS, blk), jnp.int32),
            pltpu.SMEM((TABLE_ROWS, blk), jnp.int32),
            pltpu.SemaphoreType.DMA((8,)),
            pltpu.SemaphoreType.DMA((2 + PIECES,)),
            pltpu.SemaphoreType.DMA((2,)),
        ],
        cost_estimate=pl.CostEstimate(
            flops=4 * rows * up_and_down * blk,
            bytes_accessed=12_000_000,
            transcendentals=rows * hidden,
        ),
        compiler_params=pltpu.CompilerParams(vmem_limit_bytes=60 * 2**20),
    )(chosen[None].astype(jnp.int32), got, *weights)


def gate_matrix(order, slots, choice_ref, gate_ref, cap, high, low):
    tokens = choice_ref.shape[1]
    row = lax.broadcasted_iota(jnp.int32, (cap, tokens), 0)
    tops, rests = [], []
    for n in range(8):
        line = slots[pl.ds(order[n], 1), :]
        gate = jnp.where(choice_ref[0:1, :] == order[n], gate_ref[0:1, :], gate_ref[1:2, :])
        top = gate.astype(jnp.bfloat16).astype(jnp.float32)
        here = line == row
        tops.append(jnp.where(here, top, 0.0).astype(jnp.bfloat16))
        rests.append(jnp.where(here, gate - top, 0.0).astype(jnp.bfloat16))
    high[...] = jnp.concatenate(tops, axis=0).T
    low[...] = jnp.concatenate(rests, axis=0).T


def first_kernel(experts, cap, order_a, order_b, choice_ref, gate_ref, rows, sum_ref, *refs):
    high_b, low_b, slots, high, low = refs

    @pl.when(pl.program_id(0) == 0)
    def _():
        slots[...] = slot_rows(choice_ref[0:1, :], choice_ref[1:2, :], experts)
        gate_matrix(order_a, slots, choice_ref, gate_ref, cap, high, low)
        gate_matrix(order_b, slots, choice_ref, gate_ref, cap, high_b, low_b)

    total = jnp.dot(high[...], rows[...], preferred_element_type=jnp.float32)
    total += jnp.dot(low[...], rows[...], preferred_element_type=jnp.float32)
    sum_ref[...] = total


def combine_first(order_a, order_b, choice, gates, rows, experts, cap):
    tokens = choice.shape[1]
    columns, row_width = rows.shape
    chunk = 512
    whole = pl.BlockSpec((2, tokens), lambda j, a, c: (0, 0))
    matrix = pl.BlockSpec((tokens, columns), lambda j, a, c: (0, 0))
    return pl.pallas_call(
        lambda *a: first_kernel(experts, cap, *a),
        grid_spec=pltpu.PrefetchScalarGridSpec(
            num_scalar_prefetch=2,
            grid=(row_width // chunk,),
            in_specs=[whole, whole, pl.BlockSpec((columns, chunk), lambda j, a, c: (0, j))],
            out_specs=[pl.BlockSpec((tokens, chunk), lambda j, a, c: (0, j)), matrix, matrix],
            scratch_shapes=[
                pltpu.VMEM((experts, tokens), jnp.int32),
                pltpu.VMEM((tokens, columns), jnp.bfloat16),
                pltpu.VMEM((tokens, columns), jnp.bfloat16),
            ],
        ),
        out_shape=[jax.ShapeDtypeStruct((tokens, row_width), jnp.float32)]
        + [jax.ShapeDtypeStruct((tokens, columns), jnp.bfloat16)] * 2,
        cost_estimate=pl.CostEstimate(
            flops=4 * columns * tokens * row_width, bytes_accessed=9_000_000, transcendentals=0
        ),
        compiler_params=pltpu.CompilerParams(vmem_limit_bytes=60 * 2**20),
    )(order_a, order_b, choice, gates, rows)


def second_kernel(high, low, rows, sum_ref, out_ref):
    total = jnp.dot(high[...], rows[...], preferred_element_type=jnp.float32)
    total += jnp.dot(low[...], rows[...], preferred_element_type=jnp.float32)
    out_ref[...] = (total + sum_ref[...]).astype(out_ref.dtype)


def combine_second(high, low, rows, so_far):
    tokens, columns = high.shape
    row_width = rows.shape[1]
    chunk = 512
    matrix = pl.BlockSpec((tokens, columns), lambda j: (0, 0))
    block = pl.BlockSpec((tokens, chunk), lambda j: (0, j))
    return pl.pallas_call(
        second_kernel,
        grid=(row_width // chunk,),
        in_specs=[matrix, matrix, pl.BlockSpec((columns, chunk), lambda j: (0, j)), block],
        out_specs=block,
        out_shape=jax.ShapeDtypeStruct((tokens, row_width), jnp.bfloat16),
        cost_estimate=pl.CostEstimate(
            flops=4 * columns * tokens * row_width, bytes_accessed=9_000_000, transcendentals=0
        ),
        compiler_params=pltpu.CompilerParams(vmem_limit_bytes=60 * 2**20),
    )(high, low, rows, so_far)


def per_device_planes(
    attention_rows, expert_choice, gate_weights, up_blocks, up_values, down_blocks, down_values
):
    experts = 2 * lax.axis_size("z") * lax.axis_size("x")
    own_tokens = expert_choice.shape[1]
    cap = 3 * own_tokens // experts
    blk = up_values.shape[-1]
    hidden = up_values.shape[1] * blk
    g, z = lax.axis_index("grp"), lax.axis_index("z")
    y, core = g // 2, g % 2
    features = attention_rows[0]

    own = pack_weights(
        y,
        up_values.reshape(2, -1, blk),
        down_values.reshape(2, -1, blk),
        up_blocks.transpose(0, 2, 1),
        down_blocks.transpose(0, 2, 1),
    )
    r1 = send(own, along_z(1, ((0, 0), (1, 1), (2, 1))))
    l1 = send(own, along_z(-1, ((3, 0), (2, 1), (1, 1))))

    choice = expert_choice[0].T
    gates = gate_weights[0].T
    choices = lax.all_gather(after(choice, own), "grp")
    planes = [place(jnp.int32(d % 2), z) for d in range(8)]
    bases = [2 * (d // 4) + d % 4 // 2 for d in range(8)]
    order_a = jnp.stack([4 * planes[d] + bases[d] for d in range(8)]).astype(jnp.int32)
    order_b = jnp.stack([4 * (3 - planes[d]) + bases[d] for d in range(8)]).astype(jnp.int32)
    rows_a = gather_rows(features, choices, order_a, experts, cap)
    got_a = exchange(rows_a)
    rows_b = gather_rows(features, after(choices, rows_a), order_b, experts, cap)
    r1, l1, got_a, rows_b = lax.optimization_barrier((r1, l1, got_a, rows_b))
    r2 = send(r1, along_z(1, ((1, 0), (2, 1))))
    l2 = send(l1, along_z(-1, ((2, 0), (1, 1))))
    got_b = exchange(rows_b)

    pick = z * 2 + core
    take_a = jnp.array([0, 2, 1, 0, 2, 0, 0, 1], jnp.int32)[pick]
    take_b = jnp.array([5, 3, 3, 1, 2, 0, 4, 2], jnp.int32)[pick]
    out_a = expert_rows(take_a, got_a, (own, r1, l1), hidden)
    got_b, out_a = lax.optimization_barrier((got_b, out_a))
    back_a = exchange(out_a.reshape(8, cap, -1))
    r2, l2, out_a = lax.optimization_barrier((r2, l2, out_a))
    r3 = send(r2, along_z(1, ((2, 0),)))
    l3 = send(l2, along_z(-1, ((1, 0),)))
    r3, l3, back_a = lax.optimization_barrier((r3, l3, back_a))
    out_b = expert_rows(take_b, got_b, (r1, l1, r2, l2, r3, l3), hidden)
    back_b = exchange(out_b.reshape(8, cap, -1))
    sum_a, high, low = combine_first(
        after(order_a, out_b), order_b, choice, gates, back_a.reshape(8 * cap, -1), experts, cap
    )
    return combine_second(high, low, back_b.reshape(8 * cap, -1), sum_a)[None]


def expert_ffn(token_rows, up_rows, up_vals, down_rows, down_vals):
    row_count, row_width = token_rows.shape
    block_size = up_vals.shape[-1]
    in_blocks = row_width // block_size
    mid_blocks = up_rows.shape[0]
    pick_up = (up_rows[:, :, None] == jnp.arange(in_blocks)[None, None, :]).astype(jnp.bfloat16)
    chosen = jnp.einsum(
        "rnb,cin->rcib",
        token_rows.reshape(row_count, in_blocks, block_size),
        pick_up,
        preferred_element_type=jnp.float32,
    ).astype(jnp.bfloat16)
    hidden = jnp.einsum("rcib,cibd->rcd", chosen, up_vals, preferred_element_type=jnp.float32)
    hidden = jax.nn.gelu(hidden, approximate=True).astype(jnp.bfloat16)
    pick_down = (down_rows[:, :, None] == jnp.arange(mid_blocks)[None, None, :]).astype(
        jnp.bfloat16
    )
    chosen_mid = jnp.einsum(
        "rcb,jic->rjib", hidden, pick_down, preferred_element_type=jnp.float32
    ).astype(jnp.bfloat16)
    result = jnp.einsum("rjib,jibd->rjd", chosen_mid, down_vals, preferred_element_type=jnp.float32)
    return result.reshape(row_count, row_width).astype(jnp.bfloat16)


def padded_rows(all_rows, weights):
    total_rows, row_width = all_rows.shape
    tile_rows = math.gcd(total_rows, 128)
    tiles = all_rows.reshape(total_rows // tile_rows, tile_rows, row_width)
    mapped = lax.map(
        lambda tile_block: expert_ffn(tile_block, weights[0], weights[1], weights[2], weights[3]),
        tiles,
    )
    return mapped.reshape(total_rows, row_width)


def slot_targets(route_ids, expert_total, capacity):
    pair_ids = route_ids.reshape(-1)
    one_hot = (pair_ids[:, None] == jnp.arange(expert_total, dtype=jnp.int32)[None, :]).astype(
        jnp.int32
    )
    earlier = jnp.cumsum(one_hot, axis=0) - one_hot
    slot_number = jnp.sum(earlier * one_hot, axis=1)
    return (pair_ids * capacity + slot_number).reshape(route_ids.shape)


def place_rows(token_rows, targets, slot_total):
    buffer_rows = jnp.zeros((slot_total, token_rows.shape[1]), token_rows.dtype)
    buffer_rows = buffer_rows.at[targets[:, 0]].set(token_rows)
    return buffer_rows.at[targets[:, 1]].set(token_rows)


def per_device(
    attention_rows, expert_choice, gate_weights, up_blocks, up_values, down_blocks, down_values
):
    group_count = lax.axis_size("grp")
    expert_devices = lax.axis_size("exp")
    local_experts = up_values.shape[0]
    expert_total = local_experts * expert_devices
    own_tokens = expert_choice.shape[1]
    capacity = 3 * own_tokens // expert_total
    head_width = attention_rows.shape[2]
    row_width = head_width * group_count
    targets = slot_targets(expert_choice[0], expert_total, capacity)
    token_rows = lax.all_to_all(attention_rows, "grp", split_axis=1, concat_axis=2, tiled=True)[0]
    send_rows = place_rows(token_rows, targets, expert_total * capacity)
    send_rows = send_rows.reshape(expert_devices, local_experts, capacity, row_width)
    received = lax.all_to_all(send_rows, "exp", split_axis=0, concat_axis=0, tiled=True)
    outputs = []
    for local_index in range(local_experts):
        weights = (
            up_blocks[local_index],
            up_values[local_index],
            down_blocks[local_index],
            down_values[local_index],
        )
        expert_rows = received[:, local_index].reshape(expert_devices * capacity, row_width)
        expert_result = padded_rows(expert_rows, weights)
        outputs.append(expert_result.reshape(expert_devices, capacity, row_width))
    stacked = jnp.stack(outputs, axis=1)
    returned = lax.all_to_all(stacked, "exp", split_axis=0, concat_axis=0, tiled=True).reshape(
        expert_total * capacity, row_width
    )
    picked = returned[targets.reshape(-1)].reshape(own_tokens, 2, row_width)
    combined = jnp.sum(gate_weights[0][:, :, None] * picked.astype(jnp.float32), axis=1)
    return combined.astype(jnp.bfloat16)[None]


def solution(mesh):
    planes = mesh.shape["grp"] == 4 and mesh.shape["exp"] == 8
    exp = "exp"
    if planes:
        mesh = jax.sharding.Mesh(mesh.devices.reshape(4, 4, 2), AXES)
        exp = ("z", "x")
    return jax.shard_map(
        per_device_planes if planes else per_device,
        mesh=mesh,
        in_specs=(
            P(exp, None, "grp"),
            P(exp, "grp", None),
            P(exp, "grp", None),
            P(exp, None, None),
            P(exp, None, None, None, None),
            P(exp, None, None),
            P(exp, None, None, None, None),
        ),
        out_specs=P(exp, "grp", None),
        check_vma=False,
    )
```

time: 260 us -> 238 us (0.915)
  local copies, waits for them, and re-layouts: 25.1 us -> 4.14 us
  waiting for transfers between devices: 122 us -> 128 us
  starting transfers between devices: 43.4 us -> 39.8 us
    all_to_all x0 -> x4, waiting for transfers between devices: none -> 118 us  [exchange(): return lax.all_to_all(rows, PLANE, split_axis=0, concat_axis=0, tiled=True)]
    ppermute x28 -> x6, waiting for transfers between devices: 122 us -> 9.28 us  [send(): return lax.ppermute(value, AXES, pairs)]
    ppermute x28 -> x6, starting transfers between devices: 43.4 us -> 19.2 us  [send(): return lax.ppermute(value, AXES, pairs)]
    unnamed x70 -> x12, local copies, waits for them, and re-layouts: 23.5 us -> 1.7 us
    all_to_all x0 -> x4, starting transfers between devices: none -> 20.6 us  [exchange(): return lax.all_to_all(rows, PLANE, split_axis=0, concat_axis=0, tiled=True)]
    pallas_call x6, Pallas kernels: 59.3 us -> 54.9 us  [the longest x2 26 us: expert_rows(): pl.pallas_call(lambda *a: ffn_kernel(len(weights), *a), in_specs=[smem] +...]
    pallas_call x1, Pallas kernels: 2.68 us -> 5.38 us  [pack_weights(): pl.pallas_call(lambda *a: pack_kernel(pieces, *a), grid_spec=pltpu.Prefet...]
  transfers between devices with their start and end apart: 28 -> 10, of which waited for: 15 -> 5; matrix products, arithmetic and copies ran while one was open for 1% -> 1% of each run, Pallas kernels for 13% -> 14%
where the time goes in v2:
time: 238 us; the launch traced here: 237 us
  waiting for transfers between devices  128 us (54%)
  Pallas kernels  60.3 us (25%)
  starting transfers between devices  39.8 us (17%)
  blocking collectives  5.6 us (2%)
  local copies, waits for them, and re-layouts  4.14 us (2%)
    all_to_all x4, waiting for transfers between devices, exchange(): return lax.all_to_all(rows, PLANE, split_axis=0, concat_axis=0, tiled=True)  118 us
    pallas_call x2, Pallas kernels, expert_rows(): pl.pallas_call(lambda *a: ffn_kernel(len(weights), *a), in_specs=[smem] +...  26 us
    all_to_all x4, starting transfers between devices, exchange(): return lax.all_to_all(rows, PLANE, split_axis=0, concat_axis=0, tiled=True)  20.6 us
    ppermute x6, starting transfers between devices, send(): return lax.ppermute(value, AXES, pairs)  19.2 us
    pallas_call x2, Pallas kernels, gather_rows(): pl.pallas_call(lambda *a: gather_kernel(experts, cap, *a), grid_spec=pltp...  12.7 us
    ppermute x6, waiting for transfers between devices, send(): return lax.ppermute(value, AXES, pairs)  9.28 us
    pallas_call x1, Pallas kernels, combine_first(): pl.pallas_call(lambda *a: first_kernel(experts, cap, *a), grid_spec=pltpu...  8.68 us
    pallas_call x1, Pallas kernels, combine_second(): pl.pallas_call(second_kernel, grid=(row_width // chunk,), in_specs=[matri...  7.51 us
  transfers between devices with their start and end apart: 10, of which 5 were waited for; matrix products, arithmetic and copies ran while one was open for 1% of the time, Pallas kernels for 14%

profile of v2, /device:TPU:0, one launch (start us, length us, event | category | flops | bytes accessed | tf_op | source)
XLA Modules:
  0.0 237.4 jit_solution(14353691386608208172)
XLA Ops:
  0.0 0.0 copy-start.3
  0.0 5.4 %shard_map.91.a_2_ = bf16[16400,128]{1,0:T(8,128)(2,1)} custom-call(s32[1]{0:T(128)} %bitcast.8.a_0_, bf16[2,8192,128]{2,1,0:T(8,128)(2,1)} %bitcast.35, bf16[2,8192,128]{2,1,0:T(8,128)(2,1)} %bitcast.36, s32[2,2,32]{2,1,0:T(2,128)} %bitcast.42, s32[2,4,16]{2,1,0:T(4,128)} %bitcast.39), custom_call_target="tpu_custom_call" | custom-call | bytes 8400000 | tf_op jit(solution)/shard_map/pallas_call | solution.py:74
  5.4 2.7 %collective-permute-start.1 = (bf16[16400,128]{1,0:T(8,128)(2,1)}, bf16[16400,128]{1,0:T(8,128)(2,1)}, u32[]{:S(2)}, u32[]{:S(2)}) collective-permute-start(bf16[16400,128]{1,0:T(8,128)(2,1)} %shard_map.91.a_2_), channel_id=1, source_target_pairs={{6,4},{7,5},{10,8},{11,9},{12,10},{13,11},{22,20},{23,21},{26,24},... | collective-permute-start | bytes 12595208 | tf_op jit(solution)/shard_map/ppermute | solution.py:38
  8.0 6.9 %collective-permute-start = (bf16[16400,128]{1,0:T(8,128)(2,1)}, bf16[16400,128]{1,0:T(8,128)(2,1)}, u32[]{:S(2)}, u32[]{:S(2)}) collective-permute-start(bf16[16400,128]{1,0:T(8,128)(2,1)} %shard_map.91.a_2_), channel_id=1, source_target_pairs={{0,2},{1,3},{10,12},{11,13},{12,14},{13,15},{16,18},{17,19},{26,28... | collective-permute-start | bytes 12595208 | tf_op jit(solution)/shard_map/ppermute | solution.py:38
  14.9 0.6 stack.62.a_0_
  15.5 0.0 copy-done.3
  15.5 5.6 %all-gather.1.a_2_ = s32[4,2,512]{2,1,0:T(2,128)} all-gather(s32[1,2,512]{2,1,0:T(2,128)S(1)} %bitcast.41), channel_id=2, replica_groups=mesh['grp'=4,'z'=4,'x'=2] {'grp'}, dimensions={0}, use_global_device_ids=true | all-gather | bytes 20480 | tf_op jit(solution)/shard_map/all_gather | solution.py:386
  21.1 6.4 %shard_map.92 = bf16[8,384,512]{2,1,0:T(8,128)(2,1)} custom-call(s32[8]{0:T(128)} %stack.62.a_0_, bf16[2048,512]{1,0:T(8,128)(2,1)} %bitcast.43, s32[4,2,512]{2,1,0:T(2,128)} %all-gather.1.a_2_), custom_call_target="tpu_custom_call" | custom-call | flops 1610612736 | bytes 9000000 | tf_op jit(solution)/shard_map/pallas_call | solution.py:132
  27.5 3.7 %all-to-all-start = ((bf16[8,384,512]{2,1,0:T(8,128)(2,1)}), bf16[8,384,512]{2,1,0:T(8,128)(2,1)S(1)}, u32[]{:S(2)}, u32[]{:S(2)}) async-start(bf16[8,384,512]{2,1,0:T(8,128)(2,1)} %shard_map.92), calls=%async_computation | async-start | bytes 6291456 | tf_op jit(solution)/shard_map/all_to_all | solution.py:111
  31.2 0.7 stack.71.a_0_.a_1_
  31.9 6.3 %shard_map.93 = bf16[8,384,512]{2,1,0:T(8,128)(2,1)} custom-call(s32[8]{0:T(128)} %stack.71.a_0_.a_1_, bf16[2048,512]{1,0:T(8,128)(2,1)} %bitcast.44, s32[4,2,512]{2,1,0:T(2,128)} %all-gather.1.a_2_), custom_call_target="tpu_custom_call" | custom-call | flops 1610612736 | bytes 9000000 | tf_op jit(solution)/shard_map/pallas_call | solution.py:132
  38.2 0.0 copy-start.5
  38.2 29.9 %all-to-all-done.a_1_ = bf16[8,384,512]{2,1,0:T(8,128)(2,1)S(1)} async-done(((bf16[8,384,512]{2,1,0:T(8,128)(2,1)}), bf16[8,384,512]{2,1,0:T(8,128)(2,1)S(1)}, u32[]{:S(2)}, u32[]{:S(2)}) %all-to-all-start) | async-done | bytes 3145760 | tf_op jit(solution)/shard_map/all_to_all | solution.py:111
  68.1 0.0 copy-start.1
  68.1 0.0 collective-permute-done.1.a_4_.a_3_
  68.1 0.0 collective-permute-done.a_3_.a_2_
  68.1 2.9 %collective-permute-start.2 = (bf16[16400,128]{1,0:T(8,128)(2,1)}, bf16[16400,128]{1,0:T(8,128)(2,1)}, u32[]{:S(2)}, u32[]{:S(2)}) collective-permute-start(bf16[16400,128]{1,0:T(8,128)(2,1)} %collective-permute-done.a_3_.a_2_), channel_id=1, source_target_pairs={{2,4},{3,5},{12,14},{13,15},{18,20},{19,21},{28,30},{29,31}} | collective-permute-start | bytes 12595208 | tf_op jit(solution)/shard_map/ppermute | solution.py:38
  71.0 2.6 %collective-permute-start.3 = (bf16[16400,128]{1,0:T(8,128)(2,1)}, bf16[16400,128]{1,0:T(8,128)(2,1)}, u32[]{:S(2)}, u32[]{:S(2)}) collective-permute-start(bf16[16400,128]{1,0:T(8,128)(2,1)} %collective-permute-done.1.a_4_.a_3_), channel_id=1, source_target_pairs={{4,2},{5,3},{10,8},{11,9},{20,18},{21,19},{26,24},{27,25}} | collective-permute-start | bytes 12595208 | tf_op jit(solution)/shard_map/ppermute | solution.py:38
  73.6 0.0 copy-done.1
  73.6 3.6 %all-to-all-start.1 = ((bf16[8,384,512]{2,1,0:T(8,128)(2,1)}), bf16[8,384,512]{2,1,0:T(8,128)(2,1)S(1)}, u32[]{:S(2)}, u32[]{:S(2)}) async-start(bf16[8,384,512]{2,1,0:T(8,128)(2,1)} %shard_map.93), calls=%async_computation.1 | async-start | bytes 6291456 | tf_op jit(solution)/shard_map/all_to_all | solution.py:111
  77.3 0.0 copy-done.5
  77.3 0.6 dynamic_slice.7.a_0_
  77.9 13.0 %shard_map.94 = bf16[768,2048]{1,0:T(8,128)(2,1)} custom-call(s32[1]{0:T(128)} %dynamic_slice.7.a_0_, bf16[8,384,512]{2,1,0:T(8,128)(2,1)} %copy-done.1, bf16[16400,128]{1,0:T(8,128)(2,1)} %shard_map.91.a_2_, bf16[16400,128]{1,0:T(8,128)(2,1)} %collective-permute-done.a_3_.a_2_, bf16[16400,128]{1,0:T(8,128)(2,1)} %collective-permute-done.1.a_4_.a_3_), custom_call_target="tpu_custom_call" | custom-call | flops 6442450944 | bytes 12000000 | tf_op jit(solution)/shard_map/pallas_call | solution.py:254
  90.9 0.0 copy-start.4
  90.9 23.2 %all-to-all-done.1.a_1_ = bf16[8,384,512]{2,1,0:T(8,128)(2,1)S(1)} async-done(((bf16[8,384,512]{2,1,0:T(8,128)(2,1)}), bf16[8,384,512]{2,1,0:T(8,128)(2,1)S(1)}, u32[]{:S(2)}, u32[]{:S(2)}) %all-to-all-start.1) | async-done | bytes 3145760 | tf_op jit(solution)/shard_map/all_to_all | solution.py:111
  114.1 0.0 copy-start
  114.1 0.0 collective-permute-done.2.a_4_
  114.1 0.0 collective-permute-done.3.a_5_
  114.1 2.9 %collective-permute-start.4 = (bf16[16400,128]{1,0:T(8,128)(2,1)}, bf16[16400,128]{1,0:T(8,128)(2,1)}, u32[]{:S(2)}, u32[]{:S(2)}) collective-permute-start(bf16[16400,128]{1,0:T(8,128)(2,1)} %collective-permute-done.2.a_4_), channel_id=1, source_target_pairs={{4,6},{5,7},{20,22},{21,23}} | collective-permute-start | bytes 12595208 | tf_op jit(solution)/shard_map/ppermute | solution.py:38
  117.1 1.3 collective-permute-start.5
  118.3 9.6 %all-to-all-start.2 = ((bf16[8,96,2048]{2,1,0:T(8,128)(2,1)}), bf16[8,96,2048]{2,1,0:T(8,128)(2,1)}, u32[]{:S(2)}, u32[]{:S(2)}) async-start(bf16[8,96,2048]{2,1,0:T(8,128)(2,1)} %bitcast.37), calls=%async_computation.2 | async-start | bytes 6291456 | tf_op jit(solution)/shard_map/all_to_all | solution.py:111
  127.9 0.0 copy-done.4
  127.9 0.6 dynamic_slice.6.a_0_
  128.5 37.0 %all-to-all-done.2 = bf16[8,96,2048]{2,1,0:T(8,128)(2,1)} async-done(((bf16[8,96,2048]{2,1,0:T(8,128)(2,1)}), bf16[8,96,2048]{2,1,0:T(8,128)(2,1)}, u32[]{:S(2)}, u32[]{:S(2)}) %all-to-all-start.2) | async-done | bytes 3145760 | tf_op jit(solution)/shard_map/all_to_all | solution.py:111
  165.5 0.0 collective-permute-done.4.a_6_
  165.5 9.3 %collective-permute-done.5.a_7_ = bf16[16400,128]{1,0:T(8,128)(2,1)} collective-permute-done((bf16[16400,128]{1,0:T(8,128)(2,1)}, bf16[16400,128]{1,0:T(8,128)(2,1)}, u32[]{:S(2)}, u32[]{:S(2)}) %collective-permute-start.5) | collective-permute-done | bytes 4198432 | tf_op jit(solution)/shard_map/ppermute | solution.py:38
  174.8 0.0 copy-done
  174.8 13.0 %shard_map.95 = bf16[768,2048]{1,0:T(8,128)(2,1)} custom-call(s32[1]{0:T(128)} %dynamic_slice.6.a_0_, bf16[8,384,512]{2,1,0:T(8,128)(2,1)} %copy-done, bf16[16400,128]{1,0:T(8,128)(2,1)} %collective-permute-done.a_3_.a_2_, bf16[16400,128]{1,0:T(8,128)(2,1)} %collective-permute-done.1.a_4_.a_3_, bf16[16400,128]{1,0:T(8,128)(2,1)} %collective-permute-done.2.a_4_, ...), custom_call_target="tpu_custom_call" | custom-call | flops 6442450944 | bytes 12000000 | tf_op jit(solution)/shard_map/pallas_call | solution.py:254
  187.7 3.7 %all-to-all-start.3 = ((bf16[8,96,2048]{2,1,0:T(8,128)(2,1)}), bf16[8,96,2048]{2,1,0:T(8,128)(2,1)S(1)}, u32[]{:S(2)}, u32[]{:S(2)}) async-start(bf16[8,96,2048]{2,1,0:T(8,128)(2,1)} %bitcast.34), calls=%async_computation.3 | async-start | bytes 6291456 | tf_op jit(solution)/shard_map/all_to_all | solution.py:111
  191.4 8.7 %shard_map.96 = (f32[512,2048]{1,0:T(8,128)}, bf16[512,768]{1,0:T(8,128)(2,1)}, bf16[512,768]{1,0:T(8,128)(2,1)}) custom-call(s32[8]{0:T(128)} %stack.62.a_0_, s32[8]{0:T(128)} %stack.71.a_0_.a_1_, s32[2,512]{1,0:T(2,128)} %bitcast.40, f32[2,512]{1,0:T(2,128)} %bitcast.45, bf16[768,2048]{1,0:T(8,128)(2,1)} %bitcast.28.a_4_), custom_call_target="tpu_custom_call" | custom-call | flops 3221225472 | bytes 9000000 | tf_op jit(solution)/shard_map/pallas_call | solution.py:315
  200.1 28.2 %all-to-all-done.3 = bf16[8,96,2048]{2,1,0:T(8,128)(2,1)S(1)} async-done(((bf16[8,96,2048]{2,1,0:T(8,128)(2,1)}), bf16[8,96,2048]{2,1,0:T(8,128)(2,1)S(1)}, u32[]{:S(2)}, u32[]{:S(2)}) %all-to-all-start.3) | async-done | bytes 3145760 | tf_op jit(solution)/shard_map/all_to_all | solution.py:111
  228.3 0.0 copy-start.2
  228.3 1.7 copy-done.2
  229.9 7.5 %shard_map.97 = bf16[512,2048]{1,0:T(8,128)(2,1)} custom-call(bf16[512,768]{1,0:T(8,128)(2,1)} %get-tuple-element.36.high, bf16[512,768]{1,0:T(8,128)(2,1)} %get-tuple-element.37.low, bf16[768,2048]{1,0:T(8,128)(2,1)} %bitcast.38, f32[512,2048]{1,0:T(8,128)} %get-tuple-element.38.sum_ref), custom_call_target="tpu_custom_call" | custom-call | flops 3221225472 | bytes 9000000 | tf_op jit(solution)/shard_map/pallas_call | solution.py:349
Async XLA Ops:
  0.0 15.5 %copy-start.3 = (s32[1,512,2]{1,2,0:T(2,128)S(1)}, s32[1,512,2]{1,2,0:T(2,128)}, u32[]{:S(2)}) copy-start(s32[1,512,2]{1,2,0:T(2,128)} %param.10) | copy-start | bytes 12292
  5.4 62.8 %collective-permute-start.1 = (bf16[16400,128]{1,0:T(8,128)(2,1)}, bf16[16400,128]{1,0:T(8,128)(2,1)}, u32[]{:S(2)}, u32[]{:S(2)}) collective-permute-start(bf16[16400,128]{1,0:T(8,128)(2,1)} %shard_map.91.a_2_), channel_id=1, source_target_pairs={{6,4},{7,5},{10,8},{11,9},{12,10},{13,11},{22,20},{23,21},{26,24},... | collective-permute-start | bytes 12595208 | tf_op jit(solution)/shard_map/ppermute | solution.py:38
  8.0 60.1 %collective-permute-start = (bf16[16400,128]{1,0:T(8,128)(2,1)}, bf16[16400,128]{1,0:T(8,128)(2,1)}, u32[]{:S(2)}, u32[]{:S(2)}) collective-permute-start(bf16[16400,128]{1,0:T(8,128)(2,1)} %shard_map.91.a_2_), channel_id=1, source_target_pairs={{0,2},{1,3},{10,12},{11,13},{12,14},{13,15},{16,18},{17,19},{26,28... | collective-permute-start | bytes 12595208 | tf_op jit(solution)/shard_map/ppermute | solution.py:38
  27.5 40.6 %all-to-all-start = ((bf16[8,384,512]{2,1,0:T(8,128)(2,1)}), bf16[8,384,512]{2,1,0:T(8,128)(2,1)S(1)}, u32[]{:S(2)}, u32[]{:S(2)}) async-start(bf16[8,384,512]{2,1,0:T(8,128)(2,1)} %shard_map.92), calls=%async_computation | async-start | bytes 6291456 | tf_op jit(solution)/shard_map/all_to_all | solution.py:111
  38.2 39.1 %copy-start.5 = (s32[8]{0:T(128)S(1)}, s32[8]{0:T(128)}, u32[]{:S(2)}) copy-start(s32[8]{0:T(128)} %constant.45.clone) | copy-start | bytes 100
  68.1 5.5 %copy-start.1 = (bf16[8,384,512]{2,1,0:T(8,128)(2,1)}, bf16[8,384,512]{2,1,0:T(8,128)(2,1)S(1)}, u32[]{:S(2)}) copy-start(bf16[8,384,512]{2,1,0:T(8,128)(2,1)S(1)} %all-to-all-done.a_1_) | copy-start | bytes 9437188
  68.1 46.0 %collective-permute-start.2 = (bf16[16400,128]{1,0:T(8,128)(2,1)}, bf16[16400,128]{1,0:T(8,128)(2,1)}, u32[]{:S(2)}, u32[]{:S(2)}) collective-permute-start(bf16[16400,128]{1,0:T(8,128)(2,1)} %collective-permute-done.a_3_.a_2_), channel_id=1, source_target_pairs={{2,4},{3,5},{12,14},{13,15},{18,20},{19,21},{28,30},{29,31}} | collective-permute-start | bytes 12595208 | tf_op jit(solution)/shard_map/ppermute | solution.py:38
  71.0 43.1 %collective-permute-start.3 = (bf16[16400,128]{1,0:T(8,128)(2,1)}, bf16[16400,128]{1,0:T(8,128)(2,1)}, u32[]{:S(2)}, u32[]{:S(2)}) collective-permute-start(bf16[16400,128]{1,0:T(8,128)(2,1)} %collective-permute-done.1.a_4_.a_3_), channel_id=1, source_target_pairs={{4,2},{5,3},{10,8},{11,9},{20,18},{21,19},{26,24},{27,25}} | collective-permute-start | bytes 12595208 | tf_op jit(solution)/shard_map/ppermute | solution.py:38
  73.6 40.5 %all-to-all-start.1 = ((bf16[8,384,512]{2,1,0:T(8,128)(2,1)}), bf16[8,384,512]{2,1,0:T(8,128)(2,1)S(1)}, u32[]{:S(2)}, u32[]{:S(2)}) async-start(bf16[8,384,512]{2,1,0:T(8,128)(2,1)} %shard_map.93), calls=%async_computation.1 | async-start | bytes 6291456 | tf_op jit(solution)/shard_map/all_to_all | solution.py:111
  90.9 37.0 %copy-start.4 = (s32[8]{0:T(128)S(1)}, s32[8]{0:T(128)}, u32[]{:S(2)}) copy-start(s32[8]{0:T(128)} %constant.46.clone) | copy-start | bytes 100
  114.1 60.6 %copy-start = (bf16[8,384,512]{2,1,0:T(8,128)(2,1)}, bf16[8,384,512]{2,1,0:T(8,128)(2,1)S(1)}, u32[]{:S(2)}) copy-start(bf16[8,384,512]{2,1,0:T(8,128)(2,1)S(1)} %all-to-all-done.1.a_1_) | copy-start | bytes 9437188
  114.1 51.3 %collective-permute-start.4 = (bf16[16400,128]{1,0:T(8,128)(2,1)}, bf16[16400,128]{1,0:T(8,128)(2,1)}, u32[]{:S(2)}, u32[]{:S(2)}) collective-permute-start(bf16[16400,128]{1,0:T(8,128)(2,1)} %collective-permute-done.2.a_4_), channel_id=1, source_target_pairs={{4,6},{5,7},{20,22},{21,23}} | collective-permute-start | bytes 12595208 | tf_op jit(solution)/shard_map/ppermute | solution.py:38
  117.1 57.7 %collective-permute-start.5 = (bf16[16400,128]{1,0:T(8,128)(2,1)}, bf16[16400,128]{1,0:T(8,128)(2,1)}, u32[]{:S(2)}, u32[]{:S(2)}) collective-permute-start(bf16[16400,128]{1,0:T(8,128)(2,1)} %collective-permute-done.3.a_5_), channel_id=1, source_target_pairs={{2,0},{3,1},{18,16},{19,17}} | collective-permute-start | bytes 12595208 | tf_op jit(solution)/shard_map/ppermute | solution.py:38
  118.3 47.1 %all-to-all-start.2 = ((bf16[8,96,2048]{2,1,0:T(8,128)(2,1)}), bf16[8,96,2048]{2,1,0:T(8,128)(2,1)}, u32[]{:S(2)}, u32[]{:S(2)}) async-start(bf16[8,96,2048]{2,1,0:T(8,128)(2,1)} %bitcast.37), calls=%async_computation.2 | async-start | bytes 6291456 | tf_op jit(solution)/shard_map/all_to_all | solution.py:111
  187.7 40.5 %all-to-all-start.3 = ((bf16[8,96,2048]{2,1,0:T(8,128)(2,1)}), bf16[8,96,2048]{2,1,0:T(8,128)(2,1)S(1)}, u32[]{:S(2)}, u32[]{:S(2)}) async-start(bf16[8,96,2048]{2,1,0:T(8,128)(2,1)} %bitcast.34), calls=%async_computation.3 | async-start | bytes 6291456 | tf_op jit(solution)/shard_map/all_to_all | solution.py:111
  228.3 1.7 copy-start.2

commit v3 on v2

--- a/solution.py
+++ b/solution.py
@@ -391,9 +391,10 @@
     rows_a = gather_rows(features, choices, order_a, experts, cap)
     got_a = exchange(rows_a)
     rows_b = gather_rows(features, after(choices, rows_a), order_b, experts, cap)
-    r1, l1, got_a, rows_b = lax.optimization_barrier((r1, l1, got_a, rows_b))
+    r1, l1, rows_b = lax.optimization_barrier((r1, l1, rows_b))
     r2 = send(r1, along_z(1, ((1, 0), (2, 1))))
     l2 = send(l1, along_z(-1, ((2, 0), (1, 1))))
+    got_a, rows_b = lax.optimization_barrier((got_a, rows_b))
     got_b = exchange(rows_b)
 
     pick = z * 2 + core

time: 238 us -> 230 us (0.966)
  waiting for transfers between devices: 128 us -> 122 us
  starting transfers between devices: 39.8 us -> 35.3 us
    all_to_all x4, waiting for transfers between devices: 118 us -> 92.1 us  [exchange(): return lax.all_to_all(rows, PLANE, split_axis=0, concat_axis=0, tiled=True)]
    ppermute x6, waiting for transfers between devices: 9.28 us -> 30.3 us  [send(): return lax.ppermute(value, AXES, pairs)]
    all_to_all x4, starting transfers between devices: 20.6 us -> 16.4 us  [exchange(): return lax.all_to_all(rows, PLANE, split_axis=0, concat_axis=0, tiled=True)]
  transfers between devices with their start and end apart: 10 -> 10, of which waited for: 5 -> 6; matrix products, arithmetic and copies ran while one was open for 1% -> 1% of each run, Pallas kernels for 14% -> 15%
where the time goes in v3:
time: 230 us; the launch traced here: 229 us
  waiting for transfers between devices  122 us (53%)
  Pallas kernels  60.2 us (26%)
  starting transfers between devices  35.3 us (15%)
  local copies, waits for them, and re-layouts  5.81 us (3%)
  blocking collectives  5.6 us (2%)
    all_to_all x4, waiting for transfers between devices, exchange(): return lax.all_to_all(rows, PLANE, split_axis=0, concat_axis=0, tiled=True)  92.1 us
    ppermute x6, waiting for transfers between devices, send(): return lax.ppermute(value, AXES, pairs)  30.3 us
    pallas_call x2, Pallas kernels, expert_rows(): pl.pallas_call(lambda *a: ffn_kernel(len(weights), *a), in_specs=[smem] +...  26 us
    ppermute x6, starting transfers between devices, send(): return lax.ppermute(value, AXES, pairs)  18.9 us
    all_to_all x4, starting transfers between devices, exchange(): return lax.all_to_all(rows, PLANE, split_axis=0, concat_axis=0, tiled=True)  16.4 us
    pallas_call x2, Pallas kernels, gather_rows(): pl.pallas_call(lambda *a: gather_kernel(experts, cap, *a), grid_spec=pltp...  12.7 us
    pallas_call x1, Pallas kernels, combine_first(): pl.pallas_call(lambda *a: first_kernel(experts, cap, *a), grid_spec=pltpu...  8.67 us
    pallas_call x1, Pallas kernels, combine_second(): pl.pallas_call(second_kernel, grid=(row_width // chunk,), in_specs=[matri...  7.51 us
  transfers between devices with their start and end apart: 10, of which 6 were waited for; matrix products, arithmetic and copies ran while one was open for 1% of the time, Pallas kernels for 15%

profile of v3, /device:TPU:0, one launch (start us, length us, event | category | flops | bytes accessed | tf_op | source)
XLA Modules:
  0.0 229.4 jit_solution(7326020139872094029)
XLA Ops:
  0.0 0.0 copy-start.3
  0.0 5.4 %shard_map.91.a_2_ = bf16[16400,128]{1,0:T(8,128)(2,1)} custom-call(s32[1]{0:T(128)} %bitcast.11.a_0_, bf16[2,8192,128]{2,1,0:T(8,128)(2,1)} %bitcast.35, bf16[2,8192,128]{2,1,0:T(8,128)(2,1)} %bitcast.36, s32[2,2,32]{2,1,0:T(2,128)} %bitcast.42, s32[2,4,16]{2,1,0:T(4,128)} %bitcast.39), custom_call_target="tpu_custom_call" | custom-call | bytes 8400000 | tf_op jit(solution)/shard_map/pallas_call | solution.py:74
  5.4 2.7 %collective-permute-start.1 = (bf16[16400,128]{1,0:T(8,128)(2,1)}, bf16[16400,128]{1,0:T(8,128)(2,1)}, u32[]{:S(2)}, u32[]{:S(2)}) collective-permute-start(bf16[16400,128]{1,0:T(8,128)(2,1)} %shard_map.91.a_2_), channel_id=1, source_target_pairs={{6,4},{7,5},{10,8},{11,9},{12,10},{13,11},{22,20},{23,21},{26,24},... | collective-permute-start | bytes 12595208 | tf_op jit(solution)/shard_map/ppermute | solution.py:38
  8.0 6.9 %collective-permute-start = (bf16[16400,128]{1,0:T(8,128)(2,1)}, bf16[16400,128]{1,0:T(8,128)(2,1)}, u32[]{:S(2)}, u32[]{:S(2)}) collective-permute-start(bf16[16400,128]{1,0:T(8,128)(2,1)} %shard_map.91.a_2_), channel_id=1, source_target_pairs={{0,2},{1,3},{10,12},{11,13},{12,14},{13,15},{16,18},{17,19},{26,28... | collective-permute-start | bytes 12595208 | tf_op jit(solution)/shard_map/ppermute | solution.py:38
  14.9 0.6 stack.62.a_0_
  15.5 0.0 copy-done.3
  15.5 5.6 %all-gather.1.a_2_ = s32[4,2,512]{2,1,0:T(2,128)} all-gather(s32[1,2,512]{2,1,0:T(2,128)S(1)} %bitcast.41), channel_id=2, replica_groups=mesh['grp'=4,'z'=4,'x'=2] {'grp'}, dimensions={0}, use_global_device_ids=true | all-gather | bytes 20480 | tf_op jit(solution)/shard_map/all_gather | solution.py:386
  21.1 6.3 %shard_map.92 = bf16[8,384,512]{2,1,0:T(8,128)(2,1)} custom-call(s32[8]{0:T(128)} %stack.62.a_0_, bf16[2048,512]{1,0:T(8,128)(2,1)} %bitcast.43, s32[4,2,512]{2,1,0:T(2,128)} %all-gather.1.a_2_), custom_call_target="tpu_custom_call" | custom-call | flops 1610612736 | bytes 9000000 | tf_op jit(solution)/shard_map/pallas_call | solution.py:132
  27.5 3.7 %all-to-all-start = ((bf16[8,384,512]{2,1,0:T(8,128)(2,1)}), bf16[8,384,512]{2,1,0:T(8,128)(2,1)S(1)}, u32[]{:S(2)}, u32[]{:S(2)}) async-start(bf16[8,384,512]{2,1,0:T(8,128)(2,1)} %shard_map.92), calls=%async_computation | async-start | bytes 6291456 | tf_op jit(solution)/shard_map/all_to_all | solution.py:111
  31.2 0.7 stack.71.a_0_.a_1_
  31.9 6.3 %shard_map.93 = bf16[8,384,512]{2,1,0:T(8,128)(2,1)} custom-call(s32[8]{0:T(128)} %stack.71.a_0_.a_1_, bf16[2048,512]{1,0:T(8,128)(2,1)} %bitcast.44, s32[4,2,512]{2,1,0:T(2,128)} %all-gather.1.a_2_), custom_call_target="tpu_custom_call" | custom-call | flops 1610612736 | bytes 9000000 | tf_op jit(solution)/shard_map/pallas_call | solution.py:132
  38.2 0.0 copy-start.5
  38.2 0.0 collective-permute-done.1.a_4_.a_3_
  38.2 21.1 %collective-permute-done.a_3_.a_2_ = bf16[16400,128]{1,0:T(8,128)(2,1)} collective-permute-done((bf16[16400,128]{1,0:T(8,128)(2,1)}, bf16[16400,128]{1,0:T(8,128)(2,1)}, u32[]{:S(2)}, u32[]{:S(2)}) %collective-permute-start) | collective-permute-done | bytes 4198432 | tf_op jit(solution)/shard_map/ppermute | solution.py:38
  59.3 2.6 %collective-permute-start.2 = (bf16[16400,128]{1,0:T(8,128)(2,1)}, bf16[16400,128]{1,0:T(8,128)(2,1)}, u32[]{:S(2)}, u32[]{:S(2)}) collective-permute-start(bf16[16400,128]{1,0:T(8,128)(2,1)} %collective-permute-done.a_3_.a_2_), channel_id=1, source_target_pairs={{2,4},{3,5},{12,14},{13,15},{18,20},{19,21},{28,30},{29,31}} | collective-permute-start | bytes 12595208 | tf_op jit(solution)/shard_map/ppermute | solution.py:38
  61.9 2.6 %collective-permute-start.3 = (bf16[16400,128]{1,0:T(8,128)(2,1)}, bf16[16400,128]{1,0:T(8,128)(2,1)}, u32[]{:S(2)}, u32[]{:S(2)}) collective-permute-start(bf16[16400,128]{1,0:T(8,128)(2,1)} %collective-permute-done.1.a_4_.a_3_), channel_id=1, source_target_pairs={{4,2},{5,3},{10,8},{11,9},{20,18},{21,19},{26,24},{27,25}} | collective-permute-start | bytes 12595208 | tf_op jit(solution)/shard_map/ppermute | solution.py:38
  64.5 3.6 %all-to-all-done.a_1_ = bf16[8,384,512]{2,1,0:T(8,128)(2,1)S(1)} async-done(((bf16[8,384,512]{2,1,0:T(8,128)(2,1)}), bf16[8,384,512]{2,1,0:T(8,128)(2,1)S(1)}, u32[]{:S(2)}, u32[]{:S(2)}) %all-to-all-start) | async-done | bytes 3145760 | tf_op jit(solution)/shard_map/all_to_all | solution.py:111
  68.1 0.0 copy-start.1
  68.1 1.7 copy-done.1
  69.8 3.6 %all-to-all-start.1 = ((bf16[8,384,512]{2,1,0:T(8,128)(2,1)}), bf16[8,384,512]{2,1,0:T(8,128)(2,1)S(1)}, u32[]{:S(2)}, u32[]{:S(2)}) async-start(bf16[8,384,512]{2,1,0:T(8,128)(2,1)} %shard_map.93), calls=%async_computation.1 | async-start | bytes 6291456 | tf_op jit(solution)/shard_map/all_to_all | solution.py:111
  73.5 0.0 copy-done.5
  73.5 0.6 dynamic_slice.7.a_0_
  74.1 13.0 %shard_map.94 = bf16[768,2048]{1,0:T(8,128)(2,1)} custom-call(s32[1]{0:T(128)} %dynamic_slice.7.a_0_, bf16[8,384,512]{2,1,0:T(8,128)(2,1)} %copy-done.1, bf16[16400,128]{1,0:T(8,128)(2,1)} %shard_map.91.a_2_, bf16[16400,128]{1,0:T(8,128)(2,1)} %collective-permute-done.a_3_.a_2_, bf16[16400,128]{1,0:T(8,128)(2,1)} %collective-permute-done.1.a_4_.a_3_), custom_call_target="tpu_custom_call" | custom-call | flops 6442450944 | bytes 12000000 | tf_op jit(solution)/shard_map/pallas_call | solution.py:254
  87.0 0.0 copy-start.4
  87.1 23.2 %all-to-all-done.1.a_1_ = bf16[8,384,512]{2,1,0:T(8,128)(2,1)S(1)} async-done(((bf16[8,384,512]{2,1,0:T(8,128)(2,1)}), bf16[8,384,512]{2,1,0:T(8,128)(2,1)S(1)}, u32[]{:S(2)}, u32[]{:S(2)}) %all-to-all-start.1) | async-done | bytes 3145760 | tf_op jit(solution)/shard_map/all_to_all | solution.py:111
  110.3 0.0 copy-start
  110.3 0.0 collective-permute-done.2.a_4_
  110.3 0.0 collective-permute-done.3.a_5_
  110.3 2.9 %collective-permute-start.4 = (bf16[16400,128]{1,0:T(8,128)(2,1)}, bf16[16400,128]{1,0:T(8,128)(2,1)}, u32[]{:S(2)}, u32[]{:S(2)}) collective-permute-start(bf16[16400,128]{1,0:T(8,128)(2,1)} %collective-permute-done.2.a_4_), channel_id=1, source_target_pairs={{4,6},{5,7},{20,22},{21,23}} | collective-permute-start | bytes 12595208 | tf_op jit(solution)/shard_map/ppermute | solution.py:38
  113.2 1.3 collective-permute-start.5
  114.5 5.3 %all-to-all-start.2 = ((bf16[8,96,2048]{2,1,0:T(8,128)(2,1)}), bf16[8,96,2048]{2,1,0:T(8,128)(2,1)}, u32[]{:S(2)}, u32[]{:S(2)}) async-start(bf16[8,96,2048]{2,1,0:T(8,128)(2,1)} %bitcast.37), calls=%async_computation.2 | async-start | bytes 6291456 | tf_op jit(solution)/shard_map/all_to_all | solution.py:111
  119.8 0.0 copy-done.4
  119.8 0.6 dynamic_slice.6.a_0_
  120.4 37.0 %all-to-all-done.2 = bf16[8,96,2048]{2,1,0:T(8,128)(2,1)} async-done(((bf16[8,96,2048]{2,1,0:T(8,128)(2,1)}), bf16[8,96,2048]{2,1,0:T(8,128)(2,1)}, u32[]{:S(2)}, u32[]{:S(2)}) %all-to-all-start.2) | async-done | bytes 3145760 | tf_op jit(solution)/shard_map/all_to_all | solution.py:111
  157.4 0.0 collective-permute-done.4.a_6_
  157.4 9.2 %collective-permute-done.5.a_7_ = bf16[16400,128]{1,0:T(8,128)(2,1)} collective-permute-done((bf16[16400,128]{1,0:T(8,128)(2,1)}, bf16[16400,128]{1,0:T(8,128)(2,1)}, u32[]{:S(2)}, u32[]{:S(2)}) %collective-permute-start.5) | collective-permute-done | bytes 4198432 | tf_op jit(solution)/shard_map/ppermute | solution.py:38
  166.5 0.0 copy-done
  166.6 13.0 %shard_map.95 = bf16[768,2048]{1,0:T(8,128)(2,1)} custom-call(s32[1]{0:T(128)} %dynamic_slice.6.a_0_, bf16[8,384,512]{2,1,0:T(8,128)(2,1)} %copy-done, bf16[16400,128]{1,0:T(8,128)(2,1)} %collective-permute-done.a_3_.a_2_, bf16[16400,128]{1,0:T(8,128)(2,1)} %collective-permute-done.1.a_4_.a_3_, bf16[16400,128]{1,0:T(8,128)(2,1)} %collective-permute-done.2.a_4_, ...), custom_call_target="tpu_custom_call" | custom-call | flops 6442450944 | bytes 12000000 | tf_op jit(solution)/shard_map/pallas_call | solution.py:254
  179.5 3.7 %all-to-all-start.3 = ((bf16[8,96,2048]{2,1,0:T(8,128)(2,1)}), bf16[8,96,2048]{2,1,0:T(8,128)(2,1)S(1)}, u32[]{:S(2)}, u32[]{:S(2)}) async-start(bf16[8,96,2048]{2,1,0:T(8,128)(2,1)} %bitcast.34), calls=%async_computation.3 | async-start | bytes 6291456 | tf_op jit(solution)/shard_map/all_to_all | solution.py:111
  183.3 8.7 %shard_map.96 = (f32[512,2048]{1,0:T(8,128)}, bf16[512,768]{1,0:T(8,128)(2,1)}, bf16[512,768]{1,0:T(8,128)(2,1)}) custom-call(s32[8]{0:T(128)} %stack.62.a_0_, s32[8]{0:T(128)} %stack.71.a_0_.a_1_, s32[2,512]{1,0:T(2,128)} %bitcast.40, f32[2,512]{1,0:T(2,128)} %bitcast.45, bf16[768,2048]{1,0:T(8,128)(2,1)} %bitcast.28.a_4_), custom_call_target="tpu_custom_call" | custom-call | flops 3221225472 | bytes 9000000 | tf_op jit(solution)/shard_map/pallas_call | solution.py:315
  191.9 28.3 %all-to-all-done.3 = bf16[8,96,2048]{2,1,0:T(8,128)(2,1)S(1)} async-done(((bf16[8,96,2048]{2,1,0:T(8,128)(2,1)}), bf16[8,96,2048]{2,1,0:T(8,128)(2,1)S(1)}, u32[]{:S(2)}, u32[]{:S(2)}) %all-to-all-start.3) | async-done | bytes 3145760 | tf_op jit(solution)/shard_map/all_to_all | solution.py:111
  220.2 0.0 copy-start.2
  220.2 1.7 copy-done.2
  221.9 7.5 %shard_map.97 = bf16[512,2048]{1,0:T(8,128)(2,1)} custom-call(bf16[512,768]{1,0:T(8,128)(2,1)} %get-tuple-element.38.high, bf16[512,768]{1,0:T(8,128)(2,1)} %get-tuple-element.39.low, bf16[768,2048]{1,0:T(8,128)(2,1)} %bitcast.38, f32[512,2048]{1,0:T(8,128)} %get-tuple-element.40.sum_ref), custom_call_target="tpu_custom_call" | custom-call | flops 3221225472 | bytes 9000000 | tf_op jit(solution)/shard_map/pallas_call | solution.py:349
Async XLA Ops:
  0.0 15.5 %copy-start.3 = (s32[1,512,2]{1,2,0:T(2,128)S(1)}, s32[1,512,2]{1,2,0:T(2,128)}, u32[]{:S(2)}) copy-start(s32[1,512,2]{1,2,0:T(2,128)} %param.10) | copy-start | bytes 12292
  5.4 32.8 %collective-permute-start.1 = (bf16[16400,128]{1,0:T(8,128)(2,1)}, bf16[16400,128]{1,0:T(8,128)(2,1)}, u32[]{:S(2)}, u32[]{:S(2)}) collective-permute-start(bf16[16400,128]{1,0:T(8,128)(2,1)} %shard_map.91.a_2_), channel_id=1, source_target_pairs={{6,4},{7,5},{10,8},{11,9},{12,10},{13,11},{22,20},{23,21},{26,24},... | collective-permute-start | bytes 12595208 | tf_op jit(solution)/shard_map/ppermute | solution.py:38
  8.0 51.3 %collective-permute-start = (bf16[16400,128]{1,0:T(8,128)(2,1)}, bf16[16400,128]{1,0:T(8,128)(2,1)}, u32[]{:S(2)}, u32[]{:S(2)}) collective-permute-start(bf16[16400,128]{1,0:T(8,128)(2,1)} %shard_map.91.a_2_), channel_id=1, source_target_pairs={{0,2},{1,3},{10,12},{11,13},{12,14},{13,15},{16,18},{17,19},{26,28... | collective-permute-start | bytes 12595208 | tf_op jit(solution)/shard_map/ppermute | solution.py:38
  27.5 40.7 %all-to-all-start = ((bf16[8,384,512]{2,1,0:T(8,128)(2,1)}), bf16[8,384,512]{2,1,0:T(8,128)(2,1)S(1)}, u32[]{:S(2)}, u32[]{:S(2)}) async-start(bf16[8,384,512]{2,1,0:T(8,128)(2,1)} %shard_map.92), calls=%async_computation | async-start | bytes 6291456 | tf_op jit(solution)/shard_map/all_to_all | solution.py:111
  38.2 35.3 %copy-start.5 = (s32[8]{0:T(128)S(1)}, s32[8]{0:T(128)}, u32[]{:S(2)}) copy-start(s32[8]{0:T(128)} %constant.45.clone) | copy-start | bytes 100
  59.3 51.0 %collective-permute-start.2 = (bf16[16400,128]{1,0:T(8,128)(2,1)}, bf16[16400,128]{1,0:T(8,128)(2,1)}, u32[]{:S(2)}, u32[]{:S(2)}) collective-permute-start(bf16[16400,128]{1,0:T(8,128)(2,1)} %collective-permute-done.a_3_.a_2_), channel_id=1, source_target_pairs={{2,4},{3,5},{12,14},{13,15},{18,20},{19,21},{28,30},{29,31}} | collective-permute-start | bytes 12595208 | tf_op jit(solution)/shard_map/ppermute | solution.py:38
  61.9 48.4 %collective-permute-start.3 = (bf16[16400,128]{1,0:T(8,128)(2,1)}, bf16[16400,128]{1,0:T(8,128)(2,1)}, u32[]{:S(2)}, u32[]{:S(2)}) collective-permute-start(bf16[16400,128]{1,0:T(8,128)(2,1)} %collective-permute-done.1.a_4_.a_3_), channel_id=1, source_target_pairs={{4,2},{5,3},{10,8},{11,9},{20,18},{21,19},{26,24},{27,25}} | collective-permute-start | bytes 12595208 | tf_op jit(solution)/shard_map/ppermute | solution.py:38
  68.1 1.7 copy-start.1
  69.8 40.5 %all-to-all-start.1 = ((bf16[8,384,512]{2,1,0:T(8,128)(2,1)}), bf16[8,384,512]{2,1,0:T(8,128)(2,1)S(1)}, u32[]{:S(2)}, u32[]{:S(2)}) async-start(bf16[8,384,512]{2,1,0:T(8,128)(2,1)} %shard_map.93), calls=%async_computation.1 | async-start | bytes 6291456 | tf_op jit(solution)/shard_map/all_to_all | solution.py:111
  87.0 32.7 %copy-start.4 = (s32[8]{0:T(128)S(1)}, s32[8]{0:T(128)}, u32[]{:S(2)}) copy-start(s32[8]{0:T(128)} %constant.46.clone) | copy-start | bytes 100
  110.3 56.3 %copy-start = (bf16[8,384,512]{2,1,0:T(8,128)(2,1)}, bf16[8,384,512]{2,1,0:T(8,128)(2,1)S(1)}, u32[]{:S(2)}) copy-start(bf16[8,384,512]{2,1,0:T(8,128)(2,1)S(1)} %all-to-all-done.1.a_1_) | copy-start | bytes 9437188
  110.3 47.1 %collective-permute-start.4 = (bf16[16400,128]{1,0:T(8,128)(2,1)}, bf16[16400,128]{1,0:T(8,128)(2,1)}, u32[]{:S(2)}, u32[]{:S(2)}) collective-permute-start(bf16[16400,128]{1,0:T(8,128)(2,1)} %collective-permute-done.2.a_4_), channel_id=1, source_target_pairs={{4,6},{5,7},{20,22},{21,23}} | collective-permute-start | bytes 12595208 | tf_op jit(solution)/shard_map/ppermute | solution.py:38
  113.2 53.3 %collective-permute-start.5 = (bf16[16400,128]{1,0:T(8,128)(2,1)}, bf16[16400,128]{1,0:T(8,128)(2,1)}, u32[]{:S(2)}, u32[]{:S(2)}) collective-permute-start(bf16[16400,128]{1,0:T(8,128)(2,1)} %collective-permute-done.3.a_5_), channel_id=1, source_target_pairs={{2,0},{3,1},{18,16},{19,17}} | collective-permute-start | bytes 12595208 | tf_op jit(solution)/shard_map/ppermute | solution.py:38
  114.5 42.9 %all-to-all-start.2 = ((bf16[8,96,2048]{2,1,0:T(8,128)(2,1)}), bf16[8,96,2048]{2,1,0:T(8,128)(2,1)}, u32[]{:S(2)}, u32[]{:S(2)}) async-start(bf16[8,96,2048]{2,1,0:T(8,128)(2,1)} %bitcast.37), calls=%async_computation.2 | async-start | bytes 6291456 | tf_op jit(solution)/shard_map/all_to_all | solution.py:111
  179.5 40.7 %all-to-all-start.3 = ((bf16[8,96,2048]{2,1,0:T(8,128)(2,1)}), bf16[8,96,2048]{2,1,0:T(8,128)(2,1)S(1)}, u32[]{:S(2)}, u32[]{:S(2)}) async-start(bf16[8,96,2048]{2,1,0:T(8,128)(2,1)} %bitcast.34), calls=%async_computation.3 | async-start | bytes 6291456 | tf_op jit(solution)/shard_map/all_to_all | solution.py:111
  220.2 1.7 copy-start.2

commit v4 on v3

--- a/solution.py
+++ b/solution.py
@@ -158,9 +158,16 @@
     return half + half * jnp.tanh(inner)
 
 
-def ffn_kernel(n_weights, chosen, got_ref, *refs):
+def ffn_kernel(n_weights, cap, meta, *refs):
+    @pl.when(meta[1] == 1)
+    def _():
+        run_expert(n_weights, cap, meta[0], *refs)
+
+
+def run_expert(n_weights, cap, chosen, got_ref, *refs):
     sources, refs = refs[:n_weights], refs[n_weights:]
-    out_ref, xs, wts, hid, res, packed, wide, table, x_sem, w_sem, o_sem = refs
+    outs, refs = refs[:-10], refs[-10:]
+    xs, wts, hid, res, packed, wide, table, x_sem, w_sem, o_sem = refs
     part_rows, width = got_ref.shape[1], got_ref.shape[2]
     blk = wts.shape[1]
     up_cols = hid.shape[1] // blk
@@ -180,7 +187,7 @@
 
     for i in range(n_weights):
 
-        @pl.when(chosen[0] == i)
+        @pl.when(chosen == i)
         def _(i=i):
             for one in weight_copies(sources[i]):
                 one.start()
@@ -236,15 +243,22 @@
         if (col + 1) % (down_cols // 2) == 0:
             half = (col + 1) // (down_cols // 2) - 1
             cols = pl.ds(half * (down_cols // 2) * blk, (down_cols // 2) * blk)
-            out_copies.append(
-                pltpu.make_async_copy(res.at[:, cols], out_ref.at[:, cols], o_sem.at[half])
-            )
-            out_copies[-1].start()
+            share = cap // len(outs)
+            for n in range(8 * len(outs)):
+                owner, part = n // len(outs), n % len(outs)
+                out_copies.append(
+                    pltpu.make_async_copy(
+                        res.at[pl.ds(owner * cap + part * share, share), cols],
+                        outs[part].at[pl.ds(owner * share, share), cols],
+                        o_sem.at[half * 8 * len(outs) + n],
+                    )
+                )
+                out_copies[-1].start()
     for one in out_copies:
         one.wait()
 
 
-def expert_rows(chosen, got, weights, hidden):
+def expert_rows(chosen, active, got, weights, hidden, cap, shares):
     _, part_rows, width = got.shape
     blk = weights[0].shape[1]
     rows, row_width = 2 * part_rows, 4 * width
@@ -252,10 +266,10 @@
     smem = pl.BlockSpec(memory_space=pltpu.SMEM)
     up_and_down = weights[0].shape[0] - TABLE_ROWS
     return pl.pallas_call(
-        lambda *a: ffn_kernel(len(weights), *a),
+        lambda *a: ffn_kernel(len(weights), cap, *a),
         in_specs=[smem] + [hbm] * (1 + len(weights)),
-        out_specs=hbm,
-        out_shape=jax.ShapeDtypeStruct((rows, row_width), jnp.bfloat16),
+        out_specs=[hbm] * shares,
+        out_shape=[jax.ShapeDtypeStruct((rows // shares, row_width), jnp.bfloat16)] * shares,
         scratch_shapes=[
             pltpu.VMEM((rows, row_width), jnp.bfloat16),
             pltpu.VMEM((up_and_down, blk), jnp.bfloat16),
@@ -266,7 +280,7 @@
             pltpu.SMEM((TABLE_ROWS, blk), jnp.int32),
             pltpu.SemaphoreType.DMA((8,)),
             pltpu.SemaphoreType.DMA((2 + PIECES,)),
-            pltpu.SemaphoreType.DMA((2,)),
+            pltpu.SemaphoreType.DMA((32,)),
         ],
         cost_estimate=pl.CostEstimate(
             flops=4 * rows * up_and_down * blk,
@@ -274,14 +288,14 @@
             transcendentals=rows * hidden,
         ),
         compiler_params=pltpu.CompilerParams(vmem_limit_bytes=60 * 2**20),
-    )(chosen[None].astype(jnp.int32), got, *weights)
-
-
-def gate_matrix(order, slots, choice_ref, gate_ref, cap, high, low):
+    )(jnp.stack([chosen, active]).astype(jnp.int32), got, *weights)
+
+
+def gate_matrix(order, blocks, slots, choice_ref, gate_ref, high, low):
     tokens = choice_ref.shape[1]
-    row = lax.broadcasted_iota(jnp.int32, (cap, tokens), 0)
     tops, rests = [], []
-    for n in range(8):
+    for n, size, first in blocks:
+        row = lax.broadcasted_iota(jnp.int32, (size, tokens), 0) + first
         line = slots[pl.ds(order[n], 1), :]
         gate = jnp.where(choice_ref[0:1, :] == order[n], gate_ref[0:1, :], gate_ref[1:2, :])
         top = gate.astype(jnp.bfloat16).astype(jnp.float32)
@@ -292,46 +306,62 @@
     low[...] = jnp.concatenate(rests, axis=0).T
 
 
-def first_kernel(experts, cap, order_a, order_b, choice_ref, gate_ref, rows, sum_ref, *refs):
-    high_b, low_b, slots, high, low = refs
+def first_kernel(experts, cap, order, choice_ref, gate_ref, rows_a, rows_1, sum_ref, *refs):
+    high_b, low_b, slots, high, low, stack = refs
+    part = cap // 2
+
+    def of_core(on):
+        return [(8 + 8 * (1 - on) + s, part, part * ((s % 2) ^ on)) for s in range(8)]
 
     @pl.when(pl.program_id(0) == 0)
     def _():
         slots[...] = slot_rows(choice_ref[0:1, :], choice_ref[1:2, :], experts)
-        gate_matrix(order_a, slots, choice_ref, gate_ref, cap, high, low)
-        gate_matrix(order_b, slots, choice_ref, gate_ref, cap, high_b, low_b)
-
-    total = jnp.dot(high[...], rows[...], preferred_element_type=jnp.float32)
-    total += jnp.dot(low[...], rows[...], preferred_element_type=jnp.float32)
+        blocks = [(n, cap, 0) for n in range(8)] + of_core(1)
+        gate_matrix(order, blocks, slots, choice_ref, gate_ref, high, low)
+        gate_matrix(order, of_core(0), slots, choice_ref, gate_ref, high_b, low_b)
+
+    stack[0 : 8 * cap, :] = rows_a[...]
+    stack[8 * cap :, :] = rows_1[...]
+    total = jnp.dot(high[...], stack[...], preferred_element_type=jnp.float32)
+    total += jnp.dot(low[...], stack[...], preferred_element_type=jnp.float32)
     sum_ref[...] = total
 
 
-def combine_first(order_a, order_b, choice, gates, rows, experts, cap):
+def combine_first(order, choice, gates, rows_a, rows_1, experts, cap):
     tokens = choice.shape[1]
-    columns, row_width = rows.shape
+    row_width = rows_a.shape[1]
+    count_a, count_1 = rows_a.shape[0], rows_1.shape[0]
     chunk = 512
-    whole = pl.BlockSpec((2, tokens), lambda j, a, c: (0, 0))
-    matrix = pl.BlockSpec((tokens, columns), lambda j, a, c: (0, 0))
+    whole = pl.BlockSpec((2, tokens), lambda j, a: (0, 0))
+    matrix = pl.BlockSpec((tokens, count_1), lambda j, a: (0, 0))
     return pl.pallas_call(
         lambda *a: first_kernel(experts, cap, *a),
         grid_spec=pltpu.PrefetchScalarGridSpec(
-            num_scalar_prefetch=2,
+            num_scalar_prefetch=1,
             grid=(row_width // chunk,),
-            in_specs=[whole, whole, pl.BlockSpec((columns, chunk), lambda j, a, c: (0, j))],
-            out_specs=[pl.BlockSpec((tokens, chunk), lambda j, a, c: (0, j)), matrix, matrix],
+            in_specs=[
+                whole,
+                whole,
+                pl.BlockSpec((count_a, chunk), lambda j, a: (0, j)),
+                pl.BlockSpec((count_1, chunk), lambda j, a: (0, j)),
+            ],
+            out_specs=[pl.BlockSpec((tokens, chunk), lambda j, a: (0, j)), matrix, matrix],
             scratch_shapes=[
                 pltpu.VMEM((experts, tokens), jnp.int32),
-                pltpu.VMEM((tokens, columns), jnp.bfloat16),
-                pltpu.VMEM((tokens, columns), jnp.bfloat16),
+                pltpu.VMEM((tokens, count_a + count_1), jnp.bfloat16),
+                pltpu.VMEM((tokens, count_a + count_1), jnp.bfloat16),
+                pltpu.VMEM((count_a + count_1, chunk), jnp.bfloat16),
             ],
         ),
         out_shape=[jax.ShapeDtypeStruct((tokens, row_width), jnp.float32)]
-        + [jax.ShapeDtypeStruct((tokens, columns), jnp.bfloat16)] * 2,
+        + [jax.ShapeDtypeStruct((tokens, count_1), jnp.bfloat16)] * 2,
         cost_estimate=pl.CostEstimate(
-            flops=4 * columns * tokens * row_width, bytes_accessed=9_000_000, transcendentals=0
+            flops=4 * (count_a + count_1) * tokens * row_width,
+            bytes_accessed=9_000_000,
+            transcendentals=0,
         ),
         compiler_params=pltpu.CompilerParams(vmem_limit_bytes=60 * 2**20),
-    )(order_a, order_b, choice, gates, rows)
+    )(order, choice, gates, rows_a, rows_1)
 
 
 def second_kernel(high, low, rows, sum_ref, out_ref):
@@ -399,20 +429,40 @@
 
     pick = z * 2 + core
     take_a = jnp.array([0, 2, 1, 0, 2, 0, 0, 1], jnp.int32)[pick]
-    take_b = jnp.array([5, 3, 3, 1, 2, 0, 4, 2], jnp.int32)[pick]
-    out_a = expert_rows(take_a, got_a, (own, r1, l1), hidden)
+    (out_a,) = expert_rows(take_a, jnp.int32(1), got_a, (own, r1, l1), hidden, cap, 1)
     got_b, out_a = lax.optimization_barrier((got_b, out_a))
-    back_a = exchange(out_a.reshape(8, cap, -1))
+    back_a = exchange(out_a.reshape(8, cap, -1)).reshape(8 * cap, -1)
     r2, l2, out_a = lax.optimization_barrier((r2, l2, out_a))
     r3 = send(r2, along_z(1, ((2, 0),)))
     l3 = send(l2, along_z(-1, ((1, 0),)))
-    r3, l3, back_a = lax.optimization_barrier((r3, l3, back_a))
-    out_b = expert_rows(take_b, got_b, (r1, l1, r2, l2, r3, l3), hidden)
-    back_b = exchange(out_b.reshape(8, cap, -1))
+
+    def second(on, chosen, weights, earlier):
+        keep, give = expert_rows(chosen[pick], core == on, got_b, weights, hidden, cap, 2)
+        earlier, keep, give = lax.optimization_barrier((earlier, keep, give))
+        taken = send(give, all_pairs(lambda y, c, z, x: (y, 1 - c, z, x) if c == on else None))
+        return jnp.where(core == on, keep, taken), earlier
+
+    def give_back(rows):
+        return exchange(rows.reshape(8, cap // 2, -1)).reshape(4 * cap, -1)
+
+    rows_1, _ = second(1, jnp.array([0, 3, 0, 1, 0, 2, 0, 0], jnp.int32), (r2, l1, r1, l2), ())
+    back_a, rows_1 = lax.optimization_barrier((back_a, rows_1))
+    back_1 = give_back(rows_1)
+    r3, l3, got_b = lax.optimization_barrier((r3, l3, after(got_b, rows_1)))
+    rows_0, back_1 = second(
+        0, jnp.array([3, 0, 2, 0, 1, 0, 0, 0], jnp.int32), (r3, r2, l2, l3), back_1
+    )
+    back_0 = give_back(rows_0)
+    order_c = [
+        4 * (3 - place(jnp.int32(on), z)) + 2 * (s // 4) + s % 4 // 2
+        for on in (1, 0)
+        for s in range(8)
+    ]
+    order = jnp.concatenate([order_a, jnp.stack(order_c).astype(jnp.int32)])
     sum_a, high, low = combine_first(
-        after(order_a, out_b), order_b, choice, gates, back_a.reshape(8 * cap, -1), experts, cap
-    )
-    return combine_second(high, low, back_b.reshape(8 * cap, -1), sum_a)[None]
+        after(order, rows_0), choice, gates, back_a, back_1, experts, cap
+    )
+    return combine_second(high, low, back_0, sum_a)[None]
 
 
 def expert_ffn(token_rows, up_rows, up_vals, down_rows, down_vals):

time: 230 us -> 224 us (0.974); the launches traced: 229 us -> 220 us
  waiting for transfers between devices: 122 us -> 95.1 us
  other arithmetic: 0 us -> 7.99 us
  starting transfers between devices: 35.3 us -> 41.8 us
  Pallas kernels: 60.2 us -> 62.6 us
    all_to_all x4 -> x5, waiting for transfers between devices: 92.1 us -> 51.3 us  [exchange(): return lax.all_to_all(rows, PLANE, split_axis=0, concat_axis=0, tiled=True)]
    ppermute x6 -> x8, waiting for transfers between devices: 30.3 us -> 43.9 us  [send(): return lax.ppermute(value, AXES, pairs)]
    select_n x0 -> x2, other arithmetic: none -> 4.14 us  [second(): return (jnp.where(core == on, keep, taken), earlier)]
    another operation x0 -> x3, other arithmetic: none -> 3.85 us  [expert_rows(): jnp.stack([chosen, active]).astype(jnp.int32)]
    all_to_all x4 -> x5, starting transfers between devices: 16.4 us -> 19.9 us  [exchange(): return lax.all_to_all(rows, PLANE, split_axis=0, concat_axis=0, tiled=True)]
    ppermute x6 -> x8, starting transfers between devices: 18.9 us -> 22 us  [send(): return lax.ppermute(value, AXES, pairs)]
    pallas_call x2 -> x3, Pallas kernels: 26 us -> 28.1 us  [expert_rows(): pl.pallas_call(lambda *a: ffn_kernel(len(weights), cap, *a), in_specs=[sm...]
  transfers between devices with their start and end apart: 10 -> 13, of which waited for: 6 -> 9; matrix products, arithmetic and copies ran while one was open for 1% -> 4% of each run, Pallas kernels for 15% -> 23%
where the time goes in v4:
time: 224 us; the launch traced here: 220 us
  waiting for transfers between devices  95.1 us (42%)
  Pallas kernels  62.6 us (28%)
  starting transfers between devices  41.8 us (19%)
  other arithmetic  7.99 us (4%)
  local copies, waits for them, and re-layouts  6.65 us (3%)
  blocking collectives  5.58 us (2%)
    all_to_all x5, waiting for transfers between devices, exchange(): return lax.all_to_all(rows, PLANE, split_axis=0, concat_axis=0, tiled=True)  51.3 us
    ppermute x8, waiting for transfers between devices, send(): return lax.ppermute(value, AXES, pairs)  43.9 us
    pallas_call x3, Pallas kernels, expert_rows(): pl.pallas_call(lambda *a: ffn_kernel(len(weights), cap, *a), in_specs=[sm...  28.1 us
    ppermute x8, starting transfers between devices, send(): return lax.ppermute(value, AXES, pairs)  22 us
    all_to_all x5, starting transfers between devices, exchange(): return lax.all_to_all(rows, PLANE, split_axis=0, concat_axis=0, tiled=True)  19.9 us
    pallas_call x2, Pallas kernels, gather_rows(): pl.pallas_call(lambda *a: gather_kernel(experts, cap, *a), grid_spec=pltp...  12.7 us
    pallas_call x1, Pallas kernels, combine_first(): pl.pallas_call(lambda *a: first_kernel(experts, cap, *a), grid_spec=pltpu...  10.4 us
    pallas_call x1, Pallas kernels, combine_second(): pl.pallas_call(second_kernel, grid=(row_width // chunk,), in_specs=[matri...  6.16 us
  transfers between devices with their start and end apart: 13, of which 9 were waited for; matrix products, arithmetic and copies ran while one was open for 4% of the time, Pallas kernels for 23%

profile of v4, /device:TPU:0, one launch (start us, length us, event | category | flops | bytes accessed | tf_op | source)
XLA Modules:
  0.0 219.9 jit_solution(17765712095966503512)
XLA Ops:
  0.0 5.3 %shard_map.100.a_2_ = bf16[16400,128]{1,0:T(8,128)(2,1)} custom-call(s32[1]{0:T(128)} %bitcast.19.a_0_, bf16[2,8192,128]{2,1,0:T(8,128)(2,1)} %bitcast.39, bf16[2,8192,128]{2,1,0:T(8,128)(2,1)} %bitcast.40, s32[2,2,32]{2,1,0:T(2,128)} %bitcast.46, s32[2,4,16]{2,1,0:T(4,128)} %bitcast.43), custom_call_target="tpu_custom_call" | custom-call | bytes 8400000 | tf_op jit(solution)/shard_map/pallas_call | solution.py:74
  5.3 2.7 %collective-permute-start.1 = (bf16[16400,128]{1,0:T(8,128)(2,1)}, bf16[16400,128]{1,0:T(8,128)(2,1)}, u32[]{:S(2)}, u32[]{:S(2)}) collective-permute-start(bf16[16400,128]{1,0:T(8,128)(2,1)} %shard_map.100.a_2_), channel_id=1, source_target_pairs={{6,4},{7,5},{10,8},{11,9},{12,10},{13,11},{22,20},{23,21},{26,24},... | collective-permute-start | bytes 12595208 | tf_op jit(solution)/shard_map/ppermute | solution.py:38
  8.0 6.9 %collective-permute-start = (bf16[16400,128]{1,0:T(8,128)(2,1)}, bf16[16400,128]{1,0:T(8,128)(2,1)}, u32[]{:S(2)}, u32[]{:S(2)}) collective-permute-start(bf16[16400,128]{1,0:T(8,128)(2,1)} %shard_map.100.a_2_), channel_id=1, source_target_pairs={{0,2},{1,3},{10,12},{11,13},{12,14},{13,15},{16,18},{17,19},{26,28... | collective-permute-start | bytes 12595208 | tf_op jit(solution)/shard_map/ppermute | solution.py:38
  14.8 0.6 stack.107.a_0_
  15.5 5.6 %all-gather.1.a_2_ = s32[4,2,512]{2,1,0:T(2,128)} all-gather(s32[1,2,512]{2,1,0:T(2,128)S(1)} %bitcast.45), channel_id=2, replica_groups=mesh['grp'=4,'z'=4,'x'=2] {'grp'}, dimensions={0}, use_global_device_ids=true | all-gather | bytes 20480 | tf_op jit(solution)/shard_map/all_gather | solution.py:416
  21.0 6.3 %shard_map.101 = bf16[8,384,512]{2,1,0:T(8,128)(2,1)} custom-call(s32[8]{0:T(128)} %stack.107.a_0_, bf16[2048,512]{1,0:T(8,128)(2,1)} %bitcast.47, s32[4,2,512]{2,1,0:T(2,128)} %all-gather.1.a_2_), custom_call_target="tpu_custom_call" | custom-call | flops 1610612736 | bytes 9000000 | tf_op jit(solution)/shard_map/pallas_call | solution.py:132
  27.3 3.7 %all-to-all-start = ((bf16[8,384,512]{2,1,0:T(8,128)(2,1)}), bf16[8,384,512]{2,1,0:T(8,128)(2,1)S(1)}, u32[]{:S(2)}, u32[]{:S(2)}) async-start(bf16[8,384,512]{2,1,0:T(8,128)(2,1)} %shard_map.101), calls=%async_computation | async-start | bytes 6291456 | tf_op jit(solution)/shard_map/all_to_all | solution.py:111
  31.1 0.6 stack.108.a_0_
  31.7 6.4 %shard_map.102 = bf16[8,384,512]{2,1,0:T(8,128)(2,1)} custom-call(s32[8]{0:T(128)} %stack.108.a_0_, bf16[2048,512]{1,0:T(8,128)(2,1)} %bitcast.48, s32[4,2,512]{2,1,0:T(2,128)} %all-gather.1.a_2_), custom_call_target="tpu_custom_call" | custom-call | flops 1610612736 | bytes 9000000 | tf_op jit(solution)/shard_map/pallas_call | solution.py:132
  38.0 0.0 collective-permute-done.1.a_4_.a_3_
  38.0 21.2 %collective-permute-done.a_3_.a_4_ = bf16[16400,128]{1,0:T(8,128)(2,1)} collective-permute-done((bf16[16400,128]{1,0:T(8,128)(2,1)}, bf16[16400,128]{1,0:T(8,128)(2,1)}, u32[]{:S(2)}, u32[]{:S(2)}) %collective-permute-start) | collective-permute-done | bytes 4198432 | tf_op jit(solution)/shard_map/ppermute | solution.py:38
  59.3 2.7 %collective-permute-start.2 = (bf16[16400,128]{1,0:T(8,128)(2,1)}, bf16[16400,128]{1,0:T(8,128)(2,1)}, u32[]{:S(2)}, u32[]{:S(2)}) collective-permute-start(bf16[16400,128]{1,0:T(8,128)(2,1)} %collective-permute-done.a_3_.a_4_), channel_id=1, source_target_pairs={{2,4},{3,5},{12,14},{13,15},{18,20},{19,21},{28,30},{29,31}} | collective-permute-start | bytes 12595208 | tf_op jit(solution)/shard_map/ppermute | solution.py:38
  61.9 2.6 %collective-permute-start.3 = (bf16[16400,128]{1,0:T(8,128)(2,1)}, bf16[16400,128]{1,0:T(8,128)(2,1)}, u32[]{:S(2)}, u32[]{:S(2)}) collective-permute-start(bf16[16400,128]{1,0:T(8,128)(2,1)} %collective-permute-done.1.a_4_.a_3_), channel_id=1, source_target_pairs={{4,2},{5,3},{10,8},{11,9},{20,18},{21,19},{26,24},{27,25}} | collective-permute-start | bytes 12595208 | tf_op jit(solution)/shard_map/ppermute | solution.py:38
  64.5 3.5 %all-to-all-done.a_1_ = bf16[8,384,512]{2,1,0:T(8,128)(2,1)S(1)} async-done(((bf16[8,384,512]{2,1,0:T(8,128)(2,1)}), bf16[8,384,512]{2,1,0:T(8,128)(2,1)S(1)}, u32[]{:S(2)}, u32[]{:S(2)}) %all-to-all-start) | async-done | bytes 3145760 | tf_op jit(solution)/shard_map/all_to_all | solution.py:111
  68.0 1.7 copy-done.2
  69.7 3.6 %all-to-all-start.1 = ((bf16[8,384,512]{2,1,0:T(8,128)(2,1)}), bf16[8,384,512]{2,1,0:T(8,128)(2,1)S(1)}, u32[]{:S(2)}, u32[]{:S(2)}) async-start(bf16[8,384,512]{2,1,0:T(8,128)(2,1)} %shard_map.102), calls=%async_computation.1 | async-start | bytes 6291456 | tf_op jit(solution)/shard_map/all_to_all | solution.py:111
  73.4 0.6 dynamic_slice.9
  73.9 1.3 pad_add_fusion.a_0_
  75.2 13.4 %shard_map.103 = bf16[768,2048]{1,0:T(8,128)(2,1)} custom-call(s32[2]{0:T(128)} %pad_add_fusion.a_0_, bf16[8,384,512]{2,1,0:T(8,128)(2,1)} %copy-done.2, bf16[16400,128]{1,0:T(8,128)(2,1)} %shard_map.100.a_2_, bf16[16400,128]{1,0:T(8,128)(2,1)} %collective-permute-done.a_3_.a_4_, bf16[16400,128]{1,0:T(8,128)(2,1)} %collective-permute-done.1.a_4_.a_3_), custom_call_target="tpu_custom_call" | custom-call | flops 6442450944 | bytes 12000000 | tf_op jit(solution)/shard_map/pallas_call | solution.py:268
  88.7 21.5 %all-to-all-done.1.a_1_ = bf16[8,384,512]{2,1,0:T(8,128)(2,1)S(1)} async-done(((bf16[8,384,512]{2,1,0:T(8,128)(2,1)}), bf16[8,384,512]{2,1,0:T(8,128)(2,1)S(1)}, u32[]{:S(2)}, u32[]{:S(2)}) %all-to-all-start.1) | async-done | bytes 3145760 | tf_op jit(solution)/shard_map/all_to_all | solution.py:111
  110.2 0.0 collective-permute-done.2.a_2_.a_3_
  110.2 0.0 collective-permute-done.3.a_5_.a_4_
  110.2 2.9 %collective-permute-start.5 = (bf16[16400,128]{1,0:T(8,128)(2,1)}, bf16[16400,128]{1,0:T(8,128)(2,1)}, u32[]{:S(2)}, u32[]{:S(2)}) collective-permute-start(bf16[16400,128]{1,0:T(8,128)(2,1)} %collective-permute-done.2.a_2_.a_3_), channel_id=1, source_target_pairs={{4,6},{5,7},{20,22},{21,23}} | collective-permute-start | bytes 12595208 | tf_op jit(solution)/shard_map/ppermute | solution.py:38
  113.1 1.3 collective-permute-start.6
  114.4 0.7 dynamic_slice.10
  115.1 5.3 %all-to-all-start.2 = ((bf16[8,96,2048]{2,1,0:T(8,128)(2,1)}), bf16[8,96,2048]{2,1,0:T(8,128)(2,1)}, u32[]{:S(2)}, u32[]{:S(2)}) async-start(bf16[8,96,2048]{2,1,0:T(8,128)(2,1)} %bitcast.41), calls=%async_computation.2 | async-start | bytes 6291456 | tf_op jit(solution)/shard_map/all_to_all | solution.py:111
  120.4 1.3 pad_add_fusion.1.a_0_
  121.7 1.2 shard_map.104
  123.0 1.3 collective-permute-start.4
  124.3 16.3 %collective-permute-done.4 = bf16[384,2048]{1,0:T(8,128)(2,1)S(1)} collective-permute-done((bf16[384,2048]{1,0:T(8,128)(2,1)}, bf16[384,2048]{1,0:T(8,128)(2,1)S(1)}, u32[]{:S(2)}, u32[]{:S(2)}) %collective-permute-start.4) | collective-permute-done | bytes 1572896 | tf_op jit(solution)/shard_map/ppermute | solution.py:38
  140.6 1.4 broadcast_select_fusion
  141.9 15.9 %all-to-all-done.2 = bf16[8,96,2048]{2,1,0:T(8,128)(2,1)} async-done(((bf16[8,96,2048]{2,1,0:T(8,128)(2,1)}), bf16[8,96,2048]{2,1,0:T(8,128)(2,1)}, u32[]{:S(2)}, u32[]{:S(2)}) %all-to-all-start.2) | async-done | bytes 3145760 | tf_op jit(solution)/shard_map/all_to_all | solution.py:111
  157.8 3.6 %all-to-all-start.3 = ((bf16[8,48,2048]{2,1,0:T(8,128)(2,1)}), bf16[8,48,2048]{2,1,0:T(8,128)(2,1)S(1)}, u32[]{:S(2)}, u32[]{:S(2)}) async-start(bf16[8,48,2048]{2,1,0:T(8,128)(2,1)} %bitcast.28), calls=%async_computation.3 | async-start | bytes 3145728 | tf_op jit(solution)/shard_map/all_to_all | solution.py:111
  161.4 0.6 dynamic_slice.11
  162.1 1.2 pad_add_fusion.2.a_0_
  163.3 0.0 collective-permute-done.5.a_2_
  163.3 3.2 %collective-permute-done.6.a_5_ = bf16[16400,128]{1,0:T(8,128)(2,1)} collective-permute-done((bf16[16400,128]{1,0:T(8,128)(2,1)}, bf16[16400,128]{1,0:T(8,128)(2,1)}, u32[]{:S(2)}, u32[]{:S(2)}) %collective-permute-start.6) | collective-permute-done | bytes 4198432 | tf_op jit(solution)/shard_map/ppermute | solution.py:38
  166.5 13.4 %shard_map.105 = (bf16[384,2048]{1,0:T(8,128)(2,1)}, bf16[384,2048]{1,0:T(8,128)(2,1)}) custom-call(s32[2]{0:T(128)} %pad_add_fusion.2.a_0_, bf16[8,384,512]{2,1,0:T(8,128)(2,1)} %copy-done.1, bf16[16400,128]{1,0:T(8,128)(2,1)} %collective-permute-done.5.a_2_, bf16[16400,128]{1,0:T(8,128)(2,1)} %collective-permute-done.2.a_2_.a_3_, ...), custom_call_target="tpu_custom_call" | custom-call | flops 6442450944 | bytes 12000000 | tf_op jit(solution)/shard_map/pallas_call | solution.py:268
  179.9 1.5 all-to-all-done.3
  181.4 1.6 collective-permute-start.7
  183.1 3.1 %collective-permute-done.7 = bf16[384,2048]{1,0:T(8,128)(2,1)S(1)} collective-permute-done((bf16[384,2048]{1,0:T(8,128)(2,1)}, bf16[384,2048]{1,0:T(8,128)(2,1)S(1)}, u32[]{:S(2)}, u32[]{:S(2)}) %collective-permute-start.7) | collective-permute-done | bytes 1572896 | tf_op jit(solution)/shard_map/ppermute | solution.py:38
  186.2 2.8 %broadcast_select_fusion.1 = bf16[384,2048]{1,0:T(8,128)(2,1)} fusion(bf16[384,2048]{1,0:T(8,128)(2,1)} %get-tuple-element.53, bf16[384,2048]{1,0:T(8,128)(2,1)S(1)} %collective-permute-done.7, pred[]{:T(512)S(6)} %eq.10), kind=kLoop, calls=%fused_computation.1 | loop fusion | flops 786432 | bytes 4718593 | tf_op jit(solution)/shard_map/jit(_where)/select_n | solution.py:443
  189.0 3.6 %all-to-all-start.4 = ((bf16[8,48,2048]{2,1,0:T(8,128)(2,1)}), bf16[8,48,2048]{2,1,0:T(8,128)(2,1)S(1)}, u32[]{:S(2)}, u32[]{:S(2)}) async-start(bf16[8,48,2048]{2,1,0:T(8,128)(2,1)} %bitcast.33), calls=%async_computation.4 | async-start | bytes 3145728 | tf_op jit(solution)/shard_map/all_to_all | solution.py:111
  192.6 0.7 concatenate.4.a_0_
  193.3 10.4 %shard_map.106 = (f32[512,2048]{1,0:T(8,128)}, bf16[512,384]{1,0:T(8,128)(2,1)}, bf16[512,384]{1,0:T(8,128)(2,1)}) custom-call(s32[24]{0:T(128)} %concatenate.4.a_0_, s32[2,512]{1,0:T(2,128)} %bitcast.44, f32[2,512]{1,0:T(2,128)} %bitcast.49, bf16[768,2048]{1,0:T(8,128)(2,1)} %bitcast.26.a_3_, bf16[384,2048]{1,0:T(8,128)(2,1)} %bitcast.42), custom_call_target="tpu_custom_call" | custom-call | flops 4831838208 | bytes 9000000 | tf_op jit(solution)/shard_map/pallas_call | solution.py:337
  203.7 8.9 %all-to-all-done.4 = bf16[8,48,2048]{2,1,0:T(8,128)(2,1)S(1)} async-done(((bf16[8,48,2048]{2,1,0:T(8,128)(2,1)}), bf16[8,48,2048]{2,1,0:T(8,128)(2,1)S(1)}, u32[]{:S(2)}, u32[]{:S(2)}) %all-to-all-start.4) | async-done | bytes 1572896 | tf_op jit(solution)/shard_map/all_to_all | solution.py:111
  212.6 1.2 copy-done
  213.8 6.2 %shard_map.107 = bf16[512,2048]{1,0:T(8,128)(2,1)} custom-call(bf16[512,384]{1,0:T(8,128)(2,1)} %get-tuple-element.58.high, bf16[512,384]{1,0:T(8,128)(2,1)} %get-tuple-element.59.low, bf16[384,2048]{1,0:T(8,128)(2,1)} %bitcast.38, f32[512,2048]{1,0:T(8,128)} %get-tuple-element.60.sum_ref), custom_call_target="tpu_custom_call" | custom-call | flops 1610612736 | bytes 9000000 | tf_op jit(solution)/shard_map/pallas_call | solution.py:379
  (14 shorter events, 0.0 us)
Async XLA Ops:
  0.0 15.5 %copy-start.4 = (s32[1,512,2]{1,2,0:T(2,128)S(1)}, s32[1,512,2]{1,2,0:T(2,128)}, u32[]{:S(2)}) copy-start(s32[1,512,2]{1,2,0:T(2,128)} %param.11) | copy-start | bytes 12292
  5.3 32.8 %collective-permute-start.1 = (bf16[16400,128]{1,0:T(8,128)(2,1)}, bf16[16400,128]{1,0:T(8,128)(2,1)}, u32[]{:S(2)}, u32[]{:S(2)}) collective-permute-start(bf16[16400,128]{1,0:T(8,128)(2,1)} %shard_map.100.a_2_), channel_id=1, source_target_pairs={{6,4},{7,5},{10,8},{11,9},{12,10},{13,11},{22,20},{23,21},{26,24},... | collective-permute-start | bytes 12595208 | tf_op jit(solution)/shard_map/ppermute | solution.py:38
  8.0 51.3 %collective-permute-start = (bf16[16400,128]{1,0:T(8,128)(2,1)}, bf16[16400,128]{1,0:T(8,128)(2,1)}, u32[]{:S(2)}, u32[]{:S(2)}) collective-permute-start(bf16[16400,128]{1,0:T(8,128)(2,1)} %shard_map.100.a_2_), channel_id=1, source_target_pairs={{0,2},{1,3},{10,12},{11,13},{12,14},{13,15},{16,18},{17,19},{26,28... | collective-permute-start | bytes 12595208 | tf_op jit(solution)/shard_map/ppermute | solution.py:38
  27.3 40.7 %all-to-all-start = ((bf16[8,384,512]{2,1,0:T(8,128)(2,1)}), bf16[8,384,512]{2,1,0:T(8,128)(2,1)S(1)}, u32[]{:S(2)}, u32[]{:S(2)}) async-start(bf16[8,384,512]{2,1,0:T(8,128)(2,1)} %shard_map.101), calls=%async_computation | async-start | bytes 6291456 | tf_op jit(solution)/shard_map/all_to_all | solution.py:111
  38.0 35.3 %copy-start.7 = (s32[8]{0:T(128)S(1)}, s32[8]{0:T(128)}, u32[]{:S(2)}) copy-start(s32[8]{0:T(128)} %constant.51.clone) | copy-start | bytes 100
  59.3 50.9 %collective-permute-start.2 = (bf16[16400,128]{1,0:T(8,128)(2,1)}, bf16[16400,128]{1,0:T(8,128)(2,1)}, u32[]{:S(2)}, u32[]{:S(2)}) collective-permute-start(bf16[16400,128]{1,0:T(8,128)(2,1)} %collective-permute-done.a_3_.a_4_), channel_id=1, source_target_pairs={{2,4},{3,5},{12,14},{13,15},{18,20},{19,21},{28,30},{29,31}} | collective-permute-start | bytes 12595208 | tf_op jit(solution)/shard_map/ppermute | solution.py:38
  61.9 48.3 %collective-permute-start.3 = (bf16[16400,128]{1,0:T(8,128)(2,1)}, bf16[16400,128]{1,0:T(8,128)(2,1)}, u32[]{:S(2)}, u32[]{:S(2)}) collective-permute-start(bf16[16400,128]{1,0:T(8,128)(2,1)} %collective-permute-done.1.a_4_.a_3_), channel_id=1, source_target_pairs={{4,2},{5,3},{10,8},{11,9},{20,18},{21,19},{26,24},{27,25}} | collective-permute-start | bytes 12595208 | tf_op jit(solution)/shard_map/ppermute | solution.py:38
  68.0 1.7 copy-start.2
  69.7 40.5 %all-to-all-start.1 = ((bf16[8,384,512]{2,1,0:T(8,128)(2,1)}), bf16[8,384,512]{2,1,0:T(8,128)(2,1)S(1)}, u32[]{:S(2)}, u32[]{:S(2)}) async-start(bf16[8,384,512]{2,1,0:T(8,128)(2,1)} %shard_map.102), calls=%async_computation.1 | async-start | bytes 6291456 | tf_op jit(solution)/shard_map/all_to_all | solution.py:111
  75.2 39.2 %copy-start.6 = (s32[8]{0:T(128)S(1)}, s32[8]{0:T(128)}, u32[]{:S(2)}) copy-start(s32[8]{0:T(128)} %constant.52.clone) | copy-start | bytes 100
  110.2 4.9 %copy-start.1 = (bf16[8,384,512]{2,1,0:T(8,128)(2,1)}, bf16[8,384,512]{2,1,0:T(8,128)(2,1)S(1)}, u32[]{:S(2)}) copy-start(bf16[8,384,512]{2,1,0:T(8,128)(2,1)S(1)} %all-to-all-done.1.a_1_) | copy-start | bytes 9437188
  110.2 53.1 %collective-permute-start.5 = (bf16[16400,128]{1,0:T(8,128)(2,1)}, bf16[16400,128]{1,0:T(8,128)(2,1)}, u32[]{:S(2)}, u32[]{:S(2)}) collective-permute-start(bf16[16400,128]{1,0:T(8,128)(2,1)} %collective-permute-done.2.a_2_.a_3_), channel_id=1, source_target_pairs={{4,6},{5,7},{20,22},{21,23}} | collective-permute-start | bytes 12595208 | tf_op jit(solution)/shard_map/ppermute | solution.py:38
  113.1 53.4 %collective-permute-start.6 = (bf16[16400,128]{1,0:T(8,128)(2,1)}, bf16[16400,128]{1,0:T(8,128)(2,1)}, u32[]{:S(2)}, u32[]{:S(2)}) collective-permute-start(bf16[16400,128]{1,0:T(8,128)(2,1)} %collective-permute-done.3.a_5_.a_4_), channel_id=1, source_target_pairs={{2,0},{3,1},{18,16},{19,17}} | collective-permute-start | bytes 12595208 | tf_op jit(solution)/shard_map/ppermute | solution.py:38
  115.1 42.7 %all-to-all-start.2 = ((bf16[8,96,2048]{2,1,0:T(8,128)(2,1)}), bf16[8,96,2048]{2,1,0:T(8,128)(2,1)}, u32[]{:S(2)}, u32[]{:S(2)}) async-start(bf16[8,96,2048]{2,1,0:T(8,128)(2,1)} %bitcast.41), calls=%async_computation.2 | async-start | bytes 6291456 | tf_op jit(solution)/shard_map/all_to_all | solution.py:111
  123.0 17.6 %collective-permute-start.4 = (bf16[384,2048]{1,0:T(8,128)(2,1)}, bf16[384,2048]{1,0:T(8,128)(2,1)S(1)}, u32[]{:S(2)}, u32[]{:S(2)}) collective-permute-start(bf16[384,2048]{1,0:T(8,128)(2,1)} %get-tuple-element.45), channel_id=1, source_target_pairs={{8,0},{9,1},{10,2},{11,3},{12,4},{13,5},{14,6},{15,7},{24,16},{25,... | collective-permute-start | bytes 4718600 | tf_op jit(solution)/shard_map/ppermute | solution.py:38
  141.9 19.5 %copy-start.5 = (s32[8]{0:T(128)S(1)}, s32[8]{0:T(128)}, u32[]{:S(2)}) copy-start(s32[8]{0:T(128)} %constant.53.clone) | copy-start | bytes 100
  157.8 23.6 %all-to-all-start.3 = ((bf16[8,48,2048]{2,1,0:T(8,128)(2,1)}), bf16[8,48,2048]{2,1,0:T(8,128)(2,1)S(1)}, u32[]{:S(2)}, u32[]{:S(2)}) async-start(bf16[8,48,2048]{2,1,0:T(8,128)(2,1)} %bitcast.28), calls=%async_computation.3 | async-start | bytes 3145728 | tf_op jit(solution)/shard_map/all_to_all | solution.py:111
  181.4 7.6 %copy-start.3 = (bf16[8,48,2048]{2,1,0:T(8,128)(2,1)}, bf16[8,48,2048]{2,1,0:T(8,128)(2,1)S(1)}, u32[]{:S(2)}) copy-start(bf16[8,48,2048]{2,1,0:T(8,128)(2,1)S(1)} %all-to-all-done.3) | copy-start | bytes 4718596
  181.4 4.8 %collective-permute-start.7 = (bf16[384,2048]{1,0:T(8,128)(2,1)}, bf16[384,2048]{1,0:T(8,128)(2,1)S(1)}, u32[]{:S(2)}, u32[]{:S(2)}) collective-permute-start(bf16[384,2048]{1,0:T(8,128)(2,1)} %get-tuple-element.54), channel_id=1, source_target_pairs={{0,8},{1,9},{2,10},{3,11},{4,12},{5,13},{6,14},{7,15},{16,24},{17,... | collective-permute-start | bytes 4718600 | tf_op jit(solution)/shard_map/ppermute | solution.py:38
  189.0 23.6 %all-to-all-start.4 = ((bf16[8,48,2048]{2,1,0:T(8,128)(2,1)}), bf16[8,48,2048]{2,1,0:T(8,128)(2,1)S(1)}, u32[]{:S(2)}, u32[]{:S(2)}) async-start(bf16[8,48,2048]{2,1,0:T(8,128)(2,1)} %bitcast.33), calls=%async_computation.4 | async-start | bytes 3145728 | tf_op jit(solution)/shard_map/all_to_all | solution.py:111
  212.6 1.2 copy-start

commit v5 on v4

--- a/solution.py
+++ b/solution.py
@@ -46,65 +46,72 @@
 TABLE_ROWS = 16
 
 
-def pack_kernel(pieces, which, up_ref, down_ref, up_at, down_at, out_ref):
-    step = pl.program_id(0)
-
-    @pl.when(step < pieces)
-    def _():
-        out_ref[...] = up_ref[0]
-
-    @pl.when((step >= pieces) & (step < 2 * pieces))
-    def _():
-        out_ref[...] = down_ref[0]
-
-    @pl.when(step == 2 * pieces)
-    def _():
-        ups, downs = up_at.shape[1], down_at.shape[1]
-        out_ref[0:TABLE_ROWS, :] = jnp.zeros((TABLE_ROWS, out_ref.shape[1]), jnp.bfloat16)
-        out_ref[0:ups, 0 : up_at.shape[2]] = up_at[0].astype(jnp.float32).astype(jnp.bfloat16)
-        out_ref[ups : ups + downs, 0 : down_at.shape[2]] = (
-            down_at[0].astype(jnp.float32).astype(jnp.bfloat16)
+def pack_kernel(pieces, which, up, down, up_at, down_at, out, held, rows, in_sem, out_sem):
+    size = up.shape[1]
+    step = size // pieces
+    inward, outward = [], []
+    for n in range(2 * pieces):
+        source, at = (up, n * step) if n < pieces else (down, (n - pieces) * step)
+        here = held.at[pl.ds(n * step, step)]
+        inward.append(
+            pltpu.make_async_copy(source.at[which[0], pl.ds(at, step)], here, in_sem.at[n])
         )
+        outward.append(
+            pltpu.make_async_copy(here, out.at[pl.ds(n * step, step)], out_sem.at[n])
+        )
+        inward[-1].start()
+    ups, downs = up_at.shape[1], down_at.shape[1]
+    rows[...] = jnp.zeros(rows.shape, jnp.bfloat16)
+    rows[0:ups, 0 : up_at.shape[2]] = up_at[which[0]].astype(jnp.float32).astype(jnp.bfloat16)
+    rows[ups : ups + downs, 0 : down_at.shape[2]] = (
+        down_at[which[0]].astype(jnp.float32).astype(jnp.bfloat16)
+    )
+    outward.append(
+        pltpu.make_async_copy(rows, out.at[pl.ds(2 * size, TABLE_ROWS)], out_sem.at[2 * pieces])
+    )
+    outward[-1].start()
+    for n in range(2 * pieces):
+        inward[n].wait()
+        outward[n].start()
+    for one in outward:
+        one.wait()
 
 
 def pack_weights(which, up, down, up_at, down_at):
-    pieces = 2
+    pieces = 4
     size, blk = up.shape[1], up.shape[2]
-    step = size // pieces
+    hbm = pl.BlockSpec(memory_space=pltpu.HBM)
+    vmem = pl.BlockSpec(memory_space=pltpu.VMEM)
     return pl.pallas_call(
         lambda *a: pack_kernel(pieces, *a),
-        grid_spec=pltpu.PrefetchScalarGridSpec(
-            num_scalar_prefetch=1,
-            grid=(2 * pieces + 1,),
-            in_specs=[
-                pl.BlockSpec((1, step, blk), lambda i, w: (w[0], jnp.minimum(i, pieces - 1), 0)),
-                pl.BlockSpec(
-                    (1, step, blk), lambda i, w: (w[0], jnp.clip(i - pieces, 0, pieces - 1), 0)
-                ),
-                pl.BlockSpec((1,) + up_at.shape[1:], lambda i, w: (w[0], 0, 0)),
-                pl.BlockSpec((1,) + down_at.shape[1:], lambda i, w: (w[0], 0, 0)),
-            ],
-            out_specs=pl.BlockSpec((step, blk), lambda i, w: (i, 0)),
-        ),
+        in_specs=[pl.BlockSpec(memory_space=pltpu.SMEM), hbm, hbm, vmem, vmem],
+        out_specs=hbm,
         out_shape=jax.ShapeDtypeStruct((2 * size + TABLE_ROWS, blk), up.dtype),
+        scratch_shapes=[
+            pltpu.VMEM((2 * size, blk), jnp.bfloat16),
+            pltpu.VMEM((TABLE_ROWS, blk), jnp.bfloat16),
+            pltpu.SemaphoreType.DMA((2 * pieces,)),
+            pltpu.SemaphoreType.DMA((2 * pieces + 1,)),
+        ],
         cost_estimate=pl.CostEstimate(flops=0, bytes_accessed=8_400_000, transcendentals=0),
         compiler_params=pltpu.CompilerParams(vmem_limit_bytes=60 * 2**20),
     )(which[None].astype(jnp.int32), up, down, up_at, down_at)
 
 
-def slot_rows(first, second, experts):
-    tokens = first.shape[1]
+def slot_rows(pairs, experts):
+    tokens = pairs[0][0].shape[1]
     ids = lax.broadcasted_iota(jnp.int32, (experts, tokens), 0)
-    named = (ids == first) | (ids == second)
+    named = [jnp.where((ids == a) | (ids == b), 1.0, 0.0) for a, b in pairs]
+    named = jnp.concatenate(named, axis=0)
     before = lax.broadcasted_iota(jnp.int32, (tokens, tokens), 0) < lax.broadcasted_iota(
         jnp.int32, (tokens, tokens), 1
     )
     count = jnp.dot(
-        jnp.where(named, 1.0, 0.0).astype(jnp.bfloat16),
+        named.astype(jnp.bfloat16),
         jnp.where(before, 1.0, 0.0).astype(jnp.bfloat16),
         preferred_element_type=jnp.float32,
     )
-    return jnp.where(named, count.astype(jnp.int32), -1)
+    return jnp.where(named > 0.5, count.astype(jnp.int32), -1)
 
 
 def exchange(rows):
@@ -113,10 +120,16 @@
 
 def gather_kernel(experts, cap, order, x_ref, choice_ref, out_ref, slots, pick):
     tokens = x_ref.shape[0]
-    slots[...] = slot_rows(choice_ref[0, 0:1, :], choice_ref[0, 1:2, :], experts)
+    part = pl.program_id(0)
+
+    @pl.when(part == 0)
+    def _():
+        pairs = [(choice_ref[b, 0:1, :], choice_ref[b, 1:2, :]) for b in range(choice_ref.shape[0])]
+        slots[...] = slot_rows(pairs, experts)
+
     row = lax.broadcasted_iota(jnp.int32, (cap, tokens), 0)
     for n in range(8):
-        line = slots[pl.ds(order[n], 1), :]
+        line = slots[pl.ds(part * experts + order[n], 1), :]
         pick[n * cap : (n + 1) * cap, :] = jnp.where(line == row, 1.0, 0.0).astype(jnp.bfloat16)
     for n in range(0, 8, 2):
         rows = jnp.dot(
@@ -136,11 +149,11 @@
             grid=(parts,),
             in_specs=[
                 pl.BlockSpec((tokens, width), lambda b, order: (b, 0)),
-                pl.BlockSpec((1, 2, tokens), lambda b, order: (b, 0, 0)),
+                pl.BlockSpec((parts, 2, tokens), lambda b, order: (0, 0, 0)),
             ],
             out_specs=pl.BlockSpec((8, cap, width), lambda b, order: (0, b, 0)),
             scratch_shapes=[
-                pltpu.VMEM((experts, tokens), jnp.int32),
+                pltpu.VMEM((parts * experts, tokens), jnp.int32),
                 pltpu.VMEM((8 * cap, tokens), jnp.bfloat16),
             ],
         ),
@@ -184,13 +197,6 @@
             at = pl.ds(n * piece, piece)
             copies.append(pltpu.make_async_copy(source.at[at], wts.at[at], w_sem.at[2 + n]))
         return copies
-
-    for i in range(n_weights):
-
-        @pl.when(chosen == i)
-        def _(i=i):
-            for one in weight_copies(sources[i]):
-                one.start()
 
     in_copies = []
     for n in range(8):
@@ -204,6 +210,13 @@
             )
         )
         in_copies[-1].start()
+    for i in range(n_weights):
+
+        @pl.when(chosen == i)
+        def _(i=i):
+            for one in weight_copies(sources[i]):
+                one.start()
+
     waits = weight_copies(sources[0])
     waits[0].wait()
     wide[...] = packed[...].astype(jnp.float32).astype(jnp.int32)
@@ -315,7 +328,7 @@
 
     @pl.when(pl.program_id(0) == 0)
     def _():
-        slots[...] = slot_rows(choice_ref[0:1, :], choice_ref[1:2, :], experts)
+        slots[...] = slot_rows([(choice_ref[0:1, :], choice_ref[1:2, :])], experts)
         blocks = [(n, cap, 0) for n in range(8)] + of_core(1)
         gate_matrix(order, blocks, slots, choice_ref, gate_ref, high, low)
         gate_matrix(order, of_core(0), slots, choice_ref, gate_ref, high_b, low_b)
@@ -373,7 +386,7 @@
 def combine_second(high, low, rows, so_far):
     tokens, columns = high.shape
     row_width = rows.shape[1]
-    chunk = 512
+    chunk = 1024
     matrix = pl.BlockSpec((tokens, columns), lambda j: (0, 0))
     block = pl.BlockSpec((tokens, chunk), lambda j: (0, j))
     return pl.pallas_call(

time: 224 us -> 222 us (level)
  Pallas kernels: 62.6 us -> 59.7 us
where the time goes in v5:
time: 222 us; the launch traced here: 218 us
  waiting for transfers between devices  96.1 us (43%)
  Pallas kernels  59.7 us (27%)
  starting transfers between devices  42.1 us (19%)
  other arithmetic  7.99 us (4%)
  local copies, waits for them, and re-layouts  6.65 us (3%)
  blocking collectives  5.58 us (3%)
    all_to_all x5, waiting for transfers between devices, exchange(): return lax.all_to_all(rows, PLANE, split_axis=0, concat_axis=0, tiled=True)  52.1 us
    ppermute x8, waiting for transfers between devices, send(): return lax.ppermute(value, AXES, pairs)  44 us
    pallas_call x3, Pallas kernels, expert_rows(): pl.pallas_call(lambda *a: ffn_kernel(len(weights), cap, *a), in_specs=[sm...  27.4 us
    ppermute x8, starting transfers between devices, send(): return lax.ppermute(value, AXES, pairs)  22 us
    all_to_all x5, starting transfers between devices, exchange(): return lax.all_to_all(rows, PLANE, split_axis=0, concat_axis=0, tiled=True)  20.2 us
    pallas_call x2, Pallas kernels, gather_rows(): pl.pallas_call(lambda *a: gather_kernel(experts, cap, *a), grid_spec=pltp...  12 us
    pallas_call x1, Pallas kernels, combine_first(): pl.pallas_call(lambda *a: first_kernel(experts, cap, *a), grid_spec=pltpu...  10.4 us
    all_gather x1, blocking collectives, per_device_planes(): choices = lax.all_gather(after(choice, own), 'grp')  5.58 us
  transfers between devices with their start and end apart: 13, of which 9 were waited for; matrix products, arithmetic and copies ran while one was open for 4% of the time, Pallas kernels for 23%

profile of v5, /device:TPU:0, one launch (start us, length us, event | category | flops | bytes accessed | tf_op | source)
XLA Modules:
  0.0 218.3 jit_solution(2341242953610315617)
XLA Ops:
  0.0 4.3 %shard_map.100.a_2_ = bf16[16400,128]{1,0:T(8,128)(2,1)} custom-call(s32[1]{0:T(128)} %bitcast.19.a_0_, bf16[2,8192,128]{2,1,0:T(8,128)(2,1)} %bitcast.39, bf16[2,8192,128]{2,1,0:T(8,128)(2,1)} %bitcast.40, s32[2,2,32]{2,1,0:T(2,128)} %bitcast.46, s32[2,4,16]{2,1,0:T(4,128)} %bitcast.43), custom_call_target="tpu_custom_call" | custom-call | bytes 8400000 | tf_op jit(solution)/shard_map/pallas_call | solution.py:85
  4.3 2.7 %collective-permute-start.1 = (bf16[16400,128]{1,0:T(8,128)(2,1)}, bf16[16400,128]{1,0:T(8,128)(2,1)}, u32[]{:S(2)}, u32[]{:S(2)}) collective-permute-start(bf16[16400,128]{1,0:T(8,128)(2,1)} %shard_map.100.a_2_), channel_id=1, source_target_pairs={{6,4},{7,5},{10,8},{11,9},{12,10},{13,11},{22,20},{23,21},{26,24},... | collective-permute-start | bytes 12595208 | tf_op jit(solution)/shard_map/ppermute | solution.py:38
  7.0 6.9 %collective-permute-start = (bf16[16400,128]{1,0:T(8,128)(2,1)}, bf16[16400,128]{1,0:T(8,128)(2,1)}, u32[]{:S(2)}, u32[]{:S(2)}) collective-permute-start(bf16[16400,128]{1,0:T(8,128)(2,1)} %shard_map.100.a_2_), channel_id=1, source_target_pairs={{0,2},{1,3},{10,12},{11,13},{12,14},{13,15},{16,18},{17,19},{26,28... | collective-permute-start | bytes 12595208 | tf_op jit(solution)/shard_map/ppermute | solution.py:38
  13.9 0.6 stack.107.a_0_
  14.5 5.6 %all-gather.1.a_2_ = s32[4,2,512]{2,1,0:T(2,128)} all-gather(s32[1,2,512]{2,1,0:T(2,128)S(1)} %bitcast.45), channel_id=2, replica_groups=mesh['grp'=4,'z'=4,'x'=2] {'grp'}, dimensions={0}, use_global_device_ids=true | all-gather | bytes 20480 | tf_op jit(solution)/shard_map/all_gather | solution.py:429
  20.1 6.0 %shard_map.101 = bf16[8,384,512]{2,1,0:T(8,128)(2,1)} custom-call(s32[8]{0:T(128)} %stack.107.a_0_, bf16[2048,512]{1,0:T(8,128)(2,1)} %bitcast.47, s32[4,2,512]{2,1,0:T(2,128)} %all-gather.1.a_2_), custom_call_target="tpu_custom_call" | custom-call | flops 1610612736 | bytes 9000000 | tf_op jit(solution)/shard_map/pallas_call | solution.py:145
  26.1 3.7 %all-to-all-start = ((bf16[8,384,512]{2,1,0:T(8,128)(2,1)}), bf16[8,384,512]{2,1,0:T(8,128)(2,1)S(1)}, u32[]{:S(2)}, u32[]{:S(2)}) async-start(bf16[8,384,512]{2,1,0:T(8,128)(2,1)} %shard_map.101), calls=%async_computation | async-start | bytes 6291456 | tf_op jit(solution)/shard_map/all_to_all | solution.py:118
  29.8 0.6 stack.108.a_0_
  30.4 6.0 %shard_map.102 = bf16[8,384,512]{2,1,0:T(8,128)(2,1)} custom-call(s32[8]{0:T(128)} %stack.108.a_0_, bf16[2048,512]{1,0:T(8,128)(2,1)} %bitcast.48, s32[4,2,512]{2,1,0:T(2,128)} %all-gather.1.a_2_), custom_call_target="tpu_custom_call" | custom-call | flops 1610612736 | bytes 9000000 | tf_op jit(solution)/shard_map/pallas_call | solution.py:145
  36.4 0.0 collective-permute-done.1.a_4_.a_3_
  36.4 21.9 %collective-permute-done.a_3_.a_4_ = bf16[16400,128]{1,0:T(8,128)(2,1)} collective-permute-done((bf16[16400,128]{1,0:T(8,128)(2,1)}, bf16[16400,128]{1,0:T(8,128)(2,1)}, u32[]{:S(2)}, u32[]{:S(2)}) %collective-permute-start) | collective-permute-done | bytes 4198432 | tf_op jit(solution)/shard_map/ppermute | solution.py:38
  58.3 2.7 %collective-permute-start.2 = (bf16[16400,128]{1,0:T(8,128)(2,1)}, bf16[16400,128]{1,0:T(8,128)(2,1)}, u32[]{:S(2)}, u32[]{:S(2)}) collective-permute-start(bf16[16400,128]{1,0:T(8,128)(2,1)} %collective-permute-done.a_3_.a_4_), channel_id=1, source_target_pairs={{2,4},{3,5},{12,14},{13,15},{18,20},{19,21},{28,30},{29,31}} | collective-permute-start | bytes 12595208 | tf_op jit(solution)/shard_map/ppermute | solution.py:38
  61.0 2.6 %collective-permute-start.3 = (bf16[16400,128]{1,0:T(8,128)(2,1)}, bf16[16400,128]{1,0:T(8,128)(2,1)}, u32[]{:S(2)}, u32[]{:S(2)}) collective-permute-start(bf16[16400,128]{1,0:T(8,128)(2,1)} %collective-permute-done.1.a_4_.a_3_), channel_id=1, source_target_pairs={{4,2},{5,3},{10,8},{11,9},{20,18},{21,19},{26,24},{27,25}} | collective-permute-start | bytes 12595208 | tf_op jit(solution)/shard_map/ppermute | solution.py:38
  63.6 3.2 %all-to-all-done.a_1_ = bf16[8,384,512]{2,1,0:T(8,128)(2,1)S(1)} async-done(((bf16[8,384,512]{2,1,0:T(8,128)(2,1)}), bf16[8,384,512]{2,1,0:T(8,128)(2,1)S(1)}, u32[]{:S(2)}, u32[]{:S(2)}) %all-to-all-start) | async-done | bytes 3145760 | tf_op jit(solution)/shard_map/all_to_all | solution.py:118
  66.7 1.7 copy-done.2
  68.4 3.6 %all-to-all-start.1 = ((bf16[8,384,512]{2,1,0:T(8,128)(2,1)}), bf16[8,384,512]{2,1,0:T(8,128)(2,1)S(1)}, u32[]{:S(2)}, u32[]{:S(2)}) async-start(bf16[8,384,512]{2,1,0:T(8,128)(2,1)} %shard_map.102), calls=%async_computation.1 | async-start | bytes 6291456 | tf_op jit(solution)/shard_map/all_to_all | solution.py:118
  72.1 0.6 dynamic_slice.9
  72.7 1.3 pad_add_fusion.a_0_
  74.0 13.4 %shard_map.103 = bf16[768,2048]{1,0:T(8,128)(2,1)} custom-call(s32[2]{0:T(128)} %pad_add_fusion.a_0_, bf16[8,384,512]{2,1,0:T(8,128)(2,1)} %copy-done.2, bf16[16400,128]{1,0:T(8,128)(2,1)} %shard_map.100.a_2_, bf16[16400,128]{1,0:T(8,128)(2,1)} %collective-permute-done.a_3_.a_4_, bf16[16400,128]{1,0:T(8,128)(2,1)} %collective-permute-done.1.a_4_.a_3_), custom_call_target="tpu_custom_call" | custom-call | flops 6442450944 | bytes 12000000 | tf_op jit(solution)/shard_map/pallas_call | solution.py:281
  87.3 21.6 %all-to-all-done.1.a_1_ = bf16[8,384,512]{2,1,0:T(8,128)(2,1)S(1)} async-done(((bf16[8,384,512]{2,1,0:T(8,128)(2,1)}), bf16[8,384,512]{2,1,0:T(8,128)(2,1)S(1)}, u32[]{:S(2)}, u32[]{:S(2)}) %all-to-all-start.1) | async-done | bytes 3145760 | tf_op jit(solution)/shard_map/all_to_all | solution.py:118
  108.9 0.0 collective-permute-done.2.a_2_.a_3_
  108.9 0.0 collective-permute-done.3.a_5_.a_4_
  108.9 2.9 %collective-permute-start.5 = (bf16[16400,128]{1,0:T(8,128)(2,1)}, bf16[16400,128]{1,0:T(8,128)(2,1)}, u32[]{:S(2)}, u32[]{:S(2)}) collective-permute-start(bf16[16400,128]{1,0:T(8,128)(2,1)} %collective-permute-done.2.a_2_.a_3_), channel_id=1, source_target_pairs={{4,6},{5,7},{20,22},{21,23}} | collective-permute-start | bytes 12595208 | tf_op jit(solution)/shard_map/ppermute | solution.py:38
  111.9 1.3 collective-permute-start.6
  113.2 0.7 dynamic_slice.10
  113.8 5.6 %all-to-all-start.2 = ((bf16[8,96,2048]{2,1,0:T(8,128)(2,1)}), bf16[8,96,2048]{2,1,0:T(8,128)(2,1)}, u32[]{:S(2)}, u32[]{:S(2)}) async-start(bf16[8,96,2048]{2,1,0:T(8,128)(2,1)} %bitcast.41), calls=%async_computation.2 | async-start | bytes 6291456 | tf_op jit(solution)/shard_map/all_to_all | solution.py:118
  119.5 1.3 pad_add_fusion.1.a_0_
  120.8 1.2 shard_map.104
  122.0 1.3 collective-permute-start.4
  123.3 15.7 %collective-permute-done.4 = bf16[384,2048]{1,0:T(8,128)(2,1)S(1)} collective-permute-done((bf16[384,2048]{1,0:T(8,128)(2,1)}, bf16[384,2048]{1,0:T(8,128)(2,1)S(1)}, u32[]{:S(2)}, u32[]{:S(2)}) %collective-permute-start.4) | collective-permute-done | bytes 1572896 | tf_op jit(solution)/shard_map/ppermute | solution.py:38
  139.1 1.4 broadcast_select_fusion
  140.4 16.5 %all-to-all-done.2 = bf16[8,96,2048]{2,1,0:T(8,128)(2,1)} async-done(((bf16[8,96,2048]{2,1,0:T(8,128)(2,1)}), bf16[8,96,2048]{2,1,0:T(8,128)(2,1)}, u32[]{:S(2)}, u32[]{:S(2)}) %all-to-all-start.2) | async-done | bytes 3145760 | tf_op jit(solution)/shard_map/all_to_all | solution.py:118
  156.9 3.6 %all-to-all-start.3 = ((bf16[8,48,2048]{2,1,0:T(8,128)(2,1)}), bf16[8,48,2048]{2,1,0:T(8,128)(2,1)S(1)}, u32[]{:S(2)}, u32[]{:S(2)}) async-start(bf16[8,48,2048]{2,1,0:T(8,128)(2,1)} %bitcast.28), calls=%async_computation.3 | async-start | bytes 3145728 | tf_op jit(solution)/shard_map/all_to_all | solution.py:118
  160.5 0.6 dynamic_slice.11
  161.1 1.2 pad_add_fusion.2.a_0_
  162.3 0.0 collective-permute-done.5.a_2_
  162.3 3.2 %collective-permute-done.6.a_5_ = bf16[16400,128]{1,0:T(8,128)(2,1)} collective-permute-done((bf16[16400,128]{1,0:T(8,128)(2,1)}, bf16[16400,128]{1,0:T(8,128)(2,1)}, u32[]{:S(2)}, u32[]{:S(2)}) %collective-permute-start.6) | collective-permute-done | bytes 4198432 | tf_op jit(solution)/shard_map/ppermute | solution.py:38
  165.5 12.8 %shard_map.105 = (bf16[384,2048]{1,0:T(8,128)(2,1)}, bf16[384,2048]{1,0:T(8,128)(2,1)}) custom-call(s32[2]{0:T(128)} %pad_add_fusion.2.a_0_, bf16[8,384,512]{2,1,0:T(8,128)(2,1)} %copy-done.1, bf16[16400,128]{1,0:T(8,128)(2,1)} %collective-permute-done.5.a_2_, bf16[16400,128]{1,0:T(8,128)(2,1)} %collective-permute-done.2.a_2_.a_3_, ...), custom_call_target="tpu_custom_call" | custom-call | flops 6442450944 | bytes 12000000 | tf_op jit(solution)/shard_map/pallas_call | solution.py:281
  178.4 2.1 all-to-all-done.3
  180.5 1.6 collective-permute-start.7
  182.1 3.1 %collective-permute-done.7 = bf16[384,2048]{1,0:T(8,128)(2,1)S(1)} collective-permute-done((bf16[384,2048]{1,0:T(8,128)(2,1)}, bf16[384,2048]{1,0:T(8,128)(2,1)S(1)}, u32[]{:S(2)}, u32[]{:S(2)}) %collective-permute-start.7) | collective-permute-done | bytes 1572896 | tf_op jit(solution)/shard_map/ppermute | solution.py:38
  185.2 2.8 %broadcast_select_fusion.1 = bf16[384,2048]{1,0:T(8,128)(2,1)} fusion(bf16[384,2048]{1,0:T(8,128)(2,1)} %get-tuple-element.53, bf16[384,2048]{1,0:T(8,128)(2,1)S(1)} %collective-permute-done.7, pred[]{:T(512)S(6)} %eq.10), kind=kLoop, calls=%fused_computation.1 | loop fusion | flops 786432 | bytes 4718593 | tf_op jit(solution)/shard_map/jit(_where)/select_n | solution.py:456
  188.0 3.6 %all-to-all-start.4 = ((bf16[8,48,2048]{2,1,0:T(8,128)(2,1)}), bf16[8,48,2048]{2,1,0:T(8,128)(2,1)S(1)}, u32[]{:S(2)}, u32[]{:S(2)}) async-start(bf16[8,48,2048]{2,1,0:T(8,128)(2,1)} %bitcast.33), calls=%async_computation.4 | async-start | bytes 3145728 | tf_op jit(solution)/shard_map/all_to_all | solution.py:118
  191.6 0.7 concatenate.4.a_0_
  192.3 10.4 %shard_map.106 = (f32[512,2048]{1,0:T(8,128)}, bf16[512,384]{1,0:T(8,128)(2,1)}, bf16[512,384]{1,0:T(8,128)(2,1)}) custom-call(s32[24]{0:T(128)} %concatenate.4.a_0_, s32[2,512]{1,0:T(2,128)} %bitcast.44, f32[2,512]{1,0:T(2,128)} %bitcast.49, bf16[768,2048]{1,0:T(8,128)(2,1)} %bitcast.26.a_3_, bf16[384,2048]{1,0:T(8,128)(2,1)} %bitcast.42), custom_call_target="tpu_custom_call" | custom-call | flops 4831838208 | bytes 9000000 | tf_op jit(solution)/shard_map/pallas_call | solution.py:350
  202.8 8.9 %all-to-all-done.4 = bf16[8,48,2048]{2,1,0:T(8,128)(2,1)S(1)} async-done(((bf16[8,48,2048]{2,1,0:T(8,128)(2,1)}), bf16[8,48,2048]{2,1,0:T(8,128)(2,1)S(1)}, u32[]{:S(2)}, u32[]{:S(2)}) %all-to-all-start.4) | async-done | bytes 1572896 | tf_op jit(solution)/shard_map/all_to_all | solution.py:118
  211.6 1.2 copy-done
  212.8 5.5 %shard_map.107 = bf16[512,2048]{1,0:T(8,128)(2,1)} custom-call(bf16[512,384]{1,0:T(8,128)(2,1)} %get-tuple-element.58.high, bf16[512,384]{1,0:T(8,128)(2,1)} %get-tuple-element.59.low, bf16[384,2048]{1,0:T(8,128)(2,1)} %bitcast.38, f32[512,2048]{1,0:T(8,128)} %get-tuple-element.60.sum_ref), custom_call_target="tpu_custom_call" | custom-call | flops 1610612736 | bytes 9000000 | tf_op jit(solution)/shard_map/pallas_call | solution.py:392
  (14 shorter events, 0.0 us)
Async XLA Ops:
  0.0 14.5 %copy-start.4 = (s32[1,512,2]{1,2,0:T(2,128)S(1)}, s32[1,512,2]{1,2,0:T(2,128)}, u32[]{:S(2)}) copy-start(s32[1,512,2]{1,2,0:T(2,128)} %param.11) | copy-start | bytes 12292
  4.3 32.1 %collective-permute-start.1 = (bf16[16400,128]{1,0:T(8,128)(2,1)}, bf16[16400,128]{1,0:T(8,128)(2,1)}, u32[]{:S(2)}, u32[]{:S(2)}) collective-permute-start(bf16[16400,128]{1,0:T(8,128)(2,1)} %shard_map.100.a_2_), channel_id=1, source_target_pairs={{6,4},{7,5},{10,8},{11,9},{12,10},{13,11},{22,20},{23,21},{26,24},... | collective-permute-start | bytes 12595208 | tf_op jit(solution)/shard_map/ppermute | solution.py:38
  7.0 51.3 %collective-permute-start = (bf16[16400,128]{1,0:T(8,128)(2,1)}, bf16[16400,128]{1,0:T(8,128)(2,1)}, u32[]{:S(2)}, u32[]{:S(2)}) collective-permute-start(bf16[16400,128]{1,0:T(8,128)(2,1)} %shard_map.100.a_2_), channel_id=1, source_target_pairs={{0,2},{1,3},{10,12},{11,13},{12,14},{13,15},{16,18},{17,19},{26,28... | collective-permute-start | bytes 12595208 | tf_op jit(solution)/shard_map/ppermute | solution.py:38
  26.1 40.7 %all-to-all-start = ((bf16[8,384,512]{2,1,0:T(8,128)(2,1)}), bf16[8,384,512]{2,1,0:T(8,128)(2,1)S(1)}, u32[]{:S(2)}, u32[]{:S(2)}) async-start(bf16[8,384,512]{2,1,0:T(8,128)(2,1)} %shard_map.101), calls=%async_computation | async-start | bytes 6291456 | tf_op jit(solution)/shard_map/all_to_all | solution.py:118
  36.4 35.7 %copy-start.7 = (s32[8]{0:T(128)S(1)}, s32[8]{0:T(128)}, u32[]{:S(2)}) copy-start(s32[8]{0:T(128)} %constant.51.clone) | copy-start | bytes 100
  58.3 50.6 %collective-permute-start.2 = (bf16[16400,128]{1,0:T(8,128)(2,1)}, bf16[16400,128]{1,0:T(8,128)(2,1)}, u32[]{:S(2)}, u32[]{:S(2)}) collective-permute-start(bf16[16400,128]{1,0:T(8,128)(2,1)} %collective-permute-done.a_3_.a_4_), channel_id=1, source_target_pairs={{2,4},{3,5},{12,14},{13,15},{18,20},{19,21},{28,30},{29,31}} | collective-permute-start | bytes 12595208 | tf_op jit(solution)/shard_map/ppermute | solution.py:38
  61.0 48.0 %collective-permute-start.3 = (bf16[16400,128]{1,0:T(8,128)(2,1)}, bf16[16400,128]{1,0:T(8,128)(2,1)}, u32[]{:S(2)}, u32[]{:S(2)}) collective-permute-start(bf16[16400,128]{1,0:T(8,128)(2,1)} %collective-permute-done.1.a_4_.a_3_), channel_id=1, source_target_pairs={{4,2},{5,3},{10,8},{11,9},{20,18},{21,19},{26,24},{27,25}} | collective-permute-start | bytes 12595208 | tf_op jit(solution)/shard_map/ppermute | solution.py:38
  66.7 1.7 copy-start.2
  68.4 40.5 %all-to-all-start.1 = ((bf16[8,384,512]{2,1,0:T(8,128)(2,1)}), bf16[8,384,512]{2,1,0:T(8,128)(2,1)S(1)}, u32[]{:S(2)}, u32[]{:S(2)}) async-start(bf16[8,384,512]{2,1,0:T(8,128)(2,1)} %shard_map.102), calls=%async_computation.1 | async-start | bytes 6291456 | tf_op jit(solution)/shard_map/all_to_all | solution.py:118
  74.0 39.2 %copy-start.6 = (s32[8]{0:T(128)S(1)}, s32[8]{0:T(128)}, u32[]{:S(2)}) copy-start(s32[8]{0:T(128)} %constant.52.clone) | copy-start | bytes 100
  108.9 4.9 %copy-start.1 = (bf16[8,384,512]{2,1,0:T(8,128)(2,1)}, bf16[8,384,512]{2,1,0:T(8,128)(2,1)S(1)}, u32[]{:S(2)}) copy-start(bf16[8,384,512]{2,1,0:T(8,128)(2,1)S(1)} %all-to-all-done.1.a_1_) | copy-start | bytes 9437188
  108.9 53.4 %collective-permute-start.5 = (bf16[16400,128]{1,0:T(8,128)(2,1)}, bf16[16400,128]{1,0:T(8,128)(2,1)}, u32[]{:S(2)}, u32[]{:S(2)}) collective-permute-start(bf16[16400,128]{1,0:T(8,128)(2,1)} %collective-permute-done.2.a_2_.a_3_), channel_id=1, source_target_pairs={{4,6},{5,7},{20,22},{21,23}} | collective-permute-start | bytes 12595208 | tf_op jit(solution)/shard_map/ppermute | solution.py:38
  111.9 53.7 %collective-permute-start.6 = (bf16[16400,128]{1,0:T(8,128)(2,1)}, bf16[16400,128]{1,0:T(8,128)(2,1)}, u32[]{:S(2)}, u32[]{:S(2)}) collective-permute-start(bf16[16400,128]{1,0:T(8,128)(2,1)} %collective-permute-done.3.a_5_.a_4_), channel_id=1, source_target_pairs={{2,0},{3,1},{18,16},{19,17}} | collective-permute-start | bytes 12595208 | tf_op jit(solution)/shard_map/ppermute | solution.py:38
  113.8 43.1 %all-to-all-start.2 = ((bf16[8,96,2048]{2,1,0:T(8,128)(2,1)}), bf16[8,96,2048]{2,1,0:T(8,128)(2,1)}, u32[]{:S(2)}, u32[]{:S(2)}) async-start(bf16[8,96,2048]{2,1,0:T(8,128)(2,1)} %bitcast.41), calls=%async_computation.2 | async-start | bytes 6291456 | tf_op jit(solution)/shard_map/all_to_all | solution.py:118
  122.0 17.0 %collective-permute-start.4 = (bf16[384,2048]{1,0:T(8,128)(2,1)}, bf16[384,2048]{1,0:T(8,128)(2,1)S(1)}, u32[]{:S(2)}, u32[]{:S(2)}) collective-permute-start(bf16[384,2048]{1,0:T(8,128)(2,1)} %get-tuple-element.45), channel_id=1, source_target_pairs={{8,0},{9,1},{10,2},{11,3},{12,4},{13,5},{14,6},{15,7},{24,16},{25,... | collective-permute-start | bytes 4718600 | tf_op jit(solution)/shard_map/ppermute | solution.py:38
  140.4 20.1 %copy-start.5 = (s32[8]{0:T(128)S(1)}, s32[8]{0:T(128)}, u32[]{:S(2)}) copy-start(s32[8]{0:T(128)} %constant.53.clone) | copy-start | bytes 100
  156.9 23.6 %all-to-all-start.3 = ((bf16[8,48,2048]{2,1,0:T(8,128)(2,1)}), bf16[8,48,2048]{2,1,0:T(8,128)(2,1)S(1)}, u32[]{:S(2)}, u32[]{:S(2)}) async-start(bf16[8,48,2048]{2,1,0:T(8,128)(2,1)} %bitcast.28), calls=%async_computation.3 | async-start | bytes 3145728 | tf_op jit(solution)/shard_map/all_to_all | solution.py:118
  180.5 7.6 %copy-start.3 = (bf16[8,48,2048]{2,1,0:T(8,128)(2,1)}, bf16[8,48,2048]{2,1,0:T(8,128)(2,1)S(1)}, u32[]{:S(2)}) copy-start(bf16[8,48,2048]{2,1,0:T(8,128)(2,1)S(1)} %all-to-all-done.3) | copy-start | bytes 4718596
  180.5 4.8 %collective-permute-start.7 = (bf16[384,2048]{1,0:T(8,128)(2,1)}, bf16[384,2048]{1,0:T(8,128)(2,1)S(1)}, u32[]{:S(2)}, u32[]{:S(2)}) collective-permute-start(bf16[384,2048]{1,0:T(8,128)(2,1)} %get-tuple-element.54), channel_id=1, source_target_pairs={{0,8},{1,9},{2,10},{3,11},{4,12},{5,13},{6,14},{7,15},{16,24},{17,... | collective-permute-start | bytes 4718600 | tf_op jit(solution)/shard_map/ppermute | solution.py:38
  188.0 23.6 %all-to-all-start.4 = ((bf16[8,48,2048]{2,1,0:T(8,128)(2,1)}), bf16[8,48,2048]{2,1,0:T(8,128)(2,1)S(1)}, u32[]{:S(2)}, u32[]{:S(2)}) async-start(bf16[8,48,2048]{2,1,0:T(8,128)(2,1)} %bitcast.33), calls=%async_computation.4 | async-start | bytes 3145728 | tf_op jit(solution)/shard_map/all_to_all | solution.py:118
  211.6 1.2 copy-start

commit v6 on v5

--- a/solution.py
+++ b/solution.py
@@ -46,7 +46,7 @@
 TABLE_ROWS = 16
 
 
-def pack_kernel(pieces, which, up, down, up_at, down_at, out, held, rows, in_sem, out_sem):
+def pack_kernel(pieces, which, up, down, up_at, down_at, out, held, wide, rows, in_sem, out_sem):
     size = up.shape[1]
     step = size // pieces
     inward, outward = [], []
@@ -61,11 +61,10 @@
         )
         inward[-1].start()
     ups, downs = up_at.shape[1], down_at.shape[1]
-    rows[...] = jnp.zeros(rows.shape, jnp.bfloat16)
-    rows[0:ups, 0 : up_at.shape[2]] = up_at[which[0]].astype(jnp.float32).astype(jnp.bfloat16)
-    rows[ups : ups + downs, 0 : down_at.shape[2]] = (
-        down_at[which[0]].astype(jnp.float32).astype(jnp.bfloat16)
-    )
+    wide[...] = jnp.zeros(wide.shape, jnp.float32)
+    wide[0:ups, 0 : up_at.shape[2]] = up_at[which[0]].astype(jnp.float32)
+    wide[ups : ups + downs, 0 : down_at.shape[2]] = down_at[which[0]].astype(jnp.float32)
+    rows[...] = wide[...].astype(jnp.bfloat16)
     outward.append(
         pltpu.make_async_copy(rows, out.at[pl.ds(2 * size, TABLE_ROWS)], out_sem.at[2 * pieces])
     )
@@ -89,6 +88,7 @@
         out_shape=jax.ShapeDtypeStruct((2 * size + TABLE_ROWS, blk), up.dtype),
         scratch_shapes=[
             pltpu.VMEM((2 * size, blk), jnp.bfloat16),
+            pltpu.VMEM((TABLE_ROWS, blk), jnp.float32),
             pltpu.VMEM((TABLE_ROWS, blk), jnp.bfloat16),
             pltpu.SemaphoreType.DMA((2 * pieces,)),
             pltpu.SemaphoreType.DMA((2 * pieces + 1,)),

time: 222 us -> 222 us (level)
  no operation moved by 1% of the time
where the time goes in v6:
time: 222 us; the launch traced here: 218 us
  waiting for transfers between devices  96.1 us (43%)
  Pallas kernels  59.7 us (27%)
  starting transfers between devices  42.1 us (19%)
  other arithmetic  7.99 us (4%)
  local copies, waits for them, and re-layouts  6.65 us (3%)
  blocking collectives  5.58 us (3%)
    all_to_all x5, waiting for transfers between devices, exchange(): return lax.all_to_all(rows, PLANE, split_axis=0, concat_axis=0, tiled=True)  52.2 us
    ppermute x8, waiting for transfers between devices, send(): return lax.ppermute(value, AXES, pairs)  43.9 us
    pallas_call x3, Pallas kernels, expert_rows(): pl.pallas_call(lambda *a: ffn_kernel(len(weights), cap, *a), in_specs=[sm...  27.4 us
    ppermute x8, starting transfers between devices, send(): return lax.ppermute(value, AXES, pairs)  22 us
    all_to_all x5, starting transfers between devices, exchange(): return lax.all_to_all(rows, PLANE, split_axis=0, concat_axis=0, tiled=True)  20.2 us
    pallas_call x2, Pallas kernels, gather_rows(): pl.pallas_call(lambda *a: gather_kernel(experts, cap, *a), grid_spec=pltp...  12 us
    pallas_call x1, Pallas kernels, combine_first(): pl.pallas_call(lambda *a: first_kernel(experts, cap, *a), grid_spec=pltpu...  10.4 us
    all_gather x1, blocking collectives, per_device_planes(): choices = lax.all_gather(after(choice, own), 'grp')  5.58 us
  transfers between devices with their start and end apart: 13, of which 9 were waited for; matrix products, arithmetic and copies ran while one was open for 4% of the time, Pallas kernels for 23%

profile of v6, /device:TPU:0, one launch (start us, length us, event | category | flops | bytes accessed | tf_op | source)
XLA Modules:
  0.0 218.3 jit_solution(15311602241903338586)
XLA Ops:
  0.0 4.3 %shard_map.100.a_2_ = bf16[16400,128]{1,0:T(8,128)(2,1)} custom-call(s32[1]{0:T(128)} %bitcast.19.a_0_, bf16[2,8192,128]{2,1,0:T(8,128)(2,1)} %bitcast.39, bf16[2,8192,128]{2,1,0:T(8,128)(2,1)} %bitcast.40, s32[2,2,32]{2,1,0:T(2,128)} %bitcast.46, s32[2,4,16]{2,1,0:T(4,128)} %bitcast.43), custom_call_target="tpu_custom_call" | custom-call | bytes 8400000 | tf_op jit(solution)/shard_map/pallas_call | solution.py:84
  4.3 2.7 %collective-permute-start.1 = (bf16[16400,128]{1,0:T(8,128)(2,1)}, bf16[16400,128]{1,0:T(8,128)(2,1)}, u32[]{:S(2)}, u32[]{:S(2)}) collective-permute-start(bf16[16400,128]{1,0:T(8,128)(2,1)} %shard_map.100.a_2_), channel_id=1, source_target_pairs={{6,4},{7,5},{10,8},{11,9},{12,10},{13,11},{22,20},{23,21},{26,24},... | collective-permute-start | bytes 12595208 | tf_op jit(solution)/shard_map/ppermute | solution.py:38
  7.0 6.9 %collective-permute-start = (bf16[16400,128]{1,0:T(8,128)(2,1)}, bf16[16400,128]{1,0:T(8,128)(2,1)}, u32[]{:S(2)}, u32[]{:S(2)}) collective-permute-start(bf16[16400,128]{1,0:T(8,128)(2,1)} %shard_map.100.a_2_), channel_id=1, source_target_pairs={{0,2},{1,3},{10,12},{11,13},{12,14},{13,15},{16,18},{17,19},{26,28... | collective-permute-start | bytes 12595208 | tf_op jit(solution)/shard_map/ppermute | solution.py:38
  13.9 0.6 stack.107.a_0_
  14.5 5.6 %all-gather.1.a_2_ = s32[4,2,512]{2,1,0:T(2,128)} all-gather(s32[1,2,512]{2,1,0:T(2,128)S(1)} %bitcast.45), channel_id=2, replica_groups=mesh['grp'=4,'z'=4,'x'=2] {'grp'}, dimensions={0}, use_global_device_ids=true | all-gather | bytes 20480 | tf_op jit(solution)/shard_map/all_gather | solution.py:429
  20.1 6.0 %shard_map.101 = bf16[8,384,512]{2,1,0:T(8,128)(2,1)} custom-call(s32[8]{0:T(128)} %stack.107.a_0_, bf16[2048,512]{1,0:T(8,128)(2,1)} %bitcast.47, s32[4,2,512]{2,1,0:T(2,128)} %all-gather.1.a_2_), custom_call_target="tpu_custom_call" | custom-call | flops 1610612736 | bytes 9000000 | tf_op jit(solution)/shard_map/pallas_call | solution.py:145
  26.1 3.7 %all-to-all-start = ((bf16[8,384,512]{2,1,0:T(8,128)(2,1)}), bf16[8,384,512]{2,1,0:T(8,128)(2,1)S(1)}, u32[]{:S(2)}, u32[]{:S(2)}) async-start(bf16[8,384,512]{2,1,0:T(8,128)(2,1)} %shard_map.101), calls=%async_computation | async-start | bytes 6291456 | tf_op jit(solution)/shard_map/all_to_all | solution.py:118
  29.8 0.6 stack.108.a_0_
  30.4 6.0 %shard_map.102 = bf16[8,384,512]{2,1,0:T(8,128)(2,1)} custom-call(s32[8]{0:T(128)} %stack.108.a_0_, bf16[2048,512]{1,0:T(8,128)(2,1)} %bitcast.48, s32[4,2,512]{2,1,0:T(2,128)} %all-gather.1.a_2_), custom_call_target="tpu_custom_call" | custom-call | flops 1610612736 | bytes 9000000 | tf_op jit(solution)/shard_map/pallas_call | solution.py:145
  36.4 0.0 collective-permute-done.1.a_4_.a_3_
  36.4 21.9 %collective-permute-done.a_3_.a_4_ = bf16[16400,128]{1,0:T(8,128)(2,1)} collective-permute-done((bf16[16400,128]{1,0:T(8,128)(2,1)}, bf16[16400,128]{1,0:T(8,128)(2,1)}, u32[]{:S(2)}, u32[]{:S(2)}) %collective-permute-start) | collective-permute-done | bytes 4198432 | tf_op jit(solution)/shard_map/ppermute | solution.py:38
  58.3 2.7 %collective-permute-start.2 = (bf16[16400,128]{1,0:T(8,128)(2,1)}, bf16[16400,128]{1,0:T(8,128)(2,1)}, u32[]{:S(2)}, u32[]{:S(2)}) collective-permute-start(bf16[16400,128]{1,0:T(8,128)(2,1)} %collective-permute-done.a_3_.a_4_), channel_id=1, source_target_pairs={{2,4},{3,5},{12,14},{13,15},{18,20},{19,21},{28,30},{29,31}} | collective-permute-start | bytes 12595208 | tf_op jit(solution)/shard_map/ppermute | solution.py:38
  61.0 2.6 %collective-permute-start.3 = (bf16[16400,128]{1,0:T(8,128)(2,1)}, bf16[16400,128]{1,0:T(8,128)(2,1)}, u32[]{:S(2)}, u32[]{:S(2)}) collective-permute-start(bf16[16400,128]{1,0:T(8,128)(2,1)} %collective-permute-done.1.a_4_.a_3_), channel_id=1, source_target_pairs={{4,2},{5,3},{10,8},{11,9},{20,18},{21,19},{26,24},{27,25}} | collective-permute-start | bytes 12595208 | tf_op jit(solution)/shard_map/ppermute | solution.py:38
  63.6 3.2 %all-to-all-done.a_1_ = bf16[8,384,512]{2,1,0:T(8,128)(2,1)S(1)} async-done(((bf16[8,384,512]{2,1,0:T(8,128)(2,1)}), bf16[8,384,512]{2,1,0:T(8,128)(2,1)S(1)}, u32[]{:S(2)}, u32[]{:S(2)}) %all-to-all-start) | async-done | bytes 3145760 | tf_op jit(solution)/shard_map/all_to_all | solution.py:118
  66.7 1.7 copy-done.2
  68.4 3.6 %all-to-all-start.1 = ((bf16[8,384,512]{2,1,0:T(8,128)(2,1)}), bf16[8,384,512]{2,1,0:T(8,128)(2,1)S(1)}, u32[]{:S(2)}, u32[]{:S(2)}) async-start(bf16[8,384,512]{2,1,0:T(8,128)(2,1)} %shard_map.102), calls=%async_computation.1 | async-start | bytes 6291456 | tf_op jit(solution)/shard_map/all_to_all | solution.py:118
  72.1 0.6 dynamic_slice.9
  72.7 1.3 pad_add_fusion.a_0_
  74.0 13.4 %shard_map.103 = bf16[768,2048]{1,0:T(8,128)(2,1)} custom-call(s32[2]{0:T(128)} %pad_add_fusion.a_0_, bf16[8,384,512]{2,1,0:T(8,128)(2,1)} %copy-done.2, bf16[16400,128]{1,0:T(8,128)(2,1)} %shard_map.100.a_2_, bf16[16400,128]{1,0:T(8,128)(2,1)} %collective-permute-done.a_3_.a_4_, bf16[16400,128]{1,0:T(8,128)(2,1)} %collective-permute-done.1.a_4_.a_3_), custom_call_target="tpu_custom_call" | custom-call | flops 6442450944 | bytes 12000000 | tf_op jit(solution)/shard_map/pallas_call | solution.py:281
  87.3 21.6 %all-to-all-done.1.a_1_ = bf16[8,384,512]{2,1,0:T(8,128)(2,1)S(1)} async-done(((bf16[8,384,512]{2,1,0:T(8,128)(2,1)}), bf16[8,384,512]{2,1,0:T(8,128)(2,1)S(1)}, u32[]{:S(2)}, u32[]{:S(2)}) %all-to-all-start.1) | async-done | bytes 3145760 | tf_op jit(solution)/shard_map/all_to_all | solution.py:118
  108.9 0.0 collective-permute-done.2.a_2_.a_3_
  108.9 0.0 collective-permute-done.3.a_5_.a_4_
  108.9 2.9 %collective-permute-start.5 = (bf16[16400,128]{1,0:T(8,128)(2,1)}, bf16[16400,128]{1,0:T(8,128)(2,1)}, u32[]{:S(2)}, u32[]{:S(2)}) collective-permute-start(bf16[16400,128]{1,0:T(8,128)(2,1)} %collective-permute-done.2.a_2_.a_3_), channel_id=1, source_target_pairs={{4,6},{5,7},{20,22},{21,23}} | collective-permute-start | bytes 12595208 | tf_op jit(solution)/shard_map/ppermute | solution.py:38
  111.9 1.3 collective-permute-start.6
  113.2 0.7 dynamic_slice.10
  113.8 5.6 %all-to-all-start.2 = ((bf16[8,96,2048]{2,1,0:T(8,128)(2,1)}), bf16[8,96,2048]{2,1,0:T(8,128)(2,1)}, u32[]{:S(2)}, u32[]{:S(2)}) async-start(bf16[8,96,2048]{2,1,0:T(8,128)(2,1)} %bitcast.41), calls=%async_computation.2 | async-start | bytes 6291456 | tf_op jit(solution)/shard_map/all_to_all | solution.py:118
  119.5 1.3 pad_add_fusion.1.a_0_
  120.8 1.2 shard_map.104
  122.0 1.3 collective-permute-start.4
  123.3 15.7 %collective-permute-done.4 = bf16[384,2048]{1,0:T(8,128)(2,1)S(1)} collective-permute-done((bf16[384,2048]{1,0:T(8,128)(2,1)}, bf16[384,2048]{1,0:T(8,128)(2,1)S(1)}, u32[]{:S(2)}, u32[]{:S(2)}) %collective-permute-start.4) | collective-permute-done | bytes 1572896 | tf_op jit(solution)/shard_map/ppermute | solution.py:38
  139.0 1.4 broadcast_select_fusion
  140.4 16.5 %all-to-all-done.2 = bf16[8,96,2048]{2,1,0:T(8,128)(2,1)} async-done(((bf16[8,96,2048]{2,1,0:T(8,128)(2,1)}), bf16[8,96,2048]{2,1,0:T(8,128)(2,1)}, u32[]{:S(2)}, u32[]{:S(2)}) %all-to-all-start.2) | async-done | bytes 3145760 | tf_op jit(solution)/shard_map/all_to_all | solution.py:118
  156.9 3.6 %all-to-all-start.3 = ((bf16[8,48,2048]{2,1,0:T(8,128)(2,1)}), bf16[8,48,2048]{2,1,0:T(8,128)(2,1)S(1)}, u32[]{:S(2)}, u32[]{:S(2)}) async-start(bf16[8,48,2048]{2,1,0:T(8,128)(2,1)} %bitcast.28), calls=%async_computation.3 | async-start | bytes 3145728 | tf_op jit(solution)/shard_map/all_to_all | solution.py:118
  160.5 0.6 dynamic_slice.11
  161.1 1.2 pad_add_fusion.2.a_0_
  162.3 0.0 collective-permute-done.5.a_2_
  162.3 3.2 %collective-permute-done.6.a_5_ = bf16[16400,128]{1,0:T(8,128)(2,1)} collective-permute-done((bf16[16400,128]{1,0:T(8,128)(2,1)}, bf16[16400,128]{1,0:T(8,128)(2,1)}, u32[]{:S(2)}, u32[]{:S(2)}) %collective-permute-start.6) | collective-permute-done | bytes 4198432 | tf_op jit(solution)/shard_map/ppermute | solution.py:38
  165.5 12.8 %shard_map.105 = (bf16[384,2048]{1,0:T(8,128)(2,1)}, bf16[384,2048]{1,0:T(8,128)(2,1)}) custom-call(s32[2]{0:T(128)} %pad_add_fusion.2.a_0_, bf16[8,384,512]{2,1,0:T(8,128)(2,1)} %copy-done.1, bf16[16400,128]{1,0:T(8,128)(2,1)} %collective-permute-done.5.a_2_, bf16[16400,128]{1,0:T(8,128)(2,1)} %collective-permute-done.2.a_2_.a_3_, ...), custom_call_target="tpu_custom_call" | custom-call | flops 6442450944 | bytes 12000000 | tf_op jit(solution)/shard_map/pallas_call | solution.py:281
  178.4 2.1 all-to-all-done.3
  180.5 1.6 collective-permute-start.7
  182.1 3.1 %collective-permute-done.7 = bf16[384,2048]{1,0:T(8,128)(2,1)S(1)} collective-permute-done((bf16[384,2048]{1,0:T(8,128)(2,1)}, bf16[384,2048]{1,0:T(8,128)(2,1)S(1)}, u32[]{:S(2)}, u32[]{:S(2)}) %collective-permute-start.7) | collective-permute-done | bytes 1572896 | tf_op jit(solution)/shard_map/ppermute | solution.py:38
  185.2 2.8 %broadcast_select_fusion.1 = bf16[384,2048]{1,0:T(8,128)(2,1)} fusion(bf16[384,2048]{1,0:T(8,128)(2,1)} %get-tuple-element.53, bf16[384,2048]{1,0:T(8,128)(2,1)S(1)} %collective-permute-done.7, pred[]{:T(512)S(6)} %eq.10), kind=kLoop, calls=%fused_computation.1 | loop fusion | flops 786432 | bytes 4718593 | tf_op jit(solution)/shard_map/jit(_where)/select_n | solution.py:456
  188.0 3.6 %all-to-all-start.4 = ((bf16[8,48,2048]{2,1,0:T(8,128)(2,1)}), bf16[8,48,2048]{2,1,0:T(8,128)(2,1)S(1)}, u32[]{:S(2)}, u32[]{:S(2)}) async-start(bf16[8,48,2048]{2,1,0:T(8,128)(2,1)} %bitcast.33), calls=%async_computation.4 | async-start | bytes 3145728 | tf_op jit(solution)/shard_map/all_to_all | solution.py:118
  191.6 0.7 concatenate.4.a_0_
  192.3 10.4 %shard_map.106 = (f32[512,2048]{1,0:T(8,128)}, bf16[512,384]{1,0:T(8,128)(2,1)}, bf16[512,384]{1,0:T(8,128)(2,1)}) custom-call(s32[24]{0:T(128)} %concatenate.4.a_0_, s32[2,512]{1,0:T(2,128)} %bitcast.44, f32[2,512]{1,0:T(2,128)} %bitcast.49, bf16[768,2048]{1,0:T(8,128)(2,1)} %bitcast.26.a_3_, bf16[384,2048]{1,0:T(8,128)(2,1)} %bitcast.42), custom_call_target="tpu_custom_call" | custom-call | flops 4831838208 | bytes 9000000 | tf_op jit(solution)/shard_map/pallas_call | solution.py:350
  202.8 8.9 %all-to-all-done.4 = bf16[8,48,2048]{2,1,0:T(8,128)(2,1)S(1)} async-done(((bf16[8,48,2048]{2,1,0:T(8,128)(2,1)}), bf16[8,48,2048]{2,1,0:T(8,128)(2,1)S(1)}, u32[]{:S(2)}, u32[]{:S(2)}) %all-to-all-start.4) | async-done | bytes 1572896 | tf_op jit(solution)/shard_map/all_to_all | solution.py:118
  211.6 1.2 copy-done
  212.8 5.5 %shard_map.107 = bf16[512,2048]{1,0:T(8,128)(2,1)} custom-call(bf16[512,384]{1,0:T(8,128)(2,1)} %get-tuple-element.58.high, bf16[512,384]{1,0:T(8,128)(2,1)} %get-tuple-element.59.low, bf16[384,2048]{1,0:T(8,128)(2,1)} %bitcast.38, f32[512,2048]{1,0:T(8,128)} %get-tuple-element.60.sum_ref), custom_call_target="tpu_custom_call" | custom-call | flops 1610612736 | bytes 9000000 | tf_op jit(solution)/shard_map/pallas_call | solution.py:392
  (14 shorter events, 0.0 us)
Async XLA Ops:
  0.0 14.5 %copy-start.4 = (s32[1,512,2]{1,2,0:T(2,128)S(1)}, s32[1,512,2]{1,2,0:T(2,128)}, u32[]{:S(2)}) copy-start(s32[1,512,2]{1,2,0:T(2,128)} %param.11) | copy-start | bytes 12292
  4.3 32.1 %collective-permute-start.1 = (bf16[16400,128]{1,0:T(8,128)(2,1)}, bf16[16400,128]{1,0:T(8,128)(2,1)}, u32[]{:S(2)}, u32[]{:S(2)}) collective-permute-start(bf16[16400,128]{1,0:T(8,128)(2,1)} %shard_map.100.a_2_), channel_id=1, source_target_pairs={{6,4},{7,5},{10,8},{11,9},{12,10},{13,11},{22,20},{23,21},{26,24},... | collective-permute-start | bytes 12595208 | tf_op jit(solution)/shard_map/ppermute | solution.py:38
  7.0 51.3 %collective-permute-start = (bf16[16400,128]{1,0:T(8,128)(2,1)}, bf16[16400,128]{1,0:T(8,128)(2,1)}, u32[]{:S(2)}, u32[]{:S(2)}) collective-permute-start(bf16[16400,128]{1,0:T(8,128)(2,1)} %shard_map.100.a_2_), channel_id=1, source_target_pairs={{0,2},{1,3},{10,12},{11,13},{12,14},{13,15},{16,18},{17,19},{26,28... | collective-permute-start | bytes 12595208 | tf_op jit(solution)/shard_map/ppermute | solution.py:38
  26.1 40.7 %all-to-all-start = ((bf16[8,384,512]{2,1,0:T(8,128)(2,1)}), bf16[8,384,512]{2,1,0:T(8,128)(2,1)S(1)}, u32[]{:S(2)}, u32[]{:S(2)}) async-start(bf16[8,384,512]{2,1,0:T(8,128)(2,1)} %shard_map.101), calls=%async_computation | async-start | bytes 6291456 | tf_op jit(solution)/shard_map/all_to_all | solution.py:118
  36.4 35.7 %copy-start.7 = (s32[8]{0:T(128)S(1)}, s32[8]{0:T(128)}, u32[]{:S(2)}) copy-start(s32[8]{0:T(128)} %constant.51.clone) | copy-start | bytes 100
  58.3 50.6 %collective-permute-start.2 = (bf16[16400,128]{1,0:T(8,128)(2,1)}, bf16[16400,128]{1,0:T(8,128)(2,1)}, u32[]{:S(2)}, u32[]{:S(2)}) collective-permute-start(bf16[16400,128]{1,0:T(8,128)(2,1)} %collective-permute-done.a_3_.a_4_), channel_id=1, source_target_pairs={{2,4},{3,5},{12,14},{13,15},{18,20},{19,21},{28,30},{29,31}} | collective-permute-start | bytes 12595208 | tf_op jit(solution)/shard_map/ppermute | solution.py:38
  61.0 48.0 %collective-permute-start.3 = (bf16[16400,128]{1,0:T(8,128)(2,1)}, bf16[16400,128]{1,0:T(8,128)(2,1)}, u32[]{:S(2)}, u32[]{:S(2)}) collective-permute-start(bf16[16400,128]{1,0:T(8,128)(2,1)} %collective-permute-done.1.a_4_.a_3_), channel_id=1, source_target_pairs={{4,2},{5,3},{10,8},{11,9},{20,18},{21,19},{26,24},{27,25}} | collective-permute-start | bytes 12595208 | tf_op jit(solution)/shard_map/ppermute | solution.py:38
  66.7 1.7 copy-start.2
  68.4 40.5 %all-to-all-start.1 = ((bf16[8,384,512]{2,1,0:T(8,128)(2,1)}), bf16[8,384,512]{2,1,0:T(8,128)(2,1)S(1)}, u32[]{:S(2)}, u32[]{:S(2)}) async-start(bf16[8,384,512]{2,1,0:T(8,128)(2,1)} %shard_map.102), calls=%async_computation.1 | async-start | bytes 6291456 | tf_op jit(solution)/shard_map/all_to_all | solution.py:118
  74.0 39.2 %copy-start.6 = (s32[8]{0:T(128)S(1)}, s32[8]{0:T(128)}, u32[]{:S(2)}) copy-start(s32[8]{0:T(128)} %constant.52.clone) | copy-start | bytes 100
  108.9 4.9 %copy-start.1 = (bf16[8,384,512]{2,1,0:T(8,128)(2,1)}, bf16[8,384,512]{2,1,0:T(8,128)(2,1)S(1)}, u32[]{:S(2)}) copy-start(bf16[8,384,512]{2,1,0:T(8,128)(2,1)S(1)} %all-to-all-done.1.a_1_) | copy-start | bytes 9437188
  108.9 53.4 %collective-permute-start.5 = (bf16[16400,128]{1,0:T(8,128)(2,1)}, bf16[16400,128]{1,0:T(8,128)(2,1)}, u32[]{:S(2)}, u32[]{:S(2)}) collective-permute-start(bf16[16400,128]{1,0:T(8,128)(2,1)} %collective-permute-done.2.a_2_.a_3_), channel_id=1, source_target_pairs={{4,6},{5,7},{20,22},{21,23}} | collective-permute-start | bytes 12595208 | tf_op jit(solution)/shard_map/ppermute | solution.py:38
  111.9 53.7 %collective-permute-start.6 = (bf16[16400,128]{1,0:T(8,128)(2,1)}, bf16[16400,128]{1,0:T(8,128)(2,1)}, u32[]{:S(2)}, u32[]{:S(2)}) collective-permute-start(bf16[16400,128]{1,0:T(8,128)(2,1)} %collective-permute-done.3.a_5_.a_4_), channel_id=1, source_target_pairs={{2,0},{3,1},{18,16},{19,17}} | collective-permute-start | bytes 12595208 | tf_op jit(solution)/shard_map/ppermute | solution.py:38
  113.8 43.1 %all-to-all-start.2 = ((bf16[8,96,2048]{2,1,0:T(8,128)(2,1)}), bf16[8,96,2048]{2,1,0:T(8,128)(2,1)}, u32[]{:S(2)}, u32[]{:S(2)}) async-start(bf16[8,96,2048]{2,1,0:T(8,128)(2,1)} %bitcast.41), calls=%async_computation.2 | async-start | bytes 6291456 | tf_op jit(solution)/shard_map/all_to_all | solution.py:118
  122.0 17.0 %collective-permute-start.4 = (bf16[384,2048]{1,0:T(8,128)(2,1)}, bf16[384,2048]{1,0:T(8,128)(2,1)S(1)}, u32[]{:S(2)}, u32[]{:S(2)}) collective-permute-start(bf16[384,2048]{1,0:T(8,128)(2,1)} %get-tuple-element.45), channel_id=1, source_target_pairs={{8,0},{9,1},{10,2},{11,3},{12,4},{13,5},{14,6},{15,7},{24,16},{25,... | collective-permute-start | bytes 4718600 | tf_op jit(solution)/shard_map/ppermute | solution.py:38
  140.4 20.1 %copy-start.5 = (s32[8]{0:T(128)S(1)}, s32[8]{0:T(128)}, u32[]{:S(2)}) copy-start(s32[8]{0:T(128)} %constant.53.clone) | copy-start | bytes 100
  156.9 23.6 %all-to-all-start.3 = ((bf16[8,48,2048]{2,1,0:T(8,128)(2,1)}), bf16[8,48,2048]{2,1,0:T(8,128)(2,1)S(1)}, u32[]{:S(2)}, u32[]{:S(2)}) async-start(bf16[8,48,2048]{2,1,0:T(8,128)(2,1)} %bitcast.28), calls=%async_computation.3 | async-start | bytes 3145728 | tf_op jit(solution)/shard_map/all_to_all | solution.py:118
  180.5 7.6 %copy-start.3 = (bf16[8,48,2048]{2,1,0:T(8,128)(2,1)}, bf16[8,48,2048]{2,1,0:T(8,128)(2,1)S(1)}, u32[]{:S(2)}) copy-start(bf16[8,48,2048]{2,1,0:T(8,128)(2,1)S(1)} %all-to-all-done.3) | copy-start | bytes 4718596
  180.5 4.8 %collective-permute-start.7 = (bf16[384,2048]{1,0:T(8,128)(2,1)}, bf16[384,2048]{1,0:T(8,128)(2,1)S(1)}, u32[]{:S(2)}, u32[]{:S(2)}) collective-permute-start(bf16[384,2048]{1,0:T(8,128)(2,1)} %get-tuple-element.54), channel_id=1, source_target_pairs={{0,8},{1,9},{2,10},{3,11},{4,12},{5,13},{6,14},{7,15},{16,24},{17,... | collective-permute-start | bytes 4718600 | tf_op jit(solution)/shard_map/ppermute | solution.py:38
  188.0 23.6 %all-to-all-start.4 = ((bf16[8,48,2048]{2,1,0:T(8,128)(2,1)}), bf16[8,48,2048]{2,1,0:T(8,128)(2,1)S(1)}, u32[]{:S(2)}, u32[]{:S(2)}) async-start(bf16[8,48,2048]{2,1,0:T(8,128)(2,1)} %bitcast.33), calls=%async_computation.4 | async-start | bytes 3145728 | tf_op jit(solution)/shard_map/all_to_all | solution.py:118
  211.6 1.2 copy-start
